TPU v7x, 32 devices: a whole 2x2x4 slice. The times are simulated.
32 devices in a mesh: col: 8 (over z, x), gz: 4 (over y, core).
Axes of the slice: x: 2, y: 2, z: 4, core: 2. Of those that a mesh axis runs over, the one named last changes fastest.
Arguments:
- state: float32 [80, 8, 64, 128], P(None, 'gz', 'col'), may hold values from -6 to 6
- observation_site: int32 [2, 1024], replicated, may hold values from 0 to 8191
- obs_count: int32 [2, 8], P(None, 'col'), may hold values from 1 to 128, 256 in all within a row
- measured_values: float32 [2, 1024], P(None, 'col'), may hold values from -8 to 8
- observation_noise: float32 [2, 1024], P(None, 'col'), may hold values from 0.25 to 4
- loc_pattern: int32 [2, 8, 8], P(None, None, 'col'), may hold values from 0 to 1, as said below
- ocean_mask: int32 [64, 128], P('col'), may hold values 0 or 1
- zonal_current: float32 [8, 64, 128], P('gz', 'col'), may hold values from -0.45 to 0.45
Outputs:
- forecast: float32 [80, 8, 64, 128], P(None, 'gz', 'col')
Inputs may be any that keep to these rules, and one draw needn't show every extreme that they name: `obs_count`: in each batch the counts sum to 256 and the largest is 128. loc_pattern[b, a, c] is 1 where a equals c and 0 where the periodic distance of a and c along the column blocks exceeds 3.
All inputs are finite; a program needn't handle non-finite values. No bound on the sum of `obs_count` or of `ocean_mask` on one device may be relied on, other than what follows from the above.
Results may differ from a plain program's by a relative error of at most 0.0003.
Values sent between devices are 32-bit elements; how exact they have to be, the bound alone decides.
No kernel may reach another device: no remote copies, remote signals or barrier semaphores. Data moves between devices by JAX's collectives and lax.ppermute only.
A program may use at most 64 MiB of HBM per device.

v0:
```python
import functools

import jax
import jax.numpy as jnp
from jax import lax
from jax.experimental import pallas as pl
from jax.experimental.pallas import tpu as pltpu
from jax.sharding import PartitionSpec as P

LEVS = 2
LONS = 8
LATS = 128
BATCHES = 2
REACH = 3
CAP = 128
MEAN_COUNT = 32
WINDOW = 2 * REACH + 1
CHUNK = 256

CELLS = LEVS * LONS * LATS
ROWS = LEVS * LONS
CORE_ROW = 16
Y_ROW = 24
WEST_ROW = 32
EAST_ROW = 34
EXT_ROWS = 36

LATERAL_MIX = 0.2
VERTICAL_MIX = 0.15

F32 = jnp.float32
BF16 = jnp.bfloat16


def iota(shape, dim):
    return lax.broadcasted_iota(jnp.int32, shape, dim)


def halves(x):
    high = x.astype(BF16)
    return high, (x - high.astype(F32)).astype(BF16)


def dot(a, b):
    return lax.dot_general(a, b, (((1,), (0,)), ((), ())), preferred_element_type=F32)


def dot_lanes(a, b):
    return lax.dot_general(a, b, (((1,), (1,)), ((), ())), preferred_element_type=F32)


def for_each(count, body):
    if count == 1:
        body(0)
    else:
        lax.fori_loop(0, count, lambda i, unused: (body(i), unused)[1], 0)


def rows_of(members):
    names = ("mask", "value", "noise", "links", "site", "occupied", "owner", "count")
    return {name: members + i for i, name in enumerate(names)}


def pick_kernel(members, scal, site, value, noise, links, mask, state, out):
    col, gz = scal[0], scal[1]
    lane = iota((1, CAP), 1)
    index, filled = [], []
    for b in range(BATCHES):
        occupied = lane < scal[2 + b]
        filled.append(occupied)
        at = pl.multiple_of(col * CAP, CAP)
        index.append(jnp.where(occupied, site[b : b + 1, pl.ds(at, CAP)] - gz * CELLS, -1))
    wanted = jnp.concatenate(index, 1)
    total = jnp.zeros((3 * members + 16, BATCHES * CAP), F32)
    cell = iota((2 * LATS, BATCHES * CAP), 0)
    for pair in range(ROWS // 2):
        left = []
        for r in (2 * pair, 2 * pair + 1):
            x = state[pl.ds(r, members, stride=ROWS), :]
            high = x.astype(BF16)
            rest = x - high.astype(F32)
            middle = rest.astype(BF16)
            low = (rest - middle.astype(F32)).astype(BF16)
            lon = r % LONS
            ocean = jnp.broadcast_to(mask[lon : lon + 1, :], (16, LATS)).astype(BF16)
            left.append(jnp.concatenate([high, ocean, middle, low], 0))
        hit = jnp.where(cell + pair * 2 * LATS == wanted, 1.0, 0.0).astype(BF16)
        total = total + dot(jnp.concatenate(left, 1), hit)
    m = members
    picked = (total[:m] + total[m + 16 : 2 * m + 16]) + total[2 * m + 16 :]
    first = jnp.where(gz == 0, 1.0, 0.0)
    for b in range(BATCHES):
        here = slice(b * CAP, (b + 1) * CAP)
        once = jnp.where(filled[b], first, 0.0)
        at = pl.multiple_of(col * CAP, CAP)
        out[b, :m, :] = picked[:, here]
        tail = [
            total[m : m + 1, here],
            value[b : b + 1, :] * once,
            noise[b : b + 1, :] * once,
            links[b : b + 1, :] * first,
            site[b : b + 1, pl.ds(at, CAP)].astype(F32) * once,
            once,
            once * col.astype(F32),
            jnp.full((1, CAP), scal[2 + b].astype(F32) * first),
        ]
        out[b, m:, :] = jnp.concatenate(tail, 0)


def step_kernel(
    members, blocks, columns, around, chunks,
    scal, mine, other, state, core_edge, y_edge, west, east, mask, zonal, out,
    packed, fields, gained,
):
    col, gz = scal[0], scal[1]
    odd = gz % 2
    lon_all = columns * LONS
    place = rows_of(members)
    denominator = 1.0 / (members - 1)
    height = members + 8
    owners = [col ^ j if around is None else (col + around[j] + columns) % columns for j in range(blocks)]

    links = []
    packed[...] = jnp.zeros_like(packed)
    for b in range(BATCHES):
        start = 0
        own_links = []
        for j in range(blocks):
            block = jnp.where(odd == b, mine[j], other[j])
            own_links.append(block[place["links"] : place["links"] + 1, :])
            tall = jnp.concatenate([block, jnp.zeros((LATS - height, CAP), F32)], 0)
            packed[b, pl.ds(start, CAP), :] = tall.T
            start = start + block[place["count"], 0].astype(jnp.int32)
        links.append(own_links)

    for r in range(ROWS):
        fields[r] = state[pl.ds(r, members, stride=ROWS), :]
    for lon in range(LONS):
        fields[CORE_ROW + lon] = core_edge[pl.ds(lon, members, stride=LONS), :]
        fields[Y_ROW + lon] = y_edge[pl.ds(lon, members, stride=LONS), :]
    for lev in range(LEVS):
        fields[WEST_ROW + lev] = west[pl.ds(lev, members, stride=LEVS), :]
        fields[EAST_ROW + lev] = east[pl.ds(lev, members, stride=LEVS), :]
    ocean = [mask[lon : lon + 1, :] for lon in range(LONS)] * 4
    ocean += [west[members * LEVS : members * LEVS + 1, :]] * LEVS
    ocean += [east[members * LEVS : members * LEVS + 1, :]] * LEVS

    lane = iota((1, LATS), 1)
    own = lane < ROWS
    near = (lane >= CORE_ROW) & (lane < Y_ROW)
    far = (lane >= Y_ROW) & (lane < WEST_ROW)
    above, below = LEVS * gz + LEVS, LEVS * gz - 1
    row_lev = LEVS * gz + jnp.where(own, lane // LONS, lane % LEVS)
    row_lev = jnp.where(near, jnp.where(odd == 0, above, below), row_lev)
    row_lev = jnp.where(far, jnp.where(odd == 0, below, above), row_lev)
    west_lon = (col * LONS + lon_all - 1) % lon_all
    east_lon = (col * LONS + LONS) % lon_all
    row_lon = jnp.where(
        lane < WEST_ROW, col * LONS + lane % LONS, jnp.where(lane < EAST_ROW, west_lon, east_lon)
    )
    west_col = (col + columns - 1) % columns
    east_col = (col + 1) % columns

    def links_of(b, target):
        row = jnp.zeros((1, CAP), F32)
        for j in range(blocks):
            row = row + jnp.where(owners[j] == target, links[b][j], 0.0)
        return row

    def places(site, owner):
        site = site.astype(jnp.int32)
        lev = site // (LONS * LATS)
        lon = owner.astype(jnp.int32) * LONS + site // LATS % LONS
        return lev.astype(F32), lon.astype(F32), (site % LATS).astype(F32)

    def lon_square(a, b):
        gap = jnp.abs(a - b)
        gap = jnp.minimum(gap, lon_all - gap) * (1.0 / (2.0 * LONS))
        return 1.0 + gap * gap

    def lev_square(a, b):
        gap = (a - b) * 0.5
        return 1.0 + gap * gap

    def lat_square(a, b):
        gap = (a - b) * (1.0 / (LATS // 8))
        return 1.0 + gap * gap

    def slots_of(b, k):
        start = k * CHUNK if isinstance(k, int) else pl.multiple_of(k * CHUNK, CHUNK)
        tall = packed[b, pl.ds(start, CHUNK), :]
        return tall, tall.T

    def centred_parts(x):
        x = x - jnp.sum(x, 0, keepdims=True) * (1.0 / members)
        high, low = halves(x)
        return jnp.concatenate([high, low, high, jnp.zeros((16, x.shape[1]), BF16)], 0)

    def batch_terms(b, k):
        tall, wide = slots_of(b, k)
        occupied = wide[place["occupied"] : place["occupied"] + 1]
        if b == 0:
            prior = wide[:members]
        else:
            prior = jnp.concatenate([fields[EXT_ROWS + 2 * k], fields[EXT_ROWS + 2 * k + 1]], 1) * occupied
        value = wide[place["value"] : place["value"] + 1]
        noise = jnp.where(occupied > 0, wide[place["noise"] : place["noise"] + 1], 1.0)
        mean = jnp.sum(prior, 0, keepdims=True) / members
        anomaly = prior - mean
        spread = jnp.sum(anomaly * anomaly, 0, keepdims=True) * denominator
        total = spread + noise
        shrink = 1.0 / (1.0 + jnp.sqrt(noise / total))
        gain = ((value - mean) - shrink * anomaly) / total
        high = anomaly.astype(BF16).astype(F32)
        sides = jnp.concatenate([high, high, anomaly - high, jnp.zeros((16, CHUNK), F32)], 0)
        sides = sides.T.astype(BF16)
        gain_high, gain_low = halves(gain)
        gains = jnp.concatenate([gain_high, gain_low], 0)

        def column(name):
            return tall[:, place[name] : place[name] + 1]

        lev, lon, lat = places(column("site"), column("owner"))
        holder = jnp.where(lane.astype(F32) == column("owner"), 1.0, 0.0)
        weight = jnp.where(
            lane < WEST_ROW,
            jnp.sum(holder * links_of(b, col), 1, keepdims=True),
            jnp.where(
                lane < EAST_ROW,
                jnp.sum(holder * links_of(b, west_col), 1, keepdims=True),
                jnp.sum(holder * links_of(b, east_col), 1, keepdims=True),
            ),
        )
        row_part = weight * denominator / (
            lev_square(row_lev.astype(F32), lev) * lon_square(row_lon.astype(F32), lon)
        )
        lat_part = 1.0 / lat_square(lane.astype(F32), lat)
        return sides, gains, row_part, lat_part, (lev, lon, lat, holder)

    def increment(x, sides, gains, local):
        weighted = dot(sides, centred_parts(x)) * local
        high, low = halves(weighted)
        first = dot(gains, high)
        return (first[:members] + first[members:]) + dot(gains[:members], low)

    def site_weights(where0, k1):
        lev0, lon0, lat0, holder = where0
        tall, wide = slots_of(1, k1)
        owner = wide[place["owner"] : place["owner"] + 1]
        lev, lon, lat = places(wide[place["site"] : place["site"] + 1], owner)
        pad = (-blocks) % 16
        spare = [jnp.zeros((pad, CAP), F32)] if pad else []
        table = jnp.concatenate(links[0] + spare, 0).astype(BF16)
        by_block = dot_lanes(holder.astype(BF16), table).astype(BF16)
        spare = [jnp.zeros((pad, CHUNK), F32)] if pad else []
        there = [jnp.where(owner == owners[j].astype(F32), 1.0, 0.0) for j in range(blocks)]
        weight = dot(by_block, jnp.concatenate(there + spare, 0).astype(BF16))
        square = lat_square(lat0, lat) * lon_square(lon0, lon) * lev_square(lev0, lev)
        return weight * denominator / square, wide

    direct = chunks == 1

    def analyse(b):
        if not direct:
            gained[...] = jnp.zeros_like(gained)

        def chunk(k):
            sides, gains, row_part, lat_part, where = batch_terms(b, k)
            if b == 0:

                def site_chunk(k1):
                    local, wide = site_weights(where, k1)
                    x = wide[:members]
                    moved = increment(x, sides, gains, local) * wide[members : members + 1]
                    for h in range(2):
                        at = EXT_ROWS + 2 * k1 + h
                        piece = slice(h * LATS, (h + 1) * LATS)
                        if direct:
                            fields[at] = x[:, piece] + moved[:, piece]
                        else:
                            before = jnp.where(k == 0, x[:, piece], fields[at])
                            fields[at] = before + moved[:, piece]

                for_each(chunks, site_chunk)
            for r in range(0, EXT_ROWS, 2):
                x = jnp.concatenate([fields[r], fields[r + 1]], 1)
                local = jnp.concatenate(
                    [lat_part * row_part[:, r : r + 1], lat_part * row_part[:, r + 1 : r + 2]], 1
                )
                moved = increment(x, sides, gains, local)
                moved = moved * jnp.concatenate([ocean[r], ocean[r + 1]], 1)
                for h in range(2):
                    piece = slice(h * LATS, (h + 1) * LATS)
                    if direct:
                        fields[r + h] = x[:, piece] + moved[:, piece]
                    else:
                        gained[r + h] = gained[r + h] + moved[:, piece]

        for_each(chunks, chunk)
        if not direct:
            for r in range(EXT_ROWS):
                fields[r] = fields[r] + gained[r]

    for b in range(BATCHES):
        analyse(b)

    lower = jnp.where(odd == 0, Y_ROW, CORE_ROW)
    upper = jnp.where(odd == 0, CORE_ROW, Y_ROW)
    for r in range(ROWS):
        lev, lon = r // LONS, r % LONS
        x = fields[r]
        lon_next = fields[r + 1] if lon < LONS - 1 else fields[EAST_ROW + lev]
        lon_prev = fields[r - 1] if lon > 0 else fields[WEST_ROW + lev]
        lat_next = jnp.where(lane < LATS - 1, pltpu.roll(x, LATS - 1, 1), 0.0)
        lat_prev = jnp.where(lane > 0, pltpu.roll(x, 1, 1), 0.0)
        vertical = fields[r ^ LONS] + fields[(lower if lev == 0 else upper) + lon]
        tendency = (
            -0.5 * zonal[r : r + 1, :] * (lon_next - lon_prev)
            + LATERAL_MIX * (lon_next + lon_prev + lat_next + lat_prev - 4.0 * x)
            + VERTICAL_MIX * (vertical - 2.0 * x)
        )
        out[pl.ds(r, members, stride=ROWS), :] = x + ocean[lon] * tendency


def swapped(x, axis, bit):
    return lax.ppermute(x, axis, [(i, i ^ bit) for i in range(lax.axis_size(axis))])


def shifted(x, axis, by):
    count = lax.axis_size(axis)
    return lax.ppermute(x, axis, [(i, (i + by) % count) for i in range(count)])


def local(state, observation_site, obs_count, measured_values, observation_noise, loc_pattern, ocean_mask, zonal_current):
    members = state.shape[0]
    columns = lax.axis_size("col")
    floors = lax.axis_size("gz")
    col = lax.axis_index("col").astype(jnp.int32)
    gz = lax.axis_index("gz").astype(jnp.int32)
    core = gz % 2
    vmem = pl.BlockSpec(memory_space=pltpu.VMEM)
    smem = pl.BlockSpec(memory_space=pltpu.SMEM)
    height = members + 8

    mask = ocean_mask.astype(F32)
    flat = state.reshape(members * ROWS, LATS)
    scal = jnp.stack([col, gz, obs_count[0, 0], obs_count[1, 0]])
    links = jnp.pad(loc_pattern[:, :, 0].astype(F32), ((0, 0), (0, CAP - columns)))

    payload = pl.pallas_call(
        functools.partial(pick_kernel, members),
        out_shape=jax.ShapeDtypeStruct((BATCHES, height, CAP), F32),
        in_specs=[smem] + [vmem] * 6,
        out_specs=vmem,
        name="pick_priors",
    )(scal, observation_site, measured_values, observation_noise, links, mask, flat)

    core_edge = swapped(lax.dynamic_index_in_dim(state, 1 - core, 1, False), "gz", 1)
    ends = [(i, i + 1) for i in range(1, floors - 1, 2)]
    y_edge = lax.ppermute(
        lax.dynamic_index_in_dim(state, core, 1, False), "gz", ends + [(j, i) for i, j in ends]
    )
    lon_edges = []
    for lon, by in ((LONS - 1, 1), (0, -1)):
        edge = jnp.concatenate(
            [state[:, :, lon, :].reshape(members * LEVS, LATS), jnp.broadcast_to(mask[lon : lon + 1], (8, LATS))], 0
        )
        lon_edges.append(shifted(edge, "col", by))
    west, east = lon_edges

    mine = lax.dynamic_index_in_dim(payload, core, 0, False)
    given = lax.dynamic_index_in_dim(payload, 1 - core, 0, False)
    mine = mine + swapped(given, "gz", 1)
    bit = 2
    while bit < floors:
        mine = mine + swapped(mine, "gz", bit)
        bit *= 2
    if columns <= 2 * WINDOW + 1 and columns & (columns - 1) == 0:
        around = None
        pair = jnp.stack([mine, swapped(mine, "col", 1)])
        gathered = jnp.concatenate([pair] + [swapped(pair, "col", bit) for bit in range(2, columns, 2)])
    else:
        reach = min(WINDOW, (columns - 1) // 2)
        around = tuple(range(-reach, columns - reach)) if columns <= 2 * WINDOW + 1 else tuple(range(-WINDOW, WINDOW + 1))
        gathered = jnp.stack([mine if by == 0 else shifted(mine, "col", -by) for by in around])
    blocks = gathered.shape[0]
    other = swapped(gathered, "gz", 1)

    slots = min(blocks * CAP, MEAN_COUNT * columns)
    chunks = -(-slots // CHUNK)
    rows = EXT_ROWS + 2 * chunks
    out = pl.pallas_call(
        functools.partial(step_kernel, members, blocks, columns, around, chunks),
        out_shape=jax.ShapeDtypeStruct((members * ROWS, LATS), F32),
        in_specs=[smem] + [vmem] * 9,
        out_specs=vmem,
        scratch_shapes=[
            pltpu.VMEM((BATCHES, chunks * CHUNK + CAP, CAP), F32),
            pltpu.VMEM((rows, members, LATS), F32),
            pltpu.VMEM((EXT_ROWS if chunks > 1 else 1, members, LATS), F32),
        ],
        compiler_params=pltpu.CompilerParams(vmem_limit_bytes=48 * 1024 * 1024),
        name="analyse_and_step",
    )(
        scal,
        gathered,
        other,
        flat,
        core_edge.reshape(members * LONS, LATS),
        y_edge.reshape(members * LONS, LATS),
        west,
        east,
        mask,
        zonal_current.reshape(ROWS, LATS),
    )
    return out.reshape(state.shape)


def solution(mesh):
    in_specs = (
        P(None, "gz", "col", None),
        P(),
        P(None, "col"),
        P(None, "col"),
        P(None, "col"),
        P(None, None, "col"),
        P("col", None),
        P("gz", "col", None),
    )
    out_specs = P(None, "gz", "col", None)
    return jax.shard_map(local, mesh=mesh, in_specs=in_specs, out_specs=out_specs, check_vma=False)
```

profile of v0, /device:TPU:0, one launch (start us, length us, event | category | flops | bytes accessed | tf_op | source)
XLA Modules:
  0.0 48.4 jit_solution(8113540654332727684)
XLA Ops:
  0.0 0.0 copy-start
  0.0 0.7 %convert_element_type.11 = f32[2,8,1]{1,2,0:T(1,128)S(1)} convert(s32[2,8,1]{1,2,0:T(1,128)} %param.13) | non-fusion elementwise | flops 16 | bytes 128 | tf_op jit(solution)/shard_map/convert_element_type | solution.py:348
  0.8 1.3 %fusion.1 = (s32[1,1]{0,1:T(1,128)}, s32[1,1]{0,1:T(1,128)}) fusion(s32[2,1]{0,1:T(1,128)} %param.10), kind=kLoop, calls=%fused_computation.16 | loop fusion | bytes 16 | tf_op jit(solution)/shard_map/slice | solution.py:347
  2.1 1.3 %convert_element_type.13.mask = f32[8,128]{1,0:T(8,128)} convert(s32[8,128]{1,0:T(8,128)} %param.14) | non-fusion elementwise | flops 1024 | bytes 8192 | tf_op jit(solution)/shard_map/convert_element_type | solution.py:345
  3.4 0.5 %pad.4.links = f32[2,128]{1,0:T(2,128)} pad(f32[2,8]{1,0:T(2,128)S(1)} %bitcast.37, f32[]{:T(128)} %constant.35.clone.1), padding=0_0x0_120 | pad | bytes 1092 | tf_op jit(solution)/shard_map/jit(_pad)/pad | solution.py:348
  3.9 1.9 %pad_add_fusion.scal = s32[4]{0:T(128)} fusion(s32[1]{0:T(128)} %bitcast.3, s32[1]{0:T(128)} %bitcast.2, s32[1]{0:T(128)} %bitcast.1, s32[1]{0:T(128)} %bitcast), kind=kLoop, calls=%fused_computation.12 | loop fusion | flops 12 | bytes 32 | tf_op jit(solution)/shard_map/stack | solution.py:347
  5.9 2.3 %pick_priors.1 = f32[2,88,128]{2,1,0:T(8,128)} custom-call(s32[4]{0:T(128)} %pad_add_fusion.scal, s32[2,1024]{1,0:T(2,128)} %site.1, f32[2,128]{1,0:T(2,128)} %value.1, f32[2,128]{1,0:T(2,128)} %noise.1, f32[2,128]{1,0:T(2,128)} %pad.4.links, f32[8,128]{1,0:T(8,128)} %convert_element_type.13.mask, f32[1280,128]{1,0:T(8,128)} %bitcast.28), custom_call_target="tpu_custom_call" | custom-call | tf_op jit(solution)/shard_map/pick_priors/pallas_call | solution.py:350
  8.2 0.0 copy-start.4
  8.2 0.9 %dynamic-slice_bitcast_fusion.2 = f32[88,128]{1,0:T(8,128)S(1)} fusion(f32[2,88,128]{2,1,0:T(8,128)} %pick_priors.1, s32[]{:T(128)S(6)} %select_n.19), kind=kLoop, calls=%fused_computation.6 | loop fusion | bytes 90116 | tf_op jit(solution)/shard_map/jit(dynamic_index_in_dim)/squeeze | solution.py:372
  9.1 0.4 collective-permute-start
  9.5 0.9 %collective-permute-done = f32[88,128]{1,0:T(8,128)S(1)} collective-permute-done((f32[88,128]{1,0:T(8,128)S(1)}, f32[88,128]{1,0:T(8,128)S(1)}, u32[]{:S(2)}, u32[]{:S(2)}) %collective-permute-start) | collective-permute-done | bytes 45088 | tf_op jit(solution)/shard_map/ppermute | solution.py:326
  10.4 0.0 copy-done.4
  10.4 2.9 %collective-permute-start.1 = (f32[88,128]{1,0:T(8,128)S(1)}, f32[88,128]{1,0:T(8,128)S(1)}, u32[]{:S(2)}, u32[]{:S(2)}) collective-permute-start(f32[88,128]{1,0:T(8,128)S(1)} %bitcast_add_fusion), channel_id=1, source_target_pairs={{0,2},{1,3},{2,0},{3,1},{4,6},{5,7},{6,4},{7,5},{8,10},{9,11},{10,... | collective-permute-start | bytes 135176 | tf_op jit(solution)/shard_map/ppermute | solution.py:326
  13.3 0.0 copy-done
  13.4 0.7 %collective-permute-start.8 = (f32[80,8,128]{2,1,0:T(8,128)S(1)}, f32[80,8,128]{2,1,0:T(8,128)S(1)}, u32[]{:S(2)}, u32[]{:S(2)}) collective-permute-start(f32[80,8,128]{2,1,0:T(8,128)S(1)} %get-tuple-element.9), channel_id=1, source_target_pairs={{1,2},{2,1},{5,6},{6,5},{9,10},{10,9},{13,14},{14,13},{17,18},{18,... | collective-permute-start | bytes 983048 | tf_op jit(solution)/shard_map/ppermute | solution.py:360
  14.1 1.4 %collective-permute-start.7 = (f32[80,8,128]{2,1,0:T(8,128)S(1)}, f32[80,8,128]{2,1,0:T(8,128)S(1)}, u32[]{:S(2)}, u32[]{:S(2)}) collective-permute-start(f32[80,8,128]{2,1,0:T(8,128)S(1)} %get-tuple-element.10), channel_id=1, source_target_pairs={{0,1},{1,0},{2,3},{3,2},{4,5},{5,4},{6,7},{7,6},{8,9},{9,8},{10,11... | collective-permute-start | bytes 983048 | tf_op jit(solution)/shard_map/ppermute | solution.py:326
  15.5 0.0 collective-permute-done.1
  15.5 2.0 %collective-permute-start.2 = (f32[88,128]{1,0:T(8,128)S(1)}, f32[88,128]{1,0:T(8,128)S(1)}, u32[]{:S(2)}, u32[]{:S(2)}) collective-permute-start(f32[88,128]{1,0:T(8,128)S(1)} %get-tuple-element.6), channel_id=1, source_target_pairs={{0,4},{4,0},{8,12},{12,8},{16,20},{20,16},{24,28},{28,24},{1,5},{5... | collective-permute-start | bytes 135176 | tf_op jit(solution)/shard_map/ppermute | solution.py:326
  17.6 0.1 fusion
  17.7 2.0 %collective-permute-done.2 = f32[88,128]{1,0:T(8,128)S(1)} collective-permute-done((f32[88,128]{1,0:T(8,128)S(1)}, f32[88,128]{1,0:T(8,128)S(1)}, u32[]{:S(2)}, u32[]{:S(2)}) %collective-permute-start.2) | collective-permute-done | bytes 45088 | tf_op jit(solution)/shard_map/ppermute | solution.py:326
  19.7 4.1 %collective-permute-start.5 = (f32[2,88,128]{2,1,0:T(8,128)S(1)}, f32[2,88,128]{2,1,0:T(8,128)S(1)}, u32[]{:S(2)}, u32[]{:S(2)}) collective-permute-start(f32[2,88,128]{2,1,0:T(8,128)S(1)} %pad_maximum_fusion), channel_id=1, source_target_pairs={{0,24},{4,28},{8,16},{12,20},{16,8},{20,12},{24,0},{28,4},{1,25},{... | collective-permute-start | bytes 270344 | tf_op jit(solution)/shard_map/ppermute | solution.py:326
  23.8 0.0 collective-permute-start.4
  23.8 0.6 %collective-permute-start.3 = (f32[2,88,128]{2,1,0:T(8,128)S(1)}, f32[2,88,128]{2,1,0:T(8,128)S(1)}, u32[]{:S(2)}, u32[]{:S(2)}) collective-permute-start(f32[2,88,128]{2,1,0:T(8,128)S(1)} %pad_maximum_fusion), channel_id=1, source_target_pairs={{0,8},{4,12},{8,0},{12,4},{16,24},{20,28},{24,16},{28,20},{1,9},{5... | collective-permute-start | bytes 270344 | tf_op jit(solution)/shard_map/ppermute | solution.py:326
  24.4 4.2 %collective-permute-done.3 = f32[2,88,128]{2,1,0:T(8,128)S(1)} collective-permute-done((f32[2,88,128]{2,1,0:T(8,128)S(1)}, f32[2,88,128]{2,1,0:T(8,128)S(1)}, u32[]{:S(2)}, u32[]{:S(2)}) %collective-permute-start.3) | collective-permute-done | bytes 90144 | tf_op jit(solution)/shard_map/ppermute | solution.py:326
  28.6 1.9 %collective-permute-done.4 = f32[2,88,128]{2,1,0:T(8,128)S(1)} collective-permute-done((f32[2,88,128]{2,1,0:T(8,128)S(1)}, f32[2,88,128]{2,1,0:T(8,128)S(1)}, u32[]{:S(2)}, u32[]{:S(2)}) %collective-permute-start.4) | collective-permute-done | bytes 90144 | tf_op jit(solution)/shard_map/ppermute | solution.py:326
  30.6 0.0 copy-start.1
  30.6 0.0 collective-permute-done.5
  30.6 0.1 collective-permute-start.6
  30.7 0.6 %copy-done.1 = f32[8,128]{1,0:T(8,128)S(1)} copy-done((f32[8,128]{1,0:T(8,128)S(1)}, f32[8,128]{1,0:T(8,128)}, u32[]{:S(2)}) %copy-start.1) | copy-done | bytes 4120
  31.3 1.5 %collective-permute-start.9 = (f32[168,128]{1,0:T(8,128)S(1)}, f32[168,128]{1,0:T(8,128)S(1)}, u32[]{:S(2)}, u32[]{:S(2)}) collective-permute-start(f32[168,128]{1,0:T(8,128)S(1)} %pad_maximum_fusion.1), channel_id=1, source_target_pairs={{0,4},{4,8},{8,12},{12,16},{16,20},{20,24},{24,28},{28,0},{1,5},{5... | collective-permute-start | bytes 258056 | tf_op jit(solution)/shard_map/ppermute | solution.py:331
  32.8 0.0 copy-start.2
  32.8 3.3 %collective-permute-start.10 = (f32[168,128]{1,0:T(8,128)S(1)}, f32[168,128]{1,0:T(8,128)S(1)}, u32[]{:S(2)}, u32[]{:S(2)}) collective-permute-start(f32[168,128]{1,0:T(8,128)S(1)} %pad_maximum_fusion.2), channel_id=1, source_target_pairs={{0,28},{4,0},{8,4},{12,8},{16,12},{20,16},{24,20},{28,24},{1,29},{... | collective-permute-start | bytes 258056 | tf_op jit(solution)/shard_map/ppermute | solution.py:331
  36.1 2.4 %collective-permute-done.9.west = f32[168,128]{1,0:T(8,128)S(1)} collective-permute-done((f32[168,128]{1,0:T(8,128)S(1)}, f32[168,128]{1,0:T(8,128)S(1)}, u32[]{:S(2)}, u32[]{:S(2)}) %collective-permute-start.9) | collective-permute-done | bytes 86048 | tf_op jit(solution)/shard_map/ppermute | solution.py:331
  38.6 0.6 %collective-permute-done.10.east = f32[168,128]{1,0:T(8,128)S(1)} collective-permute-done((f32[168,128]{1,0:T(8,128)S(1)}, f32[168,128]{1,0:T(8,128)S(1)}, u32[]{:S(2)}, u32[]{:S(2)}) %collective-permute-start.10) | collective-permute-done | bytes 86048 | tf_op jit(solution)/shard_map/ppermute | solution.py:331
  39.2 0.0 collective-permute-done.8
  39.2 0.0 collective-permute-done.7
  39.2 0.0 collective-permute-done.6.other
  39.2 0.0 copy-start.3
  39.2 0.0 copy-done.2
  39.2 0.7 %copy-done.3 = s32[4]{0:T(128)S(1)} copy-done((s32[4]{0:T(128)S(1)}, s32[4]{0:T(128)}, u32[]{:S(2)}) %copy-start.3) | copy-done | bytes 40
  39.9 8.5 %analyse_and_step.1 = f32[1280,128]{1,0:T(8,128)} custom-call(s32[4]{0:T(128)S(1)} %copy-done.3, f32[8,88,128]{2,1,0:T(8,128)S(1)} %constant_dynamic-update-slice_fusion.mine, f32[8,88,128]{2,1,0:T(8,128)S(1)} %collective-permute-done.6.other, f32[1280,128]{1,0:T(8,128)S(1)} %bitcast.29, f32[640,128]{1,0:T(8,128)S(1)} %bitcast.31, f32[640,128]{1,0:T(8,128)S(1)} %bitcast.30, ...), custom_call_target="tpu_custom_call" | custom-call | tf_op jit(solution)/shard_map/analyse_and_step/pallas_call | solution.py:392
  (13 shorter events, 0.1 us)
Async XLA Ops:
  0.0 13.3 %copy-start = (f32[80,2,8,128]{3,2,1,0:T(8,128)S(1)}, f32[80,2,8,128]{3,2,1,0:T(8,128)}, u32[]{:S(2)}) copy-start(f32[80,2,8,128]{3,2,1,0:T(8,128)} %param.8) | copy-start | bytes 1966084
  8.2 2.2 %copy-start.4 = (f32[2,88,128]{2,1,0:T(8,128)S(1)}, f32[2,88,128]{2,1,0:T(8,128)}, u32[]{:S(2)}) copy-start(f32[2,88,128]{2,1,0:T(8,128)} %pick_priors.1) | copy-start | bytes 270340
  9.1 1.3 %collective-permute-start = (f32[88,128]{1,0:T(8,128)S(1)}, f32[88,128]{1,0:T(8,128)S(1)}, u32[]{:S(2)}, u32[]{:S(2)}) collective-permute-start(f32[88,128]{1,0:T(8,128)S(1)} %dynamic-slice_bitcast_fusion.2), channel_id=1, source_target_pairs={{0,1},{1,0},{2,3},{3,2},{4,5},{5,4},{6,7},{7,6},{8,9},{9,8},{10,11... | collective-permute-start | bytes 135176 | tf_op jit(solution)/shard_map/ppermute | solution.py:326
  10.4 5.1 %collective-permute-start.1 = (f32[88,128]{1,0:T(8,128)S(1)}, f32[88,128]{1,0:T(8,128)S(1)}, u32[]{:S(2)}, u32[]{:S(2)}) collective-permute-start(f32[88,128]{1,0:T(8,128)S(1)} %bitcast_add_fusion), channel_id=1, source_target_pairs={{0,2},{1,3},{2,0},{3,1},{4,6},{5,7},{6,4},{7,5},{8,10},{9,11},{10,... | collective-permute-start | bytes 135176 | tf_op jit(solution)/shard_map/ppermute | solution.py:326
  13.4 25.8 %collective-permute-start.8 = (f32[80,8,128]{2,1,0:T(8,128)S(1)}, f32[80,8,128]{2,1,0:T(8,128)S(1)}, u32[]{:S(2)}, u32[]{:S(2)}) collective-permute-start(f32[80,8,128]{2,1,0:T(8,128)S(1)} %get-tuple-element.9), channel_id=1, source_target_pairs={{1,2},{2,1},{5,6},{6,5},{9,10},{10,9},{13,14},{14,13},{17,18},{18,... | collective-permute-start | bytes 983048 | tf_op jit(solution)/shard_map/ppermute | solution.py:360
  14.1 25.1 %collective-permute-start.7 = (f32[80,8,128]{2,1,0:T(8,128)S(1)}, f32[80,8,128]{2,1,0:T(8,128)S(1)}, u32[]{:S(2)}, u32[]{:S(2)}) collective-permute-start(f32[80,8,128]{2,1,0:T(8,128)S(1)} %get-tuple-element.10), channel_id=1, source_target_pairs={{0,1},{1,0},{2,3},{3,2},{4,5},{5,4},{6,7},{7,6},{8,9},{9,8},{10,11... | collective-permute-start | bytes 983048 | tf_op jit(solution)/shard_map/ppermute | solution.py:326
  15.5 4.1 %collective-permute-start.2 = (f32[88,128]{1,0:T(8,128)S(1)}, f32[88,128]{1,0:T(8,128)S(1)}, u32[]{:S(2)}, u32[]{:S(2)}) collective-permute-start(f32[88,128]{1,0:T(8,128)S(1)} %get-tuple-element.6), channel_id=1, source_target_pairs={{0,4},{4,0},{8,12},{12,8},{16,20},{20,16},{24,28},{28,24},{1,5},{5... | collective-permute-start | bytes 135176 | tf_op jit(solution)/shard_map/ppermute | solution.py:326
  19.7 10.9 %collective-permute-start.5 = (f32[2,88,128]{2,1,0:T(8,128)S(1)}, f32[2,88,128]{2,1,0:T(8,128)S(1)}, u32[]{:S(2)}, u32[]{:S(2)}) collective-permute-start(f32[2,88,128]{2,1,0:T(8,128)S(1)} %pad_maximum_fusion), channel_id=1, source_target_pairs={{0,24},{4,28},{8,16},{12,20},{16,8},{20,12},{24,0},{28,4},{1,25},{... | collective-permute-start | bytes 270344 | tf_op jit(solution)/shard_map/ppermute | solution.py:326
  23.8 6.8 %collective-permute-start.4 = (f32[2,88,128]{2,1,0:T(8,128)S(1)}, f32[2,88,128]{2,1,0:T(8,128)S(1)}, u32[]{:S(2)}, u32[]{:S(2)}) collective-permute-start(f32[2,88,128]{2,1,0:T(8,128)S(1)} %pad_maximum_fusion), channel_id=1, source_target_pairs={{0,16},{4,20},{8,24},{12,28},{16,0},{20,4},{24,8},{28,12},{1,17},{... | collective-permute-start | bytes 270344 | tf_op jit(solution)/shard_map/ppermute | solution.py:326
  23.8 4.8 %collective-permute-start.3 = (f32[2,88,128]{2,1,0:T(8,128)S(1)}, f32[2,88,128]{2,1,0:T(8,128)S(1)}, u32[]{:S(2)}, u32[]{:S(2)}) collective-permute-start(f32[2,88,128]{2,1,0:T(8,128)S(1)} %pad_maximum_fusion), channel_id=1, source_target_pairs={{0,8},{4,12},{8,0},{12,4},{16,24},{20,28},{24,16},{28,20},{1,9},{5... | collective-permute-start | bytes 270344 | tf_op jit(solution)/shard_map/ppermute | solution.py:326
  30.6 0.7 %copy-start.1 = (f32[8,128]{1,0:T(8,128)S(1)}, f32[8,128]{1,0:T(8,128)}, u32[]{:S(2)}) copy-start(f32[8,128]{1,0:T(8,128)} %convert_element_type.13.mask) | copy-start | bytes 12292
  30.6 8.6 %collective-permute-start.6 = (f32[8,88,128]{2,1,0:T(8,128)S(1)}, f32[8,88,128]{2,1,0:T(8,128)S(1)}, u32[]{:S(2)}, u32[]{:S(2)}) collective-permute-start(f32[8,88,128]{2,1,0:T(8,128)S(1)} %constant_dynamic-update-slice_fusion.mine), channel_id=1, source_target_pairs={{0,1},{1,0},{2,3},{3,2},{4,5},{5,4},{6,7},{7,6},{8,9},{9,8},{10,11... | collective-permute-start | bytes 1081352 | tf_op jit(solution)/shard_map/ppermute | solution.py:326
  31.3 7.3 %collective-permute-start.9 = (f32[168,128]{1,0:T(8,128)S(1)}, f32[168,128]{1,0:T(8,128)S(1)}, u32[]{:S(2)}, u32[]{:S(2)}) collective-permute-start(f32[168,128]{1,0:T(8,128)S(1)} %pad_maximum_fusion.1), channel_id=1, source_target_pairs={{0,4},{4,8},{8,12},{12,16},{16,20},{20,24},{24,28},{28,0},{1,5},{5... | collective-permute-start | bytes 258056 | tf_op jit(solution)/shard_map/ppermute | solution.py:331
  32.8 6.4 %copy-start.2 = (f32[2,8,128]{2,1,0:T(8,128)S(1)}, f32[2,8,128]{2,1,0:T(8,128)}, u32[]{:S(2)}) copy-start(f32[2,8,128]{2,1,0:T(8,128)} %param.15) | copy-start | bytes 24580
  32.8 6.4 %collective-permute-start.10 = (f32[168,128]{1,0:T(8,128)S(1)}, f32[168,128]{1,0:T(8,128)S(1)}, u32[]{:S(2)}, u32[]{:S(2)}) collective-permute-start(f32[168,128]{1,0:T(8,128)S(1)} %pad_maximum_fusion.2), channel_id=1, source_target_pairs={{0,28},{4,0},{8,4},{12,8},{16,12},{20,16},{24,20},{28,24},{1,29},{... | collective-permute-start | bytes 258056 | tf_op jit(solution)/shard_map/ppermute | solution.py:331
  39.2 0.7 %copy-start.3 = (s32[4]{0:T(128)S(1)}, s32[4]{0:T(128)}, u32[]{:S(2)}) copy-start(s32[4]{0:T(128)} %pad_add_fusion.scal) | copy-start | bytes 52
where the time goes:
time: 48.7 us; the launch traced here: 48.4 us
  starting transfers between devices  17.2 us (35%)
  waiting for transfers between devices  12.1 us (25%)
  Pallas kernels  10.9 us (22%)
  local copies, waits for them, and re-layouts  4.18 us (9%)
  other arithmetic  4.01 us (8%)
    ppermute x8, starting transfers between devices, swapped(): lax.ppermute(x, axis, [(i, i ^ bit) for i in range(lax.axis_size(axis))])  11.7 us
    ppermute x8, waiting for transfers between devices, swapped(): lax.ppermute(x, axis, [(i, i ^ bit) for i in range(lax.axis_size(axis))])  8.98 us
    pallas_call x1, Pallas kernels, local(): pl.pallas_call(functools.partial(step_kernel, members, blocks, columns, a...  8.55 us
    ppermute x2, starting transfers between devices, shifted(): return lax.ppermute(x, axis, [(i, (i + by) % count) for i in range(count)])  4.82 us
    ppermute x2, waiting for transfers between devices, shifted(): return lax.ppermute(x, axis, [(i, (i + by) % count) for i in range(count)])  3.1 us
    pallas_call x1, Pallas kernels, local(): pl.pallas_call(functools.partial(pick_kernel, members), out_shape=jax.Sha...  2.33 us
    another operation x1, other arithmetic, local(): scal = jnp.stack([col, gz, obs_count[0, 0], obs_count[1, 0]])  1.94 us
    slice x1, local copies, waits for them, and re-layouts, local(): scal = jnp.stack([col, gz, obs_count[0, 0], obs_count[1, 0]])  1.35 us
  transfers between devices with their start and end apart: 11, of which 6 were waited for; matrix products, arithmetic and copies ran while one was open for 0% of the time, Pallas kernels for 0%

commit v1 on v0

--- a/solution.py
+++ b/solution.py
@@ -21,8 +21,8 @@
 ROWS = LEVS * LONS
 CORE_ROW = 16
 Y_ROW = 24
-WEST_ROW = 32
-EAST_ROW = 34
+INNER_ROW = 32
+OUTER_ROW = 34
 EXT_ROWS = 36
 
 LATERAL_MIX = 0.2
@@ -61,18 +61,24 @@
     return {name: members + i for i, name in enumerate(names)}
 
 
-def pick_kernel(members, scal, site, value, noise, links, mask, state, out):
-    col, gz = scal[0], scal[1]
+def position():
+    return lax.axis_index("col").astype(jnp.int32), lax.axis_index("gz").astype(jnp.int32)
+
+
+def pick_kernel(members, columns, count, linked, site, value, noise, mask, state, kept, core_send, y_send, inner, outer):
+    col, gz = position()
+    core = gz % 2
     lane = iota((1, CAP), 1)
+    at = pl.multiple_of(col * CAP, CAP)
     index, filled = [], []
     for b in range(BATCHES):
-        occupied = lane < scal[2 + b]
+        occupied = lane < count[b, 0]
         filled.append(occupied)
-        at = pl.multiple_of(col * CAP, CAP)
         index.append(jnp.where(occupied, site[b : b + 1, pl.ds(at, CAP)] - gz * CELLS, -1))
     wanted = jnp.concatenate(index, 1)
     total = jnp.zeros((3 * members + 16, BATCHES * CAP), F32)
     cell = iota((2 * LATS, BATCHES * CAP), 0)
+    ocean = mask[...].astype(F32)
     for pair in range(ROWS // 2):
         left = []
         for r in (2 * pair, 2 * pair + 1):
@@ -82,51 +88,82 @@
             middle = rest.astype(BF16)
             low = (rest - middle.astype(F32)).astype(BF16)
             lon = r % LONS
-            ocean = jnp.broadcast_to(mask[lon : lon + 1, :], (16, LATS)).astype(BF16)
-            left.append(jnp.concatenate([high, ocean, middle, low], 0))
+            row = jnp.broadcast_to(ocean[lon : lon + 1, :], (16, LATS)).astype(BF16)
+            left.append(jnp.concatenate([high, row, middle, low], 0))
         hit = jnp.where(cell + pair * 2 * LATS == wanted, 1.0, 0.0).astype(BF16)
         total = total + dot(jnp.concatenate(left, 1), hit)
     m = members
+    height = m + 8
     picked = (total[:m] + total[m + 16 : 2 * m + 16]) + total[2 * m + 16 :]
     first = jnp.where(gz == 0, 1.0, 0.0)
     for b in range(BATCHES):
         here = slice(b * CAP, (b + 1) * CAP)
         once = jnp.where(filled[b], first, 0.0)
-        at = pl.multiple_of(col * CAP, CAP)
-        out[b, :m, :] = picked[:, here]
+        links = jnp.zeros((1, CAP), F32)
+        for a in range(columns):
+            links = jnp.where(lane == a, linked[b, a, 0].astype(F32), links)
         tail = [
             total[m : m + 1, here],
             value[b : b + 1, :] * once,
             noise[b : b + 1, :] * once,
-            links[b : b + 1, :] * first,
+            links * first,
             site[b : b + 1, pl.ds(at, CAP)].astype(F32) * once,
             once,
             once * col.astype(F32),
-            jnp.full((1, CAP), scal[2 + b].astype(F32) * first),
+            jnp.full((1, CAP), count[b, 0].astype(F32) * first),
         ]
-        out[b, m:, :] = jnp.concatenate(tail, 0)
+        block = jnp.concatenate([picked[:, here]] + tail, 0)
+
+        @pl.when(core == b)
+        def _():
+            kept[...] = block
+
+        @pl.when(core != b)
+        def _():
+            core_send[:height, :] = block
+
+    for member in range(members):
+        up = state[pl.ds(pl.multiple_of(member * ROWS + (1 - core) * LONS, LONS), LONS), :]
+        core_send[height + member * LONS : height + (member + 1) * LONS, :] = up
+        down = state[pl.ds(pl.multiple_of(member * ROWS + core * LONS, LONS), LONS), :]
+        y_send[member * LONS : (member + 1) * LONS, :] = down
+    even = col % 2 == 0
+    for lev in range(LEVS):
+        west = state[pl.ds(lev * LONS, members, stride=ROWS), :]
+        east = state[pl.ds(lev * LONS + LONS - 1, members, stride=ROWS), :]
+        inner[lev * members : (lev + 1) * members, :] = jnp.where(even, east, west)
+        outer[lev * members : (lev + 1) * members, :] = jnp.where(even, west, east)
+    west = jnp.broadcast_to(ocean[:1], (8, LATS))
+    east = jnp.broadcast_to(ocean[LONS - 1 :], (8, LATS))
+    inner[LEVS * members :, :] = jnp.where(even, east, west)
+    outer[LEVS * members :, :] = jnp.where(even, west, east)
 
 
 def step_kernel(
-    members, blocks, columns, around, chunks,
-    scal, mine, other, state, core_edge, y_edge, west, east, mask, zonal, out,
-    packed, fields, gained,
+    members, parts, columns, around, chunks, mask, zonal, state, core_edge, y_edge, inner, outer, *rest
 ):
-    col, gz = scal[0], scal[1]
+    mine_parts, other_parts = rest[: len(parts)], rest[len(parts) : 2 * len(parts)]
+    out, packed, fields, gained = rest[2 * len(parts) :]
+    mine = [part.at[i] for part, size in zip(mine_parts, parts) for i in range(size)]
+    other = [part.at[i] for part, size in zip(other_parts, parts) for i in range(size)]
+    blocks = len(mine)
+    col, gz = position()
     odd = gz % 2
+    even_col = col % 2 == 0
     lon_all = columns * LONS
     place = rows_of(members)
     denominator = 1.0 / (members - 1)
     height = members + 8
     owners = [col ^ j if around is None else (col + around[j] + columns) % columns for j in range(blocks)]
 
+    inner_start = inner.shape[0] - (members * LEVS + 8)
     links = []
     packed[...] = jnp.zeros_like(packed)
     for b in range(BATCHES):
         start = 0
         own_links = []
         for j in range(blocks):
-            block = jnp.where(odd == b, mine[j], other[j])
+            block = jnp.where(odd == b, mine[j][:height, :], other[j][:height, :])
             own_links.append(block[place["links"] : place["links"] + 1, :])
             tall = jnp.concatenate([block, jnp.zeros((LATS - height, CAP), F32)], 0)
             packed[b, pl.ds(start, CAP), :] = tall.T
@@ -136,30 +173,37 @@
     for r in range(ROWS):
         fields[r] = state[pl.ds(r, members, stride=ROWS), :]
     for lon in range(LONS):
-        fields[CORE_ROW + lon] = core_edge[pl.ds(lon, members, stride=LONS), :]
+        fields[CORE_ROW + lon] = core_edge[pl.ds(height + lon, members, stride=LONS), :]
         fields[Y_ROW + lon] = y_edge[pl.ds(lon, members, stride=LONS), :]
     for lev in range(LEVS):
-        fields[WEST_ROW + lev] = west[pl.ds(lev, members, stride=LEVS), :]
-        fields[EAST_ROW + lev] = east[pl.ds(lev, members, stride=LEVS), :]
-    ocean = [mask[lon : lon + 1, :] for lon in range(LONS)] * 4
-    ocean += [west[members * LEVS : members * LEVS + 1, :]] * LEVS
-    ocean += [east[members * LEVS : members * LEVS + 1, :]] * LEVS
+        inner_at, outer_at = inner_start + lev * members, lev * members
+        fields[INNER_ROW + lev] = inner[inner_at : inner_at + members, :]
+        fields[OUTER_ROW + lev] = outer[outer_at : outer_at + members, :]
+    dry = mask[...].astype(F32)
+    ocean = [dry[lon : lon + 1] for lon in range(LONS)] * 4
+    edge = members * LEVS
+    ocean += [inner[inner_start + edge : inner_start + edge + 1, :]] * LEVS
+    ocean += [outer[edge : edge + 1, :]] * LEVS
 
     lane = iota((1, LATS), 1)
     own = lane < ROWS
     near = (lane >= CORE_ROW) & (lane < Y_ROW)
-    far = (lane >= Y_ROW) & (lane < WEST_ROW)
+    far = (lane >= Y_ROW) & (lane < INNER_ROW)
     above, below = LEVS * gz + LEVS, LEVS * gz - 1
     row_lev = LEVS * gz + jnp.where(own, lane // LONS, lane % LEVS)
     row_lev = jnp.where(near, jnp.where(odd == 0, above, below), row_lev)
     row_lev = jnp.where(far, jnp.where(odd == 0, below, above), row_lev)
     west_lon = (col * LONS + lon_all - 1) % lon_all
     east_lon = (col * LONS + LONS) % lon_all
+    inner_lon = jnp.where(even_col, east_lon, west_lon)
+    outer_lon = jnp.where(even_col, west_lon, east_lon)
     row_lon = jnp.where(
-        lane < WEST_ROW, col * LONS + lane % LONS, jnp.where(lane < EAST_ROW, west_lon, east_lon)
+        lane < INNER_ROW, col * LONS + lane % LONS, jnp.where(lane < OUTER_ROW, inner_lon, outer_lon)
     )
     west_col = (col + columns - 1) % columns
     east_col = (col + 1) % columns
+    inner_col = jnp.where(even_col, east_col, west_col)
+    outer_col = jnp.where(even_col, west_col, east_col)
 
     def links_of(b, target):
         row = jnp.zeros((1, CAP), F32)
@@ -223,12 +267,12 @@
         lev, lon, lat = places(column("site"), column("owner"))
         holder = jnp.where(lane.astype(F32) == column("owner"), 1.0, 0.0)
         weight = jnp.where(
-            lane < WEST_ROW,
+            lane < INNER_ROW,
             jnp.sum(holder * links_of(b, col), 1, keepdims=True),
             jnp.where(
-                lane < EAST_ROW,
-                jnp.sum(holder * links_of(b, west_col), 1, keepdims=True),
-                jnp.sum(holder * links_of(b, east_col), 1, keepdims=True),
+                lane < OUTER_ROW,
+                jnp.sum(holder * links_of(b, inner_col), 1, keepdims=True),
+                jnp.sum(holder * links_of(b, outer_col), 1, keepdims=True),
             ),
         )
         row_part = weight * denominator / (
@@ -306,11 +350,13 @@
 
     lower = jnp.where(odd == 0, Y_ROW, CORE_ROW)
     upper = jnp.where(odd == 0, CORE_ROW, Y_ROW)
+    east_row = jnp.where(even_col, INNER_ROW, OUTER_ROW)
+    west_row = jnp.where(even_col, OUTER_ROW, INNER_ROW)
     for r in range(ROWS):
         lev, lon = r // LONS, r % LONS
         x = fields[r]
-        lon_next = fields[r + 1] if lon < LONS - 1 else fields[EAST_ROW + lev]
-        lon_prev = fields[r - 1] if lon > 0 else fields[WEST_ROW + lev]
+        lon_next = fields[r + 1] if lon < LONS - 1 else fields[east_row + lev]
+        lon_prev = fields[r - 1] if lon > 0 else fields[west_row + lev]
         lat_next = jnp.where(lane < LATS - 1, pltpu.roll(x, LATS - 1, 1), 0.0)
         lat_prev = jnp.where(lane > 0, pltpu.roll(x, 1, 1), 0.0)
         vertical = fields[r ^ LONS] + fields[(lower if lev == 0 else upper) + lon]
@@ -335,64 +381,53 @@
     members = state.shape[0]
     columns = lax.axis_size("col")
     floors = lax.axis_size("gz")
-    col = lax.axis_index("col").astype(jnp.int32)
-    gz = lax.axis_index("gz").astype(jnp.int32)
-    core = gz % 2
     vmem = pl.BlockSpec(memory_space=pltpu.VMEM)
     smem = pl.BlockSpec(memory_space=pltpu.SMEM)
     height = members + 8
-
-    mask = ocean_mask.astype(F32)
+    level = members * LONS
+    edge = members * LEVS + 8
     flat = state.reshape(members * ROWS, LATS)
-    scal = jnp.stack([col, gz, obs_count[0, 0], obs_count[1, 0]])
-    links = jnp.pad(loc_pattern[:, :, 0].astype(F32), ((0, 0), (0, CAP - columns)))
-
-    payload = pl.pallas_call(
-        functools.partial(pick_kernel, members),
-        out_shape=jax.ShapeDtypeStruct((BATCHES, height, CAP), F32),
-        in_specs=[smem] + [vmem] * 6,
-        out_specs=vmem,
+
+    def like(*lengths):
+        return [jax.ShapeDtypeStruct((length, LATS), F32) for length in lengths]
+
+    kept, core_send, y_send, inner, outer = pl.pallas_call(
+        functools.partial(pick_kernel, members, columns),
+        out_shape=like(height, height + level, level, edge, edge),
+        in_specs=[smem] * 2 + [vmem] * 5,
+        out_specs=[vmem] * 5,
         name="pick_priors",
-    )(scal, observation_site, measured_values, observation_noise, links, mask, flat)
-
-    core_edge = swapped(lax.dynamic_index_in_dim(state, 1 - core, 1, False), "gz", 1)
+    )(obs_count, loc_pattern, observation_site, measured_values, observation_noise, ocean_mask, flat)
+
+    core_edge = swapped(core_send, "gz", 1)
+    mine = kept + core_edge[:height]
     ends = [(i, i + 1) for i in range(1, floors - 1, 2)]
-    y_edge = lax.ppermute(
-        lax.dynamic_index_in_dim(state, core, 1, False), "gz", ends + [(j, i) for i, j in ends]
-    )
-    lon_edges = []
-    for lon, by in ((LONS - 1, 1), (0, -1)):
-        edge = jnp.concatenate(
-            [state[:, :, lon, :].reshape(members * LEVS, LATS), jnp.broadcast_to(mask[lon : lon + 1], (8, LATS))], 0
-        )
-        lon_edges.append(shifted(edge, "col", by))
-    west, east = lon_edges
-
-    mine = lax.dynamic_index_in_dim(payload, core, 0, False)
-    given = lax.dynamic_index_in_dim(payload, 1 - core, 0, False)
-    mine = mine + swapped(given, "gz", 1)
+    y_edge = lax.ppermute(y_send, "gz", ends + [(j, i) for i, j in ends])
+    ring = [(i, (i + 1) % columns) for i in range(1, columns, 2)]
+    outer = lax.ppermute(outer, "col", ring + [(j, i) for i, j in ring])
     bit = 2
     while bit < floors:
         mine = mine + swapped(mine, "gz", bit)
         bit *= 2
     if columns <= 2 * WINDOW + 1 and columns & (columns - 1) == 0:
         around = None
-        pair = jnp.stack([mine, swapped(mine, "col", 1)])
-        gathered = jnp.concatenate([pair] + [swapped(pair, "col", bit) for bit in range(2, columns, 2)])
+        inner = swapped(jnp.concatenate([mine, inner]), "col", 1)
+        pair = jnp.stack([mine, inner[:height]])
+        gathered = [pair] + [swapped(pair, "col", bit) for bit in range(2, columns, 2)]
     else:
-        reach = min(WINDOW, (columns - 1) // 2)
-        around = tuple(range(-reach, columns - reach)) if columns <= 2 * WINDOW + 1 else tuple(range(-WINDOW, WINDOW + 1))
-        gathered = jnp.stack([mine if by == 0 else shifted(mine, "col", -by) for by in around])
-    blocks = gathered.shape[0]
-    other = swapped(gathered, "gz", 1)
-
-    slots = min(blocks * CAP, MEAN_COUNT * columns)
+        inner = swapped(inner, "col", 1)
+        around = tuple(range(-WINDOW, WINDOW + 1)) if columns > 2 * WINDOW + 1 else tuple(range(columns))
+        gathered = [(mine if by == 0 else shifted(mine, "col", -by))[None] for by in around]
+    parts = tuple(part.shape[0] for part in gathered)
+    other = [swapped(part, "gz", 1) for part in gathered]
+
+    slots = min(sum(parts) * CAP, MEAN_COUNT * columns)
     chunks = -(-slots // CHUNK)
     rows = EXT_ROWS + 2 * chunks
     out = pl.pallas_call(
-        functools.partial(step_kernel, members, blocks, columns, around, chunks),
+        functools.partial(step_kernel, members, parts, columns, around, chunks),
         out_shape=jax.ShapeDtypeStruct((members * ROWS, LATS), F32),
-        in_specs=[smem] + [vmem] * 9,
+        in_specs=[vmem] * (7 + 2 * len(parts)),
         out_specs=vmem,
         scratch_shapes=[
             pltpu.VMEM((BATCHES, chunks * CHUNK + CAP, CAP), F32),
@@ -402,16 +437,7 @@
         compiler_params=pltpu.CompilerParams(vmem_limit_bytes=48 * 1024 * 1024),
         name="analyse_and_step",
     )(
-        scal,
-        gathered,
-        other,
-        flat,
-        core_edge.reshape(members * LONS, LATS),
-        y_edge.reshape(members * LONS, LATS),
-        west,
-        east,
-        mask,
-        zonal_current.reshape(ROWS, LATS),
+        ocean_mask, zonal_current.reshape(ROWS, LATS), flat, core_edge, y_edge, inner, outer, *gathered, *other
     )
     return out.reshape(state.shape)
 

time: 48.7 us -> 41.2 us (0.85)
  other arithmetic: 4.01 us -> 0.82 us
  local copies, waits for them, and re-layouts: 4.18 us -> 2.03 us
  waiting for transfers between devices: 12.1 us -> 10.7 us
  starting transfers between devices: 17.2 us -> 16.6 us
    ppermute x8 -> x10, waiting for transfers between devices: 8.98 us -> 6.79 us  [swapped(): lax.ppermute(x, axis, [(i, i ^ bit) for i in range(lax.axis_size(axis))])]
    convert_element_type x2 -> x0, other arithmetic: 2.02 us -> none  [the longest x1 1.28 us: local(): mask = ocean_mask.astype(F32)]
    another operation x2 -> x1, other arithmetic: 1.95 us -> 0.01 us  [local(): pair = jnp.stack([mine, inner[:height]])]
    slice x2 -> x0, local copies, waits for them, and re-layouts: 1.45 us -> none  [the longest x1 1.35 us: local(): scal = jnp.stack([col, gz, obs_count[0, 0], obs_count[1, 0]])]
    squeeze x2 -> x0, local copies, waits for them, and re-layouts: 0.91 us -> none  [the longest x1 0.86 us: local(): given = lax.dynamic_index_in_dim(payload, 1 - core, 0, False)]
    ppermute x3 -> x2, waiting for transfers between devices: 3.1 us -> 3.9 us  [the longest x1 3.9 us: local(): outer = lax.ppermute(outer, 'col', ring + [(j, i) for i, j in ring])]
    add x1 -> x2, other arithmetic: 0.01 us -> 0.8 us  [the longest x1 0.79 us: local(): mine = kept + core_edge[:height]]
    unnamed x13 -> x14, local copies, waits for them, and re-layouts: 1.26 us -> 2.02 us
  transfers between devices with their start and end apart: 11 -> 12, of which waited for: 6 -> 8; matrix products, arithmetic and copies ran while one was open for 0% -> 0% of each run, Pallas kernels for 0% -> 0%
where the time goes in v1:
time: 41.2 us; the launch traced here: 41 us
  starting transfers between devices  16.6 us (40%)
  Pallas kernels  10.8 us (26%)
  waiting for transfers between devices  10.7 us (26%)
  local copies, waits for them, and re-layouts  2.03 us (5%)
  other arithmetic  0.82 us (2%)
    ppermute x10, starting transfers between devices, swapped(): lax.ppermute(x, axis, [(i, i ^ bit) for i in range(lax.axis_size(axis))])  11.2 us
    pallas_call x1, Pallas kernels, local(): pl.pallas_call(functools.partial(step_kernel, members, parts, columns, ar...  8.04 us
    ppermute x10, waiting for transfers between devices, swapped(): lax.ppermute(x, axis, [(i, i ^ bit) for i in range(lax.axis_size(axis))])  6.79 us
    ppermute x1, starting transfers between devices, local(): outer = lax.ppermute(outer, 'col', ring + [(j, i) for i, j in ring])  4.67 us
    ppermute x1, waiting for transfers between devices, local(): outer = lax.ppermute(outer, 'col', ring + [(j, i) for i, j in ring])  3.9 us
    pallas_call x1, Pallas kernels, local(): pl.pallas_call(functools.partial(pick_kernel, members, columns), out_shap...  2.78 us
    unnamed x14, local copies, waits for them, and re-layouts  2.02 us
  transfers between devices with their start and end apart: 12, of which 8 were waited for; matrix products, arithmetic and copies ran while one was open for 0% of the time, Pallas kernels for 0%

profile of v1, /device:TPU:0, one launch (start us, length us, event | category | flops | bytes accessed | tf_op | source)
XLA Modules:
  0.0 41.0 jit_solution(5967445938816600878)
XLA Ops:
  0.0 0.0 copy-start.4
  0.0 1.3 %copy.9.count = s32[2,1]{1,0:T(2,128)} copy(s32[2,1]{0,1:T(1,128)} %param.10) | data formatting | bytes 16 | tf_op args[2]
  1.3 0.0 copy-done.4
  1.3 0.7 %copy.10.linked = s32[2,8,1]{2,1,0:T(8,128)} copy(s32[2,8,1]{1,2,0:T(1,128)S(1)} %copy-done.4) | data formatting | bytes 128 | tf_op args[5]
  2.0 0.0 copy-start
  2.0 2.8 %pick_priors.1 = (f32[88,128]{1,0:T(8,128)}, f32[728,128]{1,0:T(8,128)}, f32[640,128]{1,0:T(8,128)}, f32[168,128]{1,0:T(8,128)}, f32[168,128]{1,0:T(8,128)}) custom-call(s32[2,1]{1,0:T(2,128)} %copy.9.count, s32[2,8,1]{2,1,0:T(8,128)} %copy.10.linked, s32[2,1024]{1,0:T(2,128)} %site.1, f32[2,128]{1,0:T(2,128)} %value.1, f32[2,128]{1,0:T(2,128)} %noise.1, ...), custom_call_target="tpu_custom_call" | custom-call | tf_op jit(solution)/shard_map/pick_priors/pallas_call | solution.py:394
  4.8 0.5 %collective-permute-start = (f32[728,128]{1,0:T(8,128)}, f32[728,128]{1,0:T(8,128)S(1)}, u32[]{:S(2)}, u32[]{:S(2)}) collective-permute-start(f32[728,128]{1,0:T(8,128)} %get-tuple-element.10), channel_id=1, source_target_pairs={{0,1},{1,0},{2,3},{3,2},{4,5},{5,4},{6,7},{7,6},{8,9},{9,8},{10,11... | collective-permute-start | bytes 1118216 | tf_op jit(solution)/shard_map/ppermute | solution.py:372
  5.2 1.5 %collective-permute-done.core_edge = f32[728,128]{1,0:T(8,128)S(1)} collective-permute-done((f32[728,128]{1,0:T(8,128)}, f32[728,128]{1,0:T(8,128)S(1)}, u32[]{:S(2)}, u32[]{:S(2)}) %collective-permute-start) | collective-permute-done | bytes 372768 | tf_op jit(solution)/shard_map/ppermute | solution.py:372
  6.8 0.8 %slice_add_fusion = f32[88,128]{1,0:T(8,128)S(1)} fusion(f32[88,128]{1,0:T(8,128)} %get-tuple-element.12, f32[728,128]{1,0:T(8,128)S(1)} %collective-permute-done.core_edge), kind=kLoop, calls=%fused_computation.3 | loop fusion | flops 11264 | bytes 135168 | tf_op jit(solution)/shard_map/add | solution.py:403
  7.6 0.0 copy-start.3
  7.6 2.9 %collective-permute-start.2 = (f32[88,128]{1,0:T(8,128)S(1)}, f32[88,128]{1,0:T(8,128)S(1)}, u32[]{:S(2)}, u32[]{:S(2)}) collective-permute-start(f32[88,128]{1,0:T(8,128)S(1)} %slice_add_fusion), channel_id=1, source_target_pairs={{0,2},{1,3},{2,0},{3,1},{4,6},{5,7},{6,4},{7,5},{8,10},{9,11},{10,... | collective-permute-start | bytes 135176 | tf_op jit(solution)/shard_map/ppermute | solution.py:372
  10.5 2.0 %collective-permute-done.2 = f32[88,128]{1,0:T(8,128)S(1)} collective-permute-done((f32[88,128]{1,0:T(8,128)S(1)}, f32[88,128]{1,0:T(8,128)S(1)}, u32[]{:S(2)}, u32[]{:S(2)}) %collective-permute-start.2) | collective-permute-done | bytes 45088 | tf_op jit(solution)/shard_map/ppermute | solution.py:372
  12.5 0.0 copy-done.3
  12.5 2.1 %collective-permute-start.3 = (f32[256,128]{1,0:T(8,128)S(1)}, f32[256,128]{1,0:T(8,128)S(1)}, u32[]{:S(2)}, u32[]{:S(2)}) collective-permute-start(f32[256,128]{1,0:T(8,128)S(1)} %pad_maximum_fusion), channel_id=1, source_target_pairs={{0,4},{4,0},{8,12},{12,8},{16,20},{20,16},{24,28},{28,24},{1,5},{5... | collective-permute-start | bytes 393224 | tf_op jit(solution)/shard_map/ppermute | solution.py:372
  14.6 0.7 %collective-permute-start.1 = (f32[640,128]{1,0:T(8,128)}, f32[640,128]{1,0:T(8,128)S(1)}, u32[]{:S(2)}, u32[]{:S(2)}) collective-permute-start(f32[640,128]{1,0:T(8,128)} %get-tuple-element.11), channel_id=1, source_target_pairs={{1,2},{2,1},{5,6},{6,5},{9,10},{10,9},{13,14},{14,13},{17,18},{18,... | collective-permute-start | bytes 983048 | tf_op jit(solution)/shard_map/ppermute | solution.py:405
  15.2 2.3 %collective-permute-done.3.inner = f32[256,128]{1,0:T(8,128)S(1)} collective-permute-done((f32[256,128]{1,0:T(8,128)S(1)}, f32[256,128]{1,0:T(8,128)S(1)}, u32[]{:S(2)}, u32[]{:S(2)}) %collective-permute-start.3) | collective-permute-done | bytes 131104 | tf_op jit(solution)/shard_map/ppermute | solution.py:372
  17.6 0.0 copy-start.5
  17.6 0.0 copy-start.1
  17.6 0.0 copy-start.2
  17.6 4.2 %collective-permute-start.7 = (f32[2,88,128]{2,1,0:T(8,128)S(1)}, f32[2,88,128]{2,1,0:T(8,128)S(1)}, u32[]{:S(2)}, u32[]{:S(2)}) collective-permute-start(f32[2,88,128]{2,1,0:T(8,128)S(1)} %pad_maximum_fusion.1.rest_0_), channel_id=1, source_target_pairs={{0,24},{4,28},{8,16},{12,20},{16,8},{20,12},{24,0},{28,4},{1,25},{... | collective-permute-start | bytes 270344 | tf_op jit(solution)/shard_map/ppermute | solution.py:372
  21.8 0.0 collective-permute-start.6
  21.8 0.6 %collective-permute-start.5 = (f32[2,88,128]{2,1,0:T(8,128)S(1)}, f32[2,88,128]{2,1,0:T(8,128)S(1)}, u32[]{:S(2)}, u32[]{:S(2)}) collective-permute-start(f32[2,88,128]{2,1,0:T(8,128)S(1)} %pad_maximum_fusion.1.rest_0_), channel_id=1, source_target_pairs={{0,8},{4,12},{8,0},{12,4},{16,24},{20,28},{24,16},{28,20},{1,9},{5... | collective-permute-start | bytes 270344 | tf_op jit(solution)/shard_map/ppermute | solution.py:372
  22.4 0.0 copy-done.5
  22.4 4.7 %collective-permute-start.4 = (f32[168,128]{1,0:T(8,128)S(1)}, f32[168,128]{1,0:T(8,128)S(1)}, u32[]{:S(2)}, u32[]{:S(2)}) collective-permute-start(f32[168,128]{1,0:T(8,128)S(1)} %copy-done.5), channel_id=1, source_target_pairs={{4,8},{12,16},{20,24},{28,0},{8,4},{16,12},{24,20},{0,28},{5,9},{1... | collective-permute-start | bytes 258056 | tf_op jit(solution)/shard_map/ppermute | solution.py:407
  27.1 3.9 %collective-permute-done.4.outer = f32[168,128]{1,0:T(8,128)S(1)} collective-permute-done((f32[168,128]{1,0:T(8,128)S(1)}, f32[168,128]{1,0:T(8,128)S(1)}, u32[]{:S(2)}, u32[]{:S(2)}) %collective-permute-start.4) | collective-permute-done | bytes 86048 | tf_op jit(solution)/shard_map/ppermute | solution.py:407
  31.0 0.0 collective-permute-start.8
  31.0 0.0 collective-permute-done.7.rest_3_
  31.0 0.5 %collective-permute-start.11 = (f32[2,88,128]{2,1,0:T(8,128)S(1)}, f32[2,88,128]{2,1,0:T(8,128)S(1)}, u32[]{:S(2)}, u32[]{:S(2)}) collective-permute-start(f32[2,88,128]{2,1,0:T(8,128)S(1)} %collective-permute-done.7.rest_3_), channel_id=1, source_target_pairs={{0,1},{1,0},{2,3},{3,2},{4,5},{5,4},{6,7},{7,6},{8,9},{9,8},{10,11... | collective-permute-start | bytes 270344 | tf_op jit(solution)/shard_map/ppermute | solution.py:372
  31.5 0.0 collective-permute-done.6.rest_2_
  31.5 0.1 collective-permute-start.10
  31.6 0.0 collective-permute-done.5.rest_1_
  31.6 0.4 %collective-permute-start.9 = (f32[2,88,128]{2,1,0:T(8,128)S(1)}, f32[2,88,128]{2,1,0:T(8,128)S(1)}, u32[]{:S(2)}, u32[]{:S(2)}) collective-permute-start(f32[2,88,128]{2,1,0:T(8,128)S(1)} %collective-permute-done.5.rest_1_), channel_id=1, source_target_pairs={{0,1},{1,0},{2,3},{3,2},{4,5},{5,4},{6,7},{7,6},{8,9},{9,8},{10,11... | collective-permute-start | bytes 270344 | tf_op jit(solution)/shard_map/ppermute | solution.py:372
  32.0 0.0 collective-permute-done.1.y_edge
  32.0 0.3 collective-permute-done.8.rest_4_
  32.3 0.2 collective-permute-done.11.rest_7_
  32.4 0.4 collective-permute-done.10.rest_6_
  32.8 0.2 collective-permute-done.9.rest_5_
  32.9 0.0 copy-done
  32.9 0.0 copy-done.1
  32.9 0.0 copy-done.2
  33.0 8.0 %analyse_and_step.1 = f32[1280,128]{1,0:T(8,128)} custom-call(s32[8,128]{1,0:T(8,128)S(1)} %copy-done.1, f32[16,128]{1,0:T(8,128)S(1)} %bitcast.8, f32[1280,128]{1,0:T(8,128)S(1)} %bitcast.7, f32[728,128]{1,0:T(8,128)S(1)} %collective-permute-done.core_edge, f32[640,128]{1,0:T(8,128)S(1)} %collective-permute-done.1.y_edge, ...), custom_call_target="tpu_custom_call" | custom-call | tf_op jit(solution)/shard_map/analyse_and_step/pallas_call | solution.py:427
  (4 shorter events, 0.0 us)
Async XLA Ops:
  0.0 1.3 %copy-start.4 = (s32[2,8,1]{1,2,0:T(1,128)S(1)}, s32[2,8,1]{1,2,0:T(1,128)}, u32[]{:S(2)}) copy-start(s32[2,8,1]{1,2,0:T(1,128)} %param.13) | copy-start | bytes 196
  2.0 30.9 %copy-start = (f32[80,2,8,128]{3,2,1,0:T(8,128)S(1)}, f32[80,2,8,128]{3,2,1,0:T(8,128)}, u32[]{:S(2)}) copy-start(f32[80,2,8,128]{3,2,1,0:T(8,128)} %param.8) | copy-start | bytes 1966084
  4.8 2.0 %collective-permute-start = (f32[728,128]{1,0:T(8,128)}, f32[728,128]{1,0:T(8,128)S(1)}, u32[]{:S(2)}, u32[]{:S(2)}) collective-permute-start(f32[728,128]{1,0:T(8,128)} %get-tuple-element.10), channel_id=1, source_target_pairs={{0,1},{1,0},{2,3},{3,2},{4,5},{5,4},{6,7},{7,6},{8,9},{9,8},{10,11... | collective-permute-start | bytes 1118216 | tf_op jit(solution)/shard_map/ppermute | solution.py:372
  7.6 4.9 %copy-start.3 = (f32[168,128]{1,0:T(8,128)S(1)}, f32[168,128]{1,0:T(8,128)}, u32[]{:S(2)}) copy-start(f32[168,128]{1,0:T(8,128)} %get-tuple-element.13) | copy-start | bytes 258052
  7.6 4.9 %collective-permute-start.2 = (f32[88,128]{1,0:T(8,128)S(1)}, f32[88,128]{1,0:T(8,128)S(1)}, u32[]{:S(2)}, u32[]{:S(2)}) collective-permute-start(f32[88,128]{1,0:T(8,128)S(1)} %slice_add_fusion), channel_id=1, source_target_pairs={{0,2},{1,3},{2,0},{3,1},{4,6},{5,7},{6,4},{7,5},{8,10},{9,11},{10,... | collective-permute-start | bytes 135176 | tf_op jit(solution)/shard_map/ppermute | solution.py:372
  12.5 5.0 %collective-permute-start.3 = (f32[256,128]{1,0:T(8,128)S(1)}, f32[256,128]{1,0:T(8,128)S(1)}, u32[]{:S(2)}, u32[]{:S(2)}) collective-permute-start(f32[256,128]{1,0:T(8,128)S(1)} %pad_maximum_fusion), channel_id=1, source_target_pairs={{0,4},{4,0},{8,12},{12,8},{16,20},{20,16},{24,28},{28,24},{1,5},{5... | collective-permute-start | bytes 393224 | tf_op jit(solution)/shard_map/ppermute | solution.py:372
  14.6 17.4 %collective-permute-start.1 = (f32[640,128]{1,0:T(8,128)}, f32[640,128]{1,0:T(8,128)S(1)}, u32[]{:S(2)}, u32[]{:S(2)}) collective-permute-start(f32[640,128]{1,0:T(8,128)} %get-tuple-element.11), channel_id=1, source_target_pairs={{1,2},{2,1},{5,6},{6,5},{9,10},{10,9},{13,14},{14,13},{17,18},{18,... | collective-permute-start | bytes 983048 | tf_op jit(solution)/shard_map/ppermute | solution.py:405
  17.6 4.9 %copy-start.5 = (f32[168,128]{1,0:T(8,128)S(1)}, f32[168,128]{1,0:T(8,128)}, u32[]{:S(2)}) copy-start(f32[168,128]{1,0:T(8,128)} %get-tuple-element.14) | copy-start | bytes 258052
  17.6 15.4 %copy-start.1 = (s32[8,128]{1,0:T(8,128)S(1)}, s32[8,128]{1,0:T(8,128)}, u32[]{:S(2)}) copy-start(s32[8,128]{1,0:T(8,128)} %mask.3) | copy-start | bytes 12292
  17.6 15.4 %copy-start.2 = (f32[2,8,128]{2,1,0:T(8,128)S(1)}, f32[2,8,128]{2,1,0:T(8,128)}, u32[]{:S(2)}) copy-start(f32[2,8,128]{2,1,0:T(8,128)} %param.15) | copy-start | bytes 24580
  17.6 13.4 %collective-permute-start.7 = (f32[2,88,128]{2,1,0:T(8,128)S(1)}, f32[2,88,128]{2,1,0:T(8,128)S(1)}, u32[]{:S(2)}, u32[]{:S(2)}) collective-permute-start(f32[2,88,128]{2,1,0:T(8,128)S(1)} %pad_maximum_fusion.1.rest_0_), channel_id=1, source_target_pairs={{0,24},{4,28},{8,16},{12,20},{16,8},{20,12},{24,0},{28,4},{1,25},{... | collective-permute-start | bytes 270344 | tf_op jit(solution)/shard_map/ppermute | solution.py:372
  21.8 9.7 %collective-permute-start.6 = (f32[2,88,128]{2,1,0:T(8,128)S(1)}, f32[2,88,128]{2,1,0:T(8,128)S(1)}, u32[]{:S(2)}, u32[]{:S(2)}) collective-permute-start(f32[2,88,128]{2,1,0:T(8,128)S(1)} %pad_maximum_fusion.1.rest_0_), channel_id=1, source_target_pairs={{0,16},{4,20},{8,24},{12,28},{16,0},{20,4},{24,8},{28,12},{1,17},{... | collective-permute-start | bytes 270344 | tf_op jit(solution)/shard_map/ppermute | solution.py:372
  21.8 9.8 %collective-permute-start.5 = (f32[2,88,128]{2,1,0:T(8,128)S(1)}, f32[2,88,128]{2,1,0:T(8,128)S(1)}, u32[]{:S(2)}, u32[]{:S(2)}) collective-permute-start(f32[2,88,128]{2,1,0:T(8,128)S(1)} %pad_maximum_fusion.1.rest_0_), channel_id=1, source_target_pairs={{0,8},{4,12},{8,0},{12,4},{16,24},{20,28},{24,16},{28,20},{1,9},{5... | collective-permute-start | bytes 270344 | tf_op jit(solution)/shard_map/ppermute | solution.py:372
  22.4 8.6 %collective-permute-start.4 = (f32[168,128]{1,0:T(8,128)S(1)}, f32[168,128]{1,0:T(8,128)S(1)}, u32[]{:S(2)}, u32[]{:S(2)}) collective-permute-start(f32[168,128]{1,0:T(8,128)S(1)} %copy-done.5), channel_id=1, source_target_pairs={{4,8},{12,16},{20,24},{28,0},{8,4},{16,12},{24,20},{0,28},{5,9},{1... | collective-permute-start | bytes 258056 | tf_op jit(solution)/shard_map/ppermute | solution.py:407
  31.0 1.3 %collective-permute-start.8 = (f32[2,88,128]{2,1,0:T(8,128)S(1)}, f32[2,88,128]{2,1,0:T(8,128)S(1)}, u32[]{:S(2)}, u32[]{:S(2)}) collective-permute-start(f32[2,88,128]{2,1,0:T(8,128)S(1)} %pad_maximum_fusion.1.rest_0_), channel_id=1, source_target_pairs={{0,1},{1,0},{2,3},{3,2},{4,5},{5,4},{6,7},{7,6},{8,9},{9,8},{10,11... | collective-permute-start | bytes 270344 | tf_op jit(solution)/shard_map/ppermute | solution.py:372
  31.0 1.4 %collective-permute-start.11 = (f32[2,88,128]{2,1,0:T(8,128)S(1)}, f32[2,88,128]{2,1,0:T(8,128)S(1)}, u32[]{:S(2)}, u32[]{:S(2)}) collective-permute-start(f32[2,88,128]{2,1,0:T(8,128)S(1)} %collective-permute-done.7.rest_3_), channel_id=1, source_target_pairs={{0,1},{1,0},{2,3},{3,2},{4,5},{5,4},{6,7},{7,6},{8,9},{9,8},{10,11... | collective-permute-start | bytes 270344 | tf_op jit(solution)/shard_map/ppermute | solution.py:372
  31.5 1.3 %collective-permute-start.10 = (f32[2,88,128]{2,1,0:T(8,128)S(1)}, f32[2,88,128]{2,1,0:T(8,128)S(1)}, u32[]{:S(2)}, u32[]{:S(2)}) collective-permute-start(f32[2,88,128]{2,1,0:T(8,128)S(1)} %collective-permute-done.6.rest_2_), channel_id=1, source_target_pairs={{0,1},{1,0},{2,3},{3,2},{4,5},{5,4},{6,7},{7,6},{8,9},{9,8},{10,11... | collective-permute-start | bytes 270344 | tf_op jit(solution)/shard_map/ppermute | solution.py:372
  31.6 1.4 %collective-permute-start.9 = (f32[2,88,128]{2,1,0:T(8,128)S(1)}, f32[2,88,128]{2,1,0:T(8,128)S(1)}, u32[]{:S(2)}, u32[]{:S(2)}) collective-permute-start(f32[2,88,128]{2,1,0:T(8,128)S(1)} %collective-permute-done.5.rest_1_), channel_id=1, source_target_pairs={{0,1},{1,0},{2,3},{3,2},{4,5},{5,4},{6,7},{7,6},{8,9},{9,8},{10,11... | collective-permute-start | bytes 270344 | tf_op jit(solution)/shard_map/ppermute | solution.py:372

commit v2 on v1

v2 whole, which is shorter than its diff:
```python
import functools

import jax
import jax.numpy as jnp
from jax import lax
from jax.experimental import pallas as pl
from jax.experimental.pallas import tpu as pltpu
from jax.sharding import PartitionSpec as P

LEVS = 2
LONS = 8
LATS = 128
BATCHES = 2
REACH = 3
CAP = 128
MEAN_COUNT = 32
WINDOW = 2 * REACH + 1
CHUNK = 256

CELLS = LEVS * LONS * LATS
ROWS = LEVS * LONS
CORE_ROW = 16
INNER_ROW = 24
Y_ROW = 26
OUTER_ROW = 34
EXT_ROWS = 36

LATERAL_MIX = 0.2
VERTICAL_MIX = 0.15

F32 = jnp.float32
BF16 = jnp.bfloat16


def iota(shape, dim):
    return lax.broadcasted_iota(jnp.int32, shape, dim)


def halves(x):
    high = x.astype(BF16)
    return high, (x - high.astype(F32)).astype(BF16)


def dot(a, b):
    return lax.dot_general(a, b, (((1,), (0,)), ((), ())), preferred_element_type=F32)


def dot_lanes(a, b):
    return lax.dot_general(a, b, (((1,), (1,)), ((), ())), preferred_element_type=F32)


def for_each(count, body):
    if count == 1:
        body(0)
    else:
        lax.fori_loop(0, count, lambda i, unused: (body(i), unused)[1], 0)


def rows_of(members):
    names = ("mask", "value", "noise", "links", "site", "occupied", "owner", "count")
    return {name: members + i for i, name in enumerate(names)}


def position():
    return lax.axis_index("col").astype(jnp.int32), lax.axis_index("gz").astype(jnp.int32)


def pick_kernel(members, columns, count, linked, site, value, noise, mask, state, kept, core_send, y_send, inner, outer):
    col, gz = position()
    core = gz % 2
    lane = iota((1, CAP), 1)
    at = pl.multiple_of(col * CAP, CAP)
    index, filled = [], []
    for b in range(BATCHES):
        occupied = lane < count[0, b]
        filled.append(occupied)
        index.append(jnp.where(occupied, site[b : b + 1, pl.ds(at, CAP)] - gz * CELLS, -1))
    wanted = jnp.concatenate(index, 1)
    total = jnp.zeros((3 * members + 16, BATCHES * CAP), F32)
    cell = iota((2 * LATS, BATCHES * CAP), 0)
    ocean = mask[...].astype(F32)
    for pair in range(ROWS // 2):
        left = []
        for r in (2 * pair, 2 * pair + 1):
            x = state[pl.ds(r, members, stride=ROWS), :]
            high = x.astype(BF16)
            rest = x - high.astype(F32)
            middle = rest.astype(BF16)
            low = (rest - middle.astype(F32)).astype(BF16)
            lon = r % LONS
            row = jnp.broadcast_to(ocean[lon : lon + 1, :], (16, LATS)).astype(BF16)
            left.append(jnp.concatenate([high, row, middle, low], 0))
        hit = jnp.where(cell + pair * 2 * LATS == wanted, 1.0, 0.0).astype(BF16)
        total = total + dot(jnp.concatenate(left, 1), hit)
    m = members
    height = m + 8
    picked = (total[:m] + total[m + 16 : 2 * m + 16]) + total[2 * m + 16 :]
    first = jnp.where(gz == 0, 1.0, 0.0)
    for b in range(BATCHES):
        here = slice(b * CAP, (b + 1) * CAP)
        once = jnp.where(filled[b], first, 0.0)
        links = jnp.concatenate([linked[b].astype(F32), jnp.zeros((1, CAP - columns), F32)], 1)
        tail = [
            total[m : m + 1, here],
            value[b : b + 1, :] * once,
            noise[b : b + 1, :] * once,
            links * first,
            site[b : b + 1, pl.ds(at, CAP)].astype(F32) * once,
            once,
            once * col.astype(F32),
            jnp.full((1, CAP), count[0, b].astype(F32) * first),
        ]
        block = jnp.concatenate([picked[:, here]] + tail, 0)

        @pl.when(core == b)
        def _():
            kept[...] = block

        @pl.when(core != b)
        def _():
            core_send[:height, :] = block

    for member in range(members):
        up = state[pl.ds(pl.multiple_of(member * ROWS + (1 - core) * LONS, LONS), LONS), :]
        core_send[height + member * LONS : height + (member + 1) * LONS, :] = up
        down = state[pl.ds(pl.multiple_of(member * ROWS + core * LONS, LONS), LONS), :]
        y_send[member * LONS : (member + 1) * LONS, :] = down
    even = col % 2 == 0
    for lev in range(LEVS):
        west = state[pl.ds(lev * LONS, members, stride=ROWS), :]
        east = state[pl.ds(lev * LONS + LONS - 1, members, stride=ROWS), :]
        inner[lev * members : (lev + 1) * members, :] = jnp.where(even, east, west)
        outer[lev * members : (lev + 1) * members, :] = jnp.where(even, west, east)
    west = jnp.broadcast_to(ocean[:1], (8, LATS))
    east = jnp.broadcast_to(ocean[LONS - 1 :], (8, LATS))
    inner[LEVS * members :, :] = jnp.where(even, east, west)
    outer[LEVS * members :, :] = jnp.where(even, west, east)


def place_terms(col, gz, columns):
    lon_all = columns * LONS
    odd = gz % 2
    even_col = col % 2 == 0
    lane = iota((1, LATS), 1)
    above, below = LEVS * gz + LEVS, LEVS * gz - 1
    own = lane < ROWS
    near = (lane >= CORE_ROW) & (lane < INNER_ROW)
    far = (lane >= Y_ROW) & (lane < OUTER_ROW)
    row_lev = LEVS * gz + jnp.where(own, lane // LONS, lane % LEVS)
    row_lev = jnp.where(near, jnp.where(odd == 0, above, below), row_lev)
    row_lev = jnp.where(far, jnp.where(odd == 0, below, above), row_lev)
    west_lon = (col * LONS + lon_all - 1) % lon_all
    east_lon = (col * LONS + LONS) % lon_all
    inner = (lane >= INNER_ROW) & (lane < Y_ROW)
    row_lon = col * LONS + jnp.where(far, lane - Y_ROW, lane % LONS)
    row_lon = jnp.where(inner, jnp.where(even_col, east_lon, west_lon), row_lon)
    row_lon = jnp.where(lane >= OUTER_ROW, jnp.where(even_col, west_lon, east_lon), row_lon)
    west_col = (col + columns - 1) % columns
    east_col = (col + 1) % columns
    inner_col = jnp.where(even_col, east_col, west_col)
    outer_col = jnp.where(even_col, west_col, east_col)
    return row_lev.astype(F32), row_lon.astype(F32), inner, inner_col, outer_col


def centred_parts(x):
    x = x - jnp.sum(x, 0, keepdims=True) * (1.0 / x.shape[0])
    high, low = halves(x)
    return jnp.concatenate([high, low, high, jnp.zeros((16, x.shape[1]), BF16)], 0)


def increment(x, sides, gains, local):
    members = x.shape[0]
    weighted = dot(sides, centred_parts(x)) * local
    high, low = halves(weighted)
    first = dot(gains, high)
    return (first[:members] + first[members:]) + dot(gains[:members], low)


def move_rows(fields, gained, first, last, ocean, terms, b, chunks):
    sides, gains, row_part, lat_part = terms

    def chunk(k):
        t = b * chunks + k
        for r in range(first, last, 2):
            at = r - first
            x = jnp.concatenate([fields[at], fields[at + 1]], 1)
            tapers = [lat_part[t] * row_part[t, :, r + h : r + h + 1] for h in range(2)]
            moved = increment(x, sides[t], gains[t], jnp.concatenate(tapers, 1))
            moved = moved * jnp.concatenate([ocean[at], ocean[at + 1]], 1)
            for h in range(2):
                piece = slice(h * LATS, (h + 1) * LATS)
                if chunks == 1:
                    fields[at + h] = x[:, piece] + moved[:, piece]
                else:
                    gained[at + h] = gained[at + h] + moved[:, piece]

    if chunks > 1:
        gained[...] = jnp.zeros_like(gained)
    for_each(chunks, chunk)
    if chunks > 1:
        for at in range(last - first):
            fields[at] = fields[at] + gained[at]


def near_kernel(members, parts, columns, around, chunks, mask, state, core_edge, inner, *rest):
    mine_parts, other_parts = rest[: len(parts)], rest[len(parts) : 2 * len(parts)]
    fields, sides, gains, row_terms, lat_terms, packed, gained = rest[2 * len(parts) :]
    mine = [part.at[i] for part, size in zip(mine_parts, parts) for i in range(size)]
    other = [part.at[i] for part, size in zip(other_parts, parts) for i in range(size)]
    blocks = len(mine)
    col, gz = position()
    core = gz % 2
    lon_all = columns * LONS
    place = rows_of(members)
    denominator = 1.0 / (members - 1)
    height = members + 8
    owners = [col ^ j if around is None else (col + around[j] + columns) % columns for j in range(blocks)]

    links = []
    packed[...] = jnp.zeros_like(packed)
    for b in range(BATCHES):
        start = 0
        own_links = []
        for j in range(blocks):
            block = jnp.where(core == b, mine[j][...], other[j][...])
            own_links.append(block[place["links"] : place["links"] + 1, :])
            tall = jnp.concatenate([block, jnp.zeros((LATS - height, CAP), F32)], 0)
            packed[b, pl.ds(start, CAP), :] = tall.T
            start = start + block[place["count"], 0].astype(jnp.int32)
        links.append(own_links)

    inner_start = inner.shape[0] - (members * LEVS + 8)
    for r in range(ROWS):
        fields[r] = state[pl.ds(r, members, stride=ROWS), :]
    for lon in range(LONS):
        fields[CORE_ROW + lon] = core_edge[pl.ds(height + lon, members, stride=LONS), :]
    for lev in range(LEVS):
        at = inner_start + lev * members
        fields[INNER_ROW + lev] = inner[at : at + members, :]
    wet = mask[...].astype(F32)
    ocean = [wet[lon : lon + 1] for lon in range(LONS)] * 3
    at = inner_start + members * LEVS
    ocean += [inner[at : at + 1, :]] * LEVS

    lane = iota((1, LATS), 1)
    row_lev, row_lon, inside, inner_col, outer_col = place_terms(col, gz, columns)

    def links_of(b, target):
        row = jnp.zeros((1, CAP), F32)
        for j in range(blocks):
            row = row + jnp.where(owners[j] == target, links[b][j], 0.0)
        return row

    def places(site, owner):
        site = site.astype(jnp.int32)
        lev = site // (LONS * LATS)
        lon = owner.astype(jnp.int32) * LONS + site // LATS % LONS
        return lev.astype(F32), lon.astype(F32), (site % LATS).astype(F32)

    def lon_square(a, b):
        gap = jnp.abs(a - b)
        gap = jnp.minimum(gap, lon_all - gap) * (1.0 / (2.0 * LONS))
        return 1.0 + gap * gap

    def lev_square(a, b):
        gap = (a - b) * 0.5
        return 1.0 + gap * gap

    def lat_square(a, b):
        gap = (a - b) * (1.0 / (LATS // 8))
        return 1.0 + gap * gap

    def slots_of(b, k):
        start = k * CHUNK if isinstance(k, int) else pl.multiple_of(k * CHUNK, CHUNK)
        tall = packed[b, pl.ds(start, CHUNK), :]
        return tall, tall.T

    def batch_terms(b, k):
        tall, wide = slots_of(b, k)
        occupied = wide[place["occupied"] : place["occupied"] + 1]
        if b == 0:
            prior = wide[:members]
        else:
            prior = jnp.concatenate([fields[Y_ROW + 2 * k], fields[Y_ROW + 2 * k + 1]], 1) * occupied
        value = wide[place["value"] : place["value"] + 1]
        noise = jnp.where(occupied > 0, wide[place["noise"] : place["noise"] + 1], 1.0)
        mean = jnp.sum(prior, 0, keepdims=True) / members
        anomaly = prior - mean
        spread = jnp.sum(anomaly * anomaly, 0, keepdims=True) * denominator
        total = spread + noise
        shrink = 1.0 / (1.0 + jnp.sqrt(noise / total))
        gain = ((value - mean) - shrink * anomaly) / total
        high = anomaly.astype(BF16).astype(F32)
        stack = jnp.concatenate([high, high, anomaly - high, jnp.zeros((16, CHUNK), F32)], 0)
        t = b * chunks + k
        sides[t] = stack.T.astype(BF16)
        gains[t] = jnp.concatenate(halves(gain), 0)

        def column(name):
            return tall[:, place[name] : place[name] + 1]

        lev, lon, lat = places(column("site"), column("owner"))
        holder = jnp.where(lane.astype(F32) == column("owner"), 1.0, 0.0)
        weight = [jnp.sum(holder * links_of(b, c), 1, keepdims=True) for c in (col, inner_col, outer_col)]
        weight = jnp.where(inside, weight[1], jnp.where(lane < OUTER_ROW, weight[0], weight[2]))
        row_terms[t] = weight * denominator / (lev_square(row_lev, lev) * lon_square(row_lon, lon))
        lat_terms[t] = 1.0 / lat_square(lane.astype(F32), lat)
        return lev, lon, lat, holder

    def site_weights(where0, k1):
        lev0, lon0, lat0, holder = where0
        tall, wide = slots_of(1, k1)
        owner = wide[place["owner"] : place["owner"] + 1]
        lev, lon, lat = places(wide[place["site"] : place["site"] + 1], owner)
        pad = (-blocks) % 16
        spare = [jnp.zeros((pad, CAP), F32)] if pad else []
        table = jnp.concatenate(links[0] + spare, 0).astype(BF16)
        by_block = dot_lanes(holder.astype(BF16), table).astype(BF16)
        spare = [jnp.zeros((pad, CHUNK), F32)] if pad else []
        there = [jnp.where(owner == owners[j].astype(F32), 1.0, 0.0) for j in range(blocks)]
        weight = dot(by_block, jnp.concatenate(there + spare, 0).astype(BF16))
        square = lat_square(lat0, lat) * lon_square(lon0, lon) * lev_square(lev0, lev)
        return weight * denominator / square, wide

    def first_terms(k):
        where = batch_terms(0, k)

        def site_chunk(k1):
            taper, wide = site_weights(where, k1)
            x = wide[:members]
            moved = increment(x, sides[k], gains[k], taper) * wide[members : members + 1]
            for h in range(2):
                at = Y_ROW + 2 * k1 + h
                piece = slice(h * LATS, (h + 1) * LATS)
                before = x[:, piece] if chunks == 1 else jnp.where(k == 0, x[:, piece], fields[at])
                fields[at] = before + moved[:, piece]

        for_each(chunks, site_chunk)

    terms = (sides, gains, row_terms, lat_terms)
    for_each(chunks, first_terms)
    for_each(chunks, lambda k: (batch_terms(1, k), None)[1])
    for b in range(BATCHES):
        move_rows(fields, gained, 0, Y_ROW, ocean, terms, b, chunks)


def far_kernel(
    members, columns, floors, chunks, mask, zonal, near, y_edge, outer, sides, gains, row_terms, lat_terms, out, fields, gained
):
    col, gz = position()
    core = gz % 2
    even_col = col % 2 == 0
    lane = iota((1, LATS), 1)
    outer_at = OUTER_ROW - Y_ROW
    beyond = gz + 2 * core - 1
    inside = jnp.where((beyond >= 0) & (beyond < floors), 1.0, 0.0)
    for lon in range(LONS):
        fields[lon] = y_edge[pl.ds(lon, members, stride=LONS), :] * inside
    for lev in range(LEVS):
        fields[outer_at + lev] = outer[lev * members : (lev + 1) * members, :]
    wet = mask[...].astype(F32)
    ocean = [wet[lon : lon + 1] for lon in range(LONS)]
    edge = members * LEVS
    terms = (sides, gains, row_terms, lat_terms)
    for b in range(BATCHES):
        move_rows(fields, gained, Y_ROW, EXT_ROWS, ocean + [outer[edge : edge + 1, :]] * LEVS, terms, b, chunks)

    for r in range(ROWS):
        lev, lon = r // LONS, r % LONS
        x = near[r]
        side = [near[INNER_ROW + lev], fields[outer_at + lev]]
        lon_next = near[r + 1] if lon < LONS - 1 else jnp.where(even_col, side[0], side[1])
        lon_prev = near[r - 1] if lon > 0 else jnp.where(even_col, side[1], side[0])
        lat_next = jnp.where(lane < LATS - 1, pltpu.roll(x, LATS - 1, 1), 0.0)
        lat_prev = jnp.where(lane > 0, pltpu.roll(x, 1, 1), 0.0)
        over = jnp.where(core == 1 - lev, near[CORE_ROW + lon], fields[lon])
        vertical = near[r ^ LONS] + over
        tendency = (
            -0.5 * zonal[r : r + 1, :] * (lon_next - lon_prev)
            + LATERAL_MIX * (lon_next + lon_prev + lat_next + lat_prev - 4.0 * x)
            + VERTICAL_MIX * (vertical - 2.0 * x)
        )
        out[pl.ds(r, members, stride=ROWS), :] = x + ocean[lon] * tendency


def room(mebibytes):
    return pltpu.CompilerParams(vmem_limit_bytes=mebibytes * 1024 * 1024)


def swapped(x, axis, bit):
    return lax.ppermute(x, axis, [(i, i ^ bit) for i in range(lax.axis_size(axis))])


def shifted(x, axis, by):
    count = lax.axis_size(axis)
    return lax.ppermute(x, axis, [(i, (i + by) % count) for i in range(count)])


def local(state, observation_site, obs_count, measured_values, observation_noise, loc_pattern, ocean_mask, zonal_current):
    members = state.shape[0]
    columns = lax.axis_size("col")
    floors = lax.axis_size("gz")
    vmem = pl.BlockSpec(memory_space=pltpu.VMEM)
    smem = pl.BlockSpec(memory_space=pltpu.SMEM)
    height = members + 8
    level = members * LONS
    edge = members * LEVS + 8
    flat = state.reshape(members * ROWS, LATS)

    def like(*lengths):
        return [pltpu.VMEM((length, LATS), F32) for length in lengths]

    kept, core_send, y_send, inner, outer = pl.pallas_call(
        functools.partial(pick_kernel, members, columns),
        out_shape=like(height, height + level, level, edge, edge),
        in_specs=[smem] + [vmem] * 6,
        out_specs=[vmem] * 5,
        name="pick_priors",
    )(
        obs_count.reshape(1, BATCHES),
        loc_pattern.reshape(BATCHES, 1, columns),
        observation_site,
        measured_values,
        observation_noise,
        ocean_mask,
        flat,
    )

    core_edge = swapped(core_send, "gz", 1)
    mine = kept + core_edge[:height]
    for bit in range(2, floors, 2):
        mine = mine + swapped(mine, "gz", bit)
    if columns <= 2 * WINDOW + 1 and columns & (columns - 1) == 0:
        around = None
        inner = swapped(jnp.concatenate([mine, inner]), "col", 1)
        pair = jnp.stack([mine, inner[:height]])
        gathered = [pair] + [swapped(pair, "col", bit) for bit in range(2, columns, 2)]
    else:
        inner = swapped(inner, "col", 1)
        around = tuple(range(-WINDOW, WINDOW + 1)) if columns > 2 * WINDOW + 1 else tuple(range(columns))
        gathered = [(mine if by == 0 else shifted(mine, "col", -by))[None] for by in around]

    ends = [(i, i + 1) for i in range(1, floors - 1, 2)]
    ends += [(j, i) for i, j in ends]
    ends += [(i, i) for i in range(floors) if i not in dict(ends)]
    y_edge = lax.ppermute(y_send, "gz", ends)
    ring = [(i, (i + 1) % columns) for i in range(1, columns, 2)]
    outer = lax.ppermute(outer, "col", ring + [(j, i) for i, j in ring])

    parts = tuple(part.shape[0] for part in gathered)
    other = [swapped(part, "gz", 1) for part in gathered]

    slots = min(sum(parts) * CAP, MEAN_COUNT * columns)
    chunks = -(-slots // CHUNK)
    rows = Y_ROW + 2 * chunks
    several = chunks > 1
    count = BATCHES * chunks
    limit = room(48 if several else 16)
    near, *terms = pl.pallas_call(
        functools.partial(near_kernel, members, parts, columns, around, chunks),
        out_shape=[
            pltpu.VMEM((rows, members, LATS), F32),
            pltpu.VMEM((count, CHUNK, CHUNK), BF16),
            pltpu.VMEM((count, 2 * members, CHUNK), BF16),
            pltpu.VMEM((count, CHUNK, LATS), F32),
            pltpu.VMEM((count, CHUNK, LATS), F32),
        ],
        in_specs=[vmem] * (4 + 2 * len(parts)),
        out_specs=[vmem] * 5,
        scratch_shapes=[
            pltpu.VMEM((BATCHES, chunks * CHUNK + CAP, CAP), F32),
            pltpu.VMEM((Y_ROW if several else 1, members, LATS), F32),
        ],
        compiler_params=limit,
        cost_estimate=pl.CostEstimate(flops=0, bytes_accessed=0, transcendentals=0),
        name="analyse_near",
    )(ocean_mask, flat, core_edge, inner, *gathered, *other)
    out = pl.pallas_call(
        functools.partial(far_kernel, members, columns, floors, chunks),
        out_shape=jax.ShapeDtypeStruct((members * ROWS, LATS), F32),
        in_specs=[vmem] * 9,
        out_specs=vmem,
        scratch_shapes=[
            pltpu.VMEM((EXT_ROWS - Y_ROW, members, LATS), F32),
            pltpu.VMEM((EXT_ROWS - Y_ROW if several else 1, members, LATS), F32),
        ],
        compiler_params=limit,
        name="analyse_far_and_step",
    )(ocean_mask, zonal_current.reshape(ROWS, LATS), near, y_edge, outer, *terms)
    return out.reshape(state.shape)


def solution(mesh):
    in_specs = (
        P(None, "gz", "col", None),
        P(),
        P(None, "col"),
        P(None, "col"),
        P(None, "col"),
        P(None, None, "col"),
        P("col", None),
        P("gz", "col", None),
    )
    out_specs = P(None, "gz", "col", None)
    return jax.shard_map(local, mesh=mesh, in_specs=in_specs, out_specs=out_specs, check_vma=False)
```

time: 41.2 us -> 37.7 us (0.915)
  starting transfers between devices: 16.6 us -> 14.1 us
  waiting for transfers between devices: 10.7 us -> 12.8 us
  local copies, waits for them, and re-layouts: 2.03 us -> 0.02 us
  other arithmetic: 0.82 us -> 0.03 us
    ppermute x10, waiting for transfers between devices: 6.79 us -> 12.8 us  [swapped(): lax.ppermute(x, axis, [(i, i ^ bit) for i in range(lax.axis_size(axis))])]
    ppermute x1, waiting for transfers between devices: 3.9 us -> 0.01 us  [local(): outer = lax.ppermute(outer, 'col', ring + [(j, i) for i, j in ring])]
    ppermute x1, starting transfers between devices: 4.67 us -> 2.57 us  [local(): outer = lax.ppermute(outer, 'col', ring + [(j, i) for i, j in ring])]
    unnamed x14 -> x6, local copies, waits for them, and re-layouts: 2.02 us -> 0.01 us
    pallas_call x1, Pallas kernels: 2.78 us -> 1.9 us  [local(): pl.pallas_call(functools.partial(pick_kernel, members, columns), out_shap...]
    add x1, other arithmetic: 0.79 us -> 0.01 us  [local(): mine = kept + core_edge[:height]]
    pallas_call x1 -> x2, Pallas kernels: 8.04 us -> 8.57 us  [the longest x1 5.81 us: local(): pl.pallas_call(functools.partial(near_kernel, members, parts, columns, ar...]
  transfers between devices with their start and end apart: 12 -> 12, of which waited for: 8 -> 5; matrix products, arithmetic and copies ran while one was open for 0% -> 0% of each run, Pallas kernels for 0% -> 15%
where the time goes in v2:
time: 37.7 us; the launch traced here: 37.5 us
  starting transfers between devices  14.1 us (37%)
  waiting for transfers between devices  12.8 us (34%)
  Pallas kernels  10.5 us (28%)
    ppermute x10, waiting for transfers between devices, swapped(): lax.ppermute(x, axis, [(i, i ^ bit) for i in range(lax.axis_size(axis))])  12.8 us
    ppermute x10, starting transfers between devices, swapped(): lax.ppermute(x, axis, [(i, i ^ bit) for i in range(lax.axis_size(axis))])  10.8 us
    pallas_call x1, Pallas kernels, local(): pl.pallas_call(functools.partial(near_kernel, members, parts, columns, ar...  5.81 us
    pallas_call x1, Pallas kernels, local(): pl.pallas_call(functools.partial(far_kernel, members, columns, floors, ch...  2.76 us
    ppermute x1, starting transfers between devices, local(): outer = lax.ppermute(outer, 'col', ring + [(j, i) for i, j in ring])  2.57 us
    pallas_call x1, Pallas kernels, local(): pl.pallas_call(functools.partial(pick_kernel, members, columns), out_shap...  1.9 us
  transfers between devices with their start and end apart: 12, of which 5 were waited for; matrix products, arithmetic and copies ran while one was open for 0% of the time, Pallas kernels for 15%

profile of v2, /device:TPU:0, one launch (start us, length us, event | category | flops | bytes accessed | tf_op | source)
XLA Modules:
  0.0 37.5 jit_solution(5907332950058370651)
XLA Ops:
  0.0 0.0 copy-start.1
  0.0 0.0 copy-start
  0.0 1.9 %pick_priors.1 = (f32[88,128]{1,0:T(8,128)S(1)}, f32[728,128]{1,0:T(8,128)S(1)}, f32[640,128]{1,0:T(8,128)S(1)}, f32[168,128]{1,0:T(8,128)S(1)}, f32[168,128]{1,0:T(8,128)S(1)}) custom-call(s32[1,2]{1,0:T(1,128)} %bitcast.15, s32[2,1,8]{2,1,0:T(1,128)} %bitcast.14, s32[2,1024]{1,0:T(2,128)} %site.1, f32[2,128]{1,0:T(2,128)} %value.1, f32[2,128]{1,0:T(2,128)} %noise.1, ...), custom_call_target="tpu_custom_call" | custom-call | tf_op jit(solution)/shard_map/pick_priors/pallas_call | solution.py:413
  1.9 0.5 %collective-permute-start = (f32[728,128]{1,0:T(8,128)S(1)}, f32[728,128]{1,0:T(8,128)S(1)}, u32[]{:S(2)}, u32[]{:S(2)}) collective-permute-start(f32[728,128]{1,0:T(8,128)S(1)} %get-tuple-element.15), channel_id=1, source_target_pairs={{0,1},{1,0},{2,3},{3,2},{4,5},{5,4},{6,7},{7,6},{8,9},{9,8},{10,11... | collective-permute-start | bytes 1118216 | tf_op jit(solution)/shard_map/ppermute | solution.py:391
  2.4 1.3 %collective-permute-done.core_edge = f32[728,128]{1,0:T(8,128)S(1)} collective-permute-done((f32[728,128]{1,0:T(8,128)S(1)}, f32[728,128]{1,0:T(8,128)S(1)}, u32[]{:S(2)}, u32[]{:S(2)}) %collective-permute-start) | collective-permute-done | bytes 372768 | tf_op jit(solution)/shard_map/ppermute | solution.py:391
  3.8 2.9 %collective-permute-start.1 = (f32[88,128]{1,0:T(8,128)S(1)}, f32[88,128]{1,0:T(8,128)S(1)}, u32[]{:S(2)}, u32[]{:S(2)}) collective-permute-start(f32[88,128]{1,0:T(8,128)S(1)} %slice_add_fusion), channel_id=1, source_target_pairs={{0,2},{1,3},{2,0},{3,1},{4,6},{5,7},{6,4},{7,5},{8,10},{9,11},{10,... | collective-permute-start | bytes 135176 | tf_op jit(solution)/shard_map/ppermute | solution.py:391
  6.7 2.0 %collective-permute-done.1 = f32[88,128]{1,0:T(8,128)S(1)} collective-permute-done((f32[88,128]{1,0:T(8,128)S(1)}, f32[88,128]{1,0:T(8,128)S(1)}, u32[]{:S(2)}, u32[]{:S(2)}) %collective-permute-start.1) | collective-permute-done | bytes 45088 | tf_op jit(solution)/shard_map/ppermute | solution.py:391
  8.8 0.0 copy-start.2
  8.8 2.1 %collective-permute-start.2 = (f32[256,128]{1,0:T(8,128)S(1)}, f32[256,128]{1,0:T(8,128)S(1)}, u32[]{:S(2)}, u32[]{:S(2)}) collective-permute-start(f32[256,128]{1,0:T(8,128)S(1)} %pad_maximum_fusion), channel_id=1, source_target_pairs={{0,4},{4,0},{8,12},{12,8},{16,20},{20,16},{24,28},{28,24},{1,5},{5... | collective-permute-start | bytes 393224 | tf_op jit(solution)/shard_map/ppermute | solution.py:391
  10.8 0.7 %collective-permute-start.10 = (f32[640,128]{1,0:T(8,128)S(1)}, f32[640,128]{1,0:T(8,128)S(1)}, u32[]{:S(2)}, u32[]{:S(2)}) collective-permute-start(f32[640,128]{1,0:T(8,128)S(1)} %get-tuple-element.19), channel_id=1, source_target_pairs={{1,2},{2,1},{0,0},{3,3},{5,6},{6,5},{4,4},{7,7},{9,10},{10,9},{8,8... | collective-permute-start | bytes 983048 | tf_op jit(solution)/shard_map/ppermute | solution.py:446
  11.5 2.3 %collective-permute-done.2.inner = f32[256,128]{1,0:T(8,128)S(1)} collective-permute-done((f32[256,128]{1,0:T(8,128)S(1)}, f32[256,128]{1,0:T(8,128)S(1)}, u32[]{:S(2)}, u32[]{:S(2)}) %collective-permute-start.2) | collective-permute-done | bytes 131104 | tf_op jit(solution)/shard_map/ppermute | solution.py:391
  13.8 4.2 %collective-permute-start.5 = (f32[2,88,128]{2,1,0:T(8,128)S(1)}, f32[2,88,128]{2,1,0:T(8,128)S(1)}, u32[]{:S(2)}, u32[]{:S(2)}) collective-permute-start(f32[2,88,128]{2,1,0:T(8,128)S(1)} %pad_maximum_fusion.1.rest_0_), channel_id=1, source_target_pairs={{0,24},{4,28},{8,16},{12,20},{16,8},{20,12},{24,0},{28,4},{1,25},{... | collective-permute-start | bytes 270344 | tf_op jit(solution)/shard_map/ppermute | solution.py:391
  18.0 0.0 collective-permute-start.4
  18.0 0.6 %collective-permute-start.3 = (f32[2,88,128]{2,1,0:T(8,128)S(1)}, f32[2,88,128]{2,1,0:T(8,128)S(1)}, u32[]{:S(2)}, u32[]{:S(2)}) collective-permute-start(f32[2,88,128]{2,1,0:T(8,128)S(1)} %pad_maximum_fusion.1.rest_0_), channel_id=1, source_target_pairs={{0,8},{4,12},{8,0},{12,4},{16,24},{20,28},{24,16},{28,20},{1,9},{5... | collective-permute-start | bytes 270344 | tf_op jit(solution)/shard_map/ppermute | solution.py:391
  18.6 0.0 collective-permute-start.6
  18.6 2.9 %collective-permute-done.5.rest_3_ = f32[2,88,128]{2,1,0:T(8,128)S(1)} collective-permute-done((f32[2,88,128]{2,1,0:T(8,128)S(1)}, f32[2,88,128]{2,1,0:T(8,128)S(1)}, u32[]{:S(2)}, u32[]{:S(2)}) %collective-permute-start.5) | collective-permute-done | bytes 90144 | tf_op jit(solution)/shard_map/ppermute | solution.py:391
  21.5 0.0 collective-permute-start.9
  21.5 4.3 %collective-permute-done.4.rest_2_ = f32[2,88,128]{2,1,0:T(8,128)S(1)} collective-permute-done((f32[2,88,128]{2,1,0:T(8,128)S(1)}, f32[2,88,128]{2,1,0:T(8,128)S(1)}, u32[]{:S(2)}, u32[]{:S(2)}) %collective-permute-start.4) | collective-permute-done | bytes 90144 | tf_op jit(solution)/shard_map/ppermute | solution.py:391
  25.8 0.0 collective-permute-start.8
  25.8 0.0 collective-permute-done.3.rest_1_
  25.8 0.5 %collective-permute-start.7 = (f32[2,88,128]{2,1,0:T(8,128)S(1)}, f32[2,88,128]{2,1,0:T(8,128)S(1)}, u32[]{:S(2)}, u32[]{:S(2)}) collective-permute-start(f32[2,88,128]{2,1,0:T(8,128)S(1)} %collective-permute-done.3.rest_1_), channel_id=1, source_target_pairs={{0,1},{1,0},{2,3},{3,2},{4,5},{5,4},{6,7},{7,6},{8,9},{9,8},{10,11... | collective-permute-start | bytes 270344 | tf_op jit(solution)/shard_map/ppermute | solution.py:391
  26.3 0.0 collective-permute-done.6.rest_4_
  26.3 2.6 %collective-permute-start.11 = (f32[168,128]{1,0:T(8,128)S(1)}, f32[168,128]{1,0:T(8,128)S(1)}, u32[]{:S(2)}, u32[]{:S(2)}) collective-permute-start(f32[168,128]{1,0:T(8,128)S(1)} %get-tuple-element.20), channel_id=1, source_target_pairs={{4,8},{12,16},{20,24},{28,0},{8,4},{16,12},{24,20},{0,28},{5,9},{1... | collective-permute-start | bytes 258056 | tf_op jit(solution)/shard_map/ppermute | solution.py:448
  28.9 0.0 collective-permute-done.9.rest_7_
  28.9 0.0 collective-permute-done.8.rest_6_
  28.9 0.0 collective-permute-done.7.rest_5_
  28.9 0.0 copy-done.1
  28.9 0.0 copy-done
  28.9 5.8 %analyse_near.1 = (f32[28,80,128]{2,1,0:T(8,128)S(1)}, bf16[2,256,256]{2,1,0:T(8,128)(2,1)S(1)}, bf16[2,160,256]{2,1,0:T(8,128)(2,1)S(1)}, f32[2,256,128]{2,1,0:T(8,128)S(1)}, f32[2,256,128]{2,1,0:T(8,128)S(1)}) custom-call(s32[8,128]{1,0:T(8,128)S(1)} %copy-done.1, f32[1280,128]{1,0:T(8,128)S(1)} %bitcast.11, ...), custom_call_target="tpu_custom_call" | custom-call | tf_op jit(solution)/shard_map/analyse_near/pallas_call | solution.py:459
  34.7 0.0 collective-permute-done.11.outer
  34.7 0.0 collective-permute-done.10.y_edge
  34.8 0.0 copy-done.2
  34.8 2.8 %analyse_far_and_step.1 = f32[1280,128]{1,0:T(8,128)} custom-call(s32[8,128]{1,0:T(8,128)S(1)} %copy-done.1, f32[16,128]{1,0:T(8,128)S(1)} %bitcast.12, f32[28,80,128]{2,1,0:T(8,128)S(1)} %get-tuple-element.18.near, f32[640,128]{1,0:T(8,128)S(1)} %collective-permute-done.10.y_edge, f32[168,128]{1,0:T(8,128)S(1)} %collective-permute-done.11.outer, ...), custom_call_target="tpu_custom_call" | custom-call | tf_op jit(solution)/shard_map/analyse_far_and_step/pallas_call | solution.py:478
  (5 shorter events, 0.0 us)
Async XLA Ops:
  0.0 28.9 %copy-start.1 = (s32[8,128]{1,0:T(8,128)S(1)}, s32[8,128]{1,0:T(8,128)}, u32[]{:S(2)}) copy-start(s32[8,128]{1,0:T(8,128)} %mask.5) | copy-start | bytes 12292
  0.0 28.9 %copy-start = (f32[80,2,8,128]{3,2,1,0:T(8,128)S(1)}, f32[80,2,8,128]{3,2,1,0:T(8,128)}, u32[]{:S(2)}) copy-start(f32[80,2,8,128]{3,2,1,0:T(8,128)} %param.8) | copy-start | bytes 1966084
  1.9 1.8 %collective-permute-start = (f32[728,128]{1,0:T(8,128)S(1)}, f32[728,128]{1,0:T(8,128)S(1)}, u32[]{:S(2)}, u32[]{:S(2)}) collective-permute-start(f32[728,128]{1,0:T(8,128)S(1)} %get-tuple-element.15), channel_id=1, source_target_pairs={{0,1},{1,0},{2,3},{3,2},{4,5},{5,4},{6,7},{7,6},{8,9},{9,8},{10,11... | collective-permute-start | bytes 1118216 | tf_op jit(solution)/shard_map/ppermute | solution.py:391
  3.8 5.0 %collective-permute-start.1 = (f32[88,128]{1,0:T(8,128)S(1)}, f32[88,128]{1,0:T(8,128)S(1)}, u32[]{:S(2)}, u32[]{:S(2)}) collective-permute-start(f32[88,128]{1,0:T(8,128)S(1)} %slice_add_fusion), channel_id=1, source_target_pairs={{0,2},{1,3},{2,0},{3,1},{4,6},{5,7},{6,4},{7,5},{8,10},{9,11},{10,... | collective-permute-start | bytes 135176 | tf_op jit(solution)/shard_map/ppermute | solution.py:391
  8.8 26.0 %copy-start.2 = (f32[2,8,128]{2,1,0:T(8,128)S(1)}, f32[2,8,128]{2,1,0:T(8,128)}, u32[]{:S(2)}) copy-start(f32[2,8,128]{2,1,0:T(8,128)} %param.15) | copy-start | bytes 24580
  8.8 5.0 %collective-permute-start.2 = (f32[256,128]{1,0:T(8,128)S(1)}, f32[256,128]{1,0:T(8,128)S(1)}, u32[]{:S(2)}, u32[]{:S(2)}) collective-permute-start(f32[256,128]{1,0:T(8,128)S(1)} %pad_maximum_fusion), channel_id=1, source_target_pairs={{0,4},{4,0},{8,12},{12,8},{16,20},{20,16},{24,28},{28,24},{1,5},{5... | collective-permute-start | bytes 393224 | tf_op jit(solution)/shard_map/ppermute | solution.py:391
  10.8 23.9 %collective-permute-start.10 = (f32[640,128]{1,0:T(8,128)S(1)}, f32[640,128]{1,0:T(8,128)S(1)}, u32[]{:S(2)}, u32[]{:S(2)}) collective-permute-start(f32[640,128]{1,0:T(8,128)S(1)} %get-tuple-element.19), channel_id=1, source_target_pairs={{1,2},{2,1},{0,0},{3,3},{5,6},{6,5},{4,4},{7,7},{9,10},{10,9},{8,8... | collective-permute-start | bytes 983048 | tf_op jit(solution)/shard_map/ppermute | solution.py:446
  13.8 7.7 %collective-permute-start.5 = (f32[2,88,128]{2,1,0:T(8,128)S(1)}, f32[2,88,128]{2,1,0:T(8,128)S(1)}, u32[]{:S(2)}, u32[]{:S(2)}) collective-permute-start(f32[2,88,128]{2,1,0:T(8,128)S(1)} %pad_maximum_fusion.1.rest_0_), channel_id=1, source_target_pairs={{0,24},{4,28},{8,16},{12,20},{16,8},{20,12},{24,0},{28,4},{1,25},{... | collective-permute-start | bytes 270344 | tf_op jit(solution)/shard_map/ppermute | solution.py:391
  18.0 7.8 %collective-permute-start.4 = (f32[2,88,128]{2,1,0:T(8,128)S(1)}, f32[2,88,128]{2,1,0:T(8,128)S(1)}, u32[]{:S(2)}, u32[]{:S(2)}) collective-permute-start(f32[2,88,128]{2,1,0:T(8,128)S(1)} %pad_maximum_fusion.1.rest_0_), channel_id=1, source_target_pairs={{0,16},{4,20},{8,24},{12,28},{16,0},{20,4},{24,8},{28,12},{1,17},{... | collective-permute-start | bytes 270344 | tf_op jit(solution)/shard_map/ppermute | solution.py:391
  18.0 7.8 %collective-permute-start.3 = (f32[2,88,128]{2,1,0:T(8,128)S(1)}, f32[2,88,128]{2,1,0:T(8,128)S(1)}, u32[]{:S(2)}, u32[]{:S(2)}) collective-permute-start(f32[2,88,128]{2,1,0:T(8,128)S(1)} %pad_maximum_fusion.1.rest_0_), channel_id=1, source_target_pairs={{0,8},{4,12},{8,0},{12,4},{16,24},{20,28},{24,16},{28,20},{1,9},{5... | collective-permute-start | bytes 270344 | tf_op jit(solution)/shard_map/ppermute | solution.py:391
  18.6 7.7 %collective-permute-start.6 = (f32[2,88,128]{2,1,0:T(8,128)S(1)}, f32[2,88,128]{2,1,0:T(8,128)S(1)}, u32[]{:S(2)}, u32[]{:S(2)}) collective-permute-start(f32[2,88,128]{2,1,0:T(8,128)S(1)} %pad_maximum_fusion.1.rest_0_), channel_id=1, source_target_pairs={{0,1},{1,0},{2,3},{3,2},{4,5},{5,4},{6,7},{7,6},{8,9},{9,8},{10,11... | collective-permute-start | bytes 270344 | tf_op jit(solution)/shard_map/ppermute | solution.py:391
  21.5 7.4 %collective-permute-start.9 = (f32[2,88,128]{2,1,0:T(8,128)S(1)}, f32[2,88,128]{2,1,0:T(8,128)S(1)}, u32[]{:S(2)}, u32[]{:S(2)}) collective-permute-start(f32[2,88,128]{2,1,0:T(8,128)S(1)} %collective-permute-done.5.rest_3_), channel_id=1, source_target_pairs={{0,1},{1,0},{2,3},{3,2},{4,5},{5,4},{6,7},{7,6},{8,9},{9,8},{10,11... | collective-permute-start | bytes 270344 | tf_op jit(solution)/shard_map/ppermute | solution.py:391
  25.8 3.1 %collective-permute-start.8 = (f32[2,88,128]{2,1,0:T(8,128)S(1)}, f32[2,88,128]{2,1,0:T(8,128)S(1)}, u32[]{:S(2)}, u32[]{:S(2)}) collective-permute-start(f32[2,88,128]{2,1,0:T(8,128)S(1)} %collective-permute-done.4.rest_2_), channel_id=1, source_target_pairs={{0,1},{1,0},{2,3},{3,2},{4,5},{5,4},{6,7},{7,6},{8,9},{9,8},{10,11... | collective-permute-start | bytes 270344 | tf_op jit(solution)/shard_map/ppermute | solution.py:391
  25.8 3.1 %collective-permute-start.7 = (f32[2,88,128]{2,1,0:T(8,128)S(1)}, f32[2,88,128]{2,1,0:T(8,128)S(1)}, u32[]{:S(2)}, u32[]{:S(2)}) collective-permute-start(f32[2,88,128]{2,1,0:T(8,128)S(1)} %collective-permute-done.3.rest_1_), channel_id=1, source_target_pairs={{0,1},{1,0},{2,3},{3,2},{4,5},{5,4},{6,7},{7,6},{8,9},{9,8},{10,11... | collective-permute-start | bytes 270344 | tf_op jit(solution)/shard_map/ppermute | solution.py:391
  26.3 8.4 %collective-permute-start.11 = (f32[168,128]{1,0:T(8,128)S(1)}, f32[168,128]{1,0:T(8,128)S(1)}, u32[]{:S(2)}, u32[]{:S(2)}) collective-permute-start(f32[168,128]{1,0:T(8,128)S(1)} %get-tuple-element.20), channel_id=1, source_target_pairs={{4,8},{12,16},{20,24},{28,0},{8,4},{16,12},{24,20},{0,28},{5,9},{1... | collective-permute-start | bytes 258056 | tf_op jit(solution)/shard_map/ppermute | solution.py:448

commit v3 on v2

--- a/solution.py
+++ b/solution.py
@@ -24,6 +24,8 @@
 Y_ROW = 26
 OUTER_ROW = 34
 EXT_ROWS = 36
+ROW_LIMIT = 40
+ROW_COLUMN = 24
 
 LATERAL_MIX = 0.2
 VERTICAL_MIX = 0.15
@@ -65,7 +67,7 @@
     return lax.axis_index("col").astype(jnp.int32), lax.axis_index("gz").astype(jnp.int32)
 
 
-def pick_kernel(members, columns, count, linked, site, value, noise, mask, state, kept, core_send, y_send, inner, outer):
+def pick_kernel(members, columns, count, linked, site, value, noise, mask, state, kept, core_send, y_send, inner, outer, rows):
     col, gz = position()
     core = gz % 2
     lane = iota((1, CAP), 1)
@@ -83,6 +85,7 @@
         left = []
         for r in (2 * pair, 2 * pair + 1):
             x = state[pl.ds(r, members, stride=ROWS), :]
+            rows[r] = x
             high = x.astype(BF16)
             rest = x - high.astype(F32)
             middle = rest.astype(BF16)
@@ -141,25 +144,25 @@
     lon_all = columns * LONS
     odd = gz % 2
     even_col = col % 2 == 0
-    lane = iota((1, LATS), 1)
+    at = iota((ROW_LIMIT, 1), 0)
     above, below = LEVS * gz + LEVS, LEVS * gz - 1
-    own = lane < ROWS
-    near = (lane >= CORE_ROW) & (lane < INNER_ROW)
-    far = (lane >= Y_ROW) & (lane < OUTER_ROW)
-    row_lev = LEVS * gz + jnp.where(own, lane // LONS, lane % LEVS)
+    own = at < ROWS
+    near = (at >= CORE_ROW) & (at < INNER_ROW)
+    far = (at >= Y_ROW) & (at < OUTER_ROW)
+    row_lev = LEVS * gz + jnp.where(own, at // LONS, at % LEVS)
     row_lev = jnp.where(near, jnp.where(odd == 0, above, below), row_lev)
     row_lev = jnp.where(far, jnp.where(odd == 0, below, above), row_lev)
     west_lon = (col * LONS + lon_all - 1) % lon_all
     east_lon = (col * LONS + LONS) % lon_all
-    inner = (lane >= INNER_ROW) & (lane < Y_ROW)
-    row_lon = col * LONS + jnp.where(far, lane - Y_ROW, lane % LONS)
+    inner = (at >= INNER_ROW) & (at < Y_ROW)
+    row_lon = col * LONS + jnp.where(far, at - Y_ROW, at % LONS)
     row_lon = jnp.where(inner, jnp.where(even_col, east_lon, west_lon), row_lon)
-    row_lon = jnp.where(lane >= OUTER_ROW, jnp.where(even_col, west_lon, east_lon), row_lon)
+    row_lon = jnp.where(at >= OUTER_ROW, jnp.where(even_col, west_lon, east_lon), row_lon)
     west_col = (col + columns - 1) % columns
     east_col = (col + 1) % columns
     inner_col = jnp.where(even_col, east_col, west_col)
     outer_col = jnp.where(even_col, west_col, east_col)
-    return row_lev.astype(F32), row_lon.astype(F32), inner, inner_col, outer_col
+    return row_lev.astype(F32), row_lon.astype(F32), inner, at >= OUTER_ROW, inner_col, outer_col
 
 
 def centred_parts(x):
@@ -184,7 +187,8 @@
         for r in range(first, last, 2):
             at = r - first
             x = jnp.concatenate([fields[at], fields[at + 1]], 1)
-            tapers = [lat_part[t] * row_part[t, :, r + h : r + h + 1] for h in range(2)]
+            columns = [ROW_COLUMN + r + h for h in range(2)]
+            tapers = [lat_part[t] * row_part[t, :, c : c + 1] for c in columns]
             moved = increment(x, sides[t], gains[t], jnp.concatenate(tapers, 1))
             moved = moved * jnp.concatenate([ocean[at], ocean[at + 1]], 1)
             for h in range(2):
@@ -202,7 +206,7 @@
             fields[at] = fields[at] + gained[at]
 
 
-def near_kernel(members, parts, columns, around, chunks, mask, state, core_edge, inner, *rest):
+def near_kernel(members, parts, columns, around, chunks, mask, own, core_edge, inner, *rest):
     mine_parts, other_parts = rest[: len(parts)], rest[len(parts) : 2 * len(parts)]
     fields, sides, gains, row_terms, lat_terms, packed, gained = rest[2 * len(parts) :]
     mine = [part.at[i] for part, size in zip(mine_parts, parts) for i in range(size)]
@@ -216,22 +220,31 @@
     height = members + 8
     owners = [col ^ j if around is None else (col + around[j] + columns) % columns for j in range(blocks)]
 
-    links = []
-    packed[...] = jnp.zeros_like(packed)
+    lane = iota((1, LATS), 1)
+    pad = (-blocks) % 16
+    tables = []
     for b in range(BATCHES):
-        start = 0
-        own_links = []
+        start = jnp.zeros((1, CAP), jnp.int32)
+        tiles = [jnp.zeros((height, CAP), F32)] * (chunks * CHUNK // CAP)
+        links = []
         for j in range(blocks):
             block = jnp.where(core == b, mine[j][...], other[j][...])
-            own_links.append(block[place["links"] : place["links"] + 1, :])
-            tall = jnp.concatenate([block, jnp.zeros((LATS - height, CAP), F32)], 0)
-            packed[b, pl.ds(start, CAP), :] = tall.T
-            start = start + block[place["count"], 0].astype(jnp.int32)
-        links.append(own_links)
+            links.append(block[place["links"] : place["links"] + 1, :])
+            if j == 0:
+                tiles[0] = block
+            else:
+                shift = start % CAP
+                turned = pltpu.roll(block, shift[0, 0], 1)
+                into = start // CAP + jnp.where(lane < shift, 1, 0)
+                tiles = [tile + jnp.where(into == i, turned, 0.0) for i, tile in enumerate(tiles)]
+            start = start + block[place["count"] : place["count"] + 1, :].astype(jnp.int32)
+        for i, tile in enumerate(tiles):
+            packed[b, i] = tile
+        tables.append(jnp.concatenate(links + [jnp.zeros((pad, CAP), F32)] * (pad > 0), 0).astype(BF16))
 
     inner_start = inner.shape[0] - (members * LEVS + 8)
     for r in range(ROWS):
-        fields[r] = state[pl.ds(r, members, stride=ROWS), :]
+        fields[r] = own[r]
     for lon in range(LONS):
         fields[CORE_ROW + lon] = core_edge[pl.ds(height + lon, members, stride=LONS), :]
     for lev in range(LEVS):
@@ -242,14 +255,7 @@
     at = inner_start + members * LEVS
     ocean += [inner[at : at + 1, :]] * LEVS
 
-    lane = iota((1, LATS), 1)
-    row_lev, row_lon, inside, inner_col, outer_col = place_terms(col, gz, columns)
-
-    def links_of(b, target):
-        row = jnp.zeros((1, CAP), F32)
-        for j in range(blocks):
-            row = row + jnp.where(owners[j] == target, links[b][j], 0.0)
-        return row
+    row_lev, row_lon, inside, outside, inner_col, outer_col = place_terms(col, gz, columns)
 
     def places(site, owner):
         site = site.astype(jnp.int32)
@@ -271,62 +277,72 @@
         return 1.0 + gap * gap
 
     def slots_of(b, k):
-        start = k * CHUNK if isinstance(k, int) else pl.multiple_of(k * CHUNK, CHUNK)
-        tall = packed[b, pl.ds(start, CHUNK), :]
-        return tall, tall.T
+        wide = jnp.concatenate([packed[b, 2 * k], packed[b, 2 * k + 1]], 1)
+
+        def row(name):
+            return wide[place[name] : place[name] + 1]
+
+        return wide, row
 
     def batch_terms(b, k):
-        tall, wide = slots_of(b, k)
-        occupied = wide[place["occupied"] : place["occupied"] + 1]
+        wide, row = slots_of(b, k)
+        occupied = row("occupied")
         if b == 0:
             prior = wide[:members]
         else:
             prior = jnp.concatenate([fields[Y_ROW + 2 * k], fields[Y_ROW + 2 * k + 1]], 1) * occupied
-        value = wide[place["value"] : place["value"] + 1]
-        noise = jnp.where(occupied > 0, wide[place["noise"] : place["noise"] + 1], 1.0)
+        noise = jnp.where(occupied > 0, row("noise"), 1.0)
         mean = jnp.sum(prior, 0, keepdims=True) / members
         anomaly = prior - mean
         spread = jnp.sum(anomaly * anomaly, 0, keepdims=True) * denominator
         total = spread + noise
         shrink = 1.0 / (1.0 + jnp.sqrt(noise / total))
-        gain = ((value - mean) - shrink * anomaly) / total
+        gain = ((row("value") - mean) - shrink * anomaly) / total
         high = anomaly.astype(BF16).astype(F32)
         stack = jnp.concatenate([high, high, anomaly - high, jnp.zeros((16, CHUNK), F32)], 0)
         t = b * chunks + k
         sides[t] = stack.T.astype(BF16)
         gains[t] = jnp.concatenate(halves(gain), 0)
 
-        def column(name):
-            return tall[:, place[name] : place[name] + 1]
-
-        lev, lon, lat = places(column("site"), column("owner"))
-        holder = jnp.where(lane.astype(F32) == column("owner"), 1.0, 0.0)
-        weight = [jnp.sum(holder * links_of(b, c), 1, keepdims=True) for c in (col, inner_col, outer_col)]
-        weight = jnp.where(inside, weight[1], jnp.where(lane < OUTER_ROW, weight[0], weight[2]))
-        row_terms[t] = weight * denominator / (lev_square(row_lev, lev) * lon_square(row_lon, lon))
-        lat_terms[t] = 1.0 / lat_square(lane.astype(F32), lat)
-        return lev, lon, lat, holder
-
-    def site_weights(where0, k1):
-        lev0, lon0, lat0, holder = where0
-        tall, wide = slots_of(1, k1)
-        owner = wide[place["owner"] : place["owner"] + 1]
-        lev, lon, lat = places(wide[place["site"] : place["site"] + 1], owner)
-        pad = (-blocks) % 16
-        spare = [jnp.zeros((pad, CAP), F32)] if pad else []
-        table = jnp.concatenate(links[0] + spare, 0).astype(BF16)
-        by_block = dot_lanes(holder.astype(BF16), table).astype(BF16)
-        spare = [jnp.zeros((pad, CHUNK), F32)] if pad else []
+    def batch_tapers(b, k):
+        wide, row = slots_of(b, k)
+        owner = row("owner")
+        lev, lon, lat = places(row("site"), owner)
+        holder = jnp.where(iota((CAP, CHUNK), 0).astype(F32) == owner, 1.0, 0.0).astype(BF16)
+        by_block = dot(tables[b], holder)
+        weight = []
+        for target in (col, inner_col, outer_col):
+            total = jnp.zeros((1, CHUNK), F32)
+            for j in range(blocks):
+                total = total + jnp.where(owners[j] == target, by_block[j : j + 1], 0.0)
+            weight.append(total)
+        weight = jnp.where(inside, weight[1], jnp.where(outside, weight[2], weight[0]))
+        weight = weight * denominator / (lev_square(row_lev, lev) * lon_square(row_lon, lon))
+        spare = LATS - ROW_COLUMN - ROW_LIMIT
+        table = jnp.concatenate(
+            [lat, lev, lon, jnp.zeros((5, CHUNK), F32), by_block[:16], weight, jnp.zeros((spare, CHUNK), F32)], 0
+        )
+        t = b * chunks + k
+        row_terms[t] = table.T
+        lat_terms[t] = 1.0 / lat_square(lane.astype(F32), row_terms[t, :, 0:1])
+
+    def site_weights(k0, k1):
+        wide, row = slots_of(1, k1)
+        owner = row("owner")
+        lev, lon, lat = places(row("site"), owner)
         there = [jnp.where(owner == owners[j].astype(F32), 1.0, 0.0) for j in range(blocks)]
-        weight = dot(by_block, jnp.concatenate(there + spare, 0).astype(BF16))
+        there += [jnp.zeros((pad, CHUNK), F32)] * (pad > 0)
+        weight = dot(row_terms[k0, :, 8:24].astype(BF16), jnp.concatenate(there, 0).astype(BF16))
+        lat0, lev0, lon0 = [row_terms[k0, :, i : i + 1] for i in range(3)]
         square = lat_square(lat0, lat) * lon_square(lon0, lon) * lev_square(lev0, lev)
         return weight * denominator / square, wide
 
     def first_terms(k):
-        where = batch_terms(0, k)
+        batch_terms(0, k)
+        batch_tapers(0, k)
 
         def site_chunk(k1):
-            taper, wide = site_weights(where, k1)
+            taper, wide = site_weights(k, k1)
             x = wide[:members]
             moved = increment(x, sides[k], gains[k], taper) * wide[members : members + 1]
             for h in range(2):
@@ -337,9 +353,13 @@
 
         for_each(chunks, site_chunk)
 
+    def second_terms(k):
+        batch_terms(1, k)
+        batch_tapers(1, k)
+
     terms = (sides, gains, row_terms, lat_terms)
     for_each(chunks, first_terms)
-    for_each(chunks, lambda k: (batch_terms(1, k), None)[1])
+    for_each(chunks, second_terms)
     for b in range(BATCHES):
         move_rows(fields, gained, 0, Y_ROW, ocean, terms, b, chunks)
 
@@ -410,11 +430,11 @@
     def like(*lengths):
         return [pltpu.VMEM((length, LATS), F32) for length in lengths]
 
-    kept, core_send, y_send, inner, outer = pl.pallas_call(
+    kept, core_send, y_send, inner, outer, own = pl.pallas_call(
         functools.partial(pick_kernel, members, columns),
-        out_shape=like(height, height + level, level, edge, edge),
+        out_shape=like(height, height + level, level, edge, edge) + [pltpu.VMEM((ROWS, members, LATS), F32)],
         in_specs=[smem] + [vmem] * 6,
-        out_specs=[vmem] * 5,
+        out_specs=[vmem] * 6,
         name="pick_priors",
     )(
         obs_count.reshape(1, BATCHES),
@@ -468,13 +488,13 @@
         in_specs=[vmem] * (4 + 2 * len(parts)),
         out_specs=[vmem] * 5,
         scratch_shapes=[
-            pltpu.VMEM((BATCHES, chunks * CHUNK + CAP, CAP), F32),
+            pltpu.VMEM((BATCHES, chunks * CHUNK // CAP, height, CAP), F32),
             pltpu.VMEM((Y_ROW if several else 1, members, LATS), F32),
         ],
         compiler_params=limit,
         cost_estimate=pl.CostEstimate(flops=0, bytes_accessed=0, transcendentals=0),
         name="analyse_near",
-    )(ocean_mask, flat, core_edge, inner, *gathered, *other)
+    )(ocean_mask, own, core_edge, inner, *gathered, *other)
     out = pl.pallas_call(
         functools.partial(far_kernel, members, columns, floors, chunks),
         out_shape=jax.ShapeDtypeStruct((members * ROWS, LATS), F32),

time: 37.7 us -> 36.6 us (0.971)
  Pallas kernels: 10.5 us -> 9.41 us
    pallas_call x1, Pallas kernels: 5.81 us -> 4.77 us  [local(): pl.pallas_call(functools.partial(near_kernel, members, parts, columns, ar...]
  transfers between devices with their start and end apart: 12 -> 12, of which waited for: 5 -> 5; matrix products, arithmetic and copies ran while one was open for 0% -> 0% of each run, Pallas kernels for 15% -> 13%
where the time goes in v3:
time: 36.6 us; the launch traced here: 36.5 us
  starting transfers between devices  14.1 us (39%)
  waiting for transfers between devices  12.8 us (35%)
  Pallas kernels  9.41 us (26%)
    ppermute x10, waiting for transfers between devices, swapped(): lax.ppermute(x, axis, [(i, i ^ bit) for i in range(lax.axis_size(axis))])  12.8 us
    ppermute x10, starting transfers between devices, swapped(): lax.ppermute(x, axis, [(i, i ^ bit) for i in range(lax.axis_size(axis))])  10.9 us
    pallas_call x1, Pallas kernels, local(): pl.pallas_call(functools.partial(near_kernel, members, parts, columns, ar...  4.77 us
    pallas_call x1, Pallas kernels, local(): pl.pallas_call(functools.partial(far_kernel, members, columns, floors, ch...  2.76 us
    ppermute x1, starting transfers between devices, local(): outer = lax.ppermute(outer, 'col', ring + [(j, i) for i, j in ring])  2.57 us
    pallas_call x1, Pallas kernels, local(): pl.pallas_call(functools.partial(pick_kernel, members, columns), out_shap...  1.87 us
  transfers between devices with their start and end apart: 12, of which 5 were waited for; matrix products, arithmetic and copies ran while one was open for 0% of the time, Pallas kernels for 13%

profile of v3, /device:TPU:0, one launch (start us, length us, event | category | flops | bytes accessed | tf_op | source)
XLA Modules:
  0.0 36.5 jit_solution(6181104540254063864)
XLA Ops:
  0.0 0.0 copy-start
  0.0 1.9 %pick_priors.1 = (f32[88,128]{1,0:T(8,128)S(1)}, f32[728,128]{1,0:T(8,128)S(1)}, f32[640,128]{1,0:T(8,128)S(1)}, f32[168,128]{1,0:T(8,128)S(1)}, f32[168,128]{1,0:T(8,128)S(1)}, /*index=5*/f32[16,80,128]{2,1,0:T(8,128)S(1)}) custom-call(s32[1,2]{1,0:T(1,128)} %bitcast.14, s32[2,1,8]{2,1,0:T(1,128)} %bitcast.13, s32[2,1024]{1,0:T(2,128)} %site.1, ...), custom_call_target="tpu_custom_call" | custom-call | tf_op jit(solution)/shard_map/pick_priors/pallas_call | solution.py:433
  1.9 0.5 %collective-permute-start = (f32[728,128]{1,0:T(8,128)S(1)}, f32[728,128]{1,0:T(8,128)S(1)}, u32[]{:S(2)}, u32[]{:S(2)}) collective-permute-start(f32[728,128]{1,0:T(8,128)S(1)} %get-tuple-element.17), channel_id=1, source_target_pairs={{0,1},{1,0},{2,3},{3,2},{4,5},{5,4},{6,7},{7,6},{8,9},{9,8},{10,11... | collective-permute-start | bytes 1118216 | tf_op jit(solution)/shard_map/ppermute | solution.py:411
  2.4 1.3 %collective-permute-done.core_edge = f32[728,128]{1,0:T(8,128)S(1)} collective-permute-done((f32[728,128]{1,0:T(8,128)S(1)}, f32[728,128]{1,0:T(8,128)S(1)}, u32[]{:S(2)}, u32[]{:S(2)}) %collective-permute-start) | collective-permute-done | bytes 372768 | tf_op jit(solution)/shard_map/ppermute | solution.py:411
  3.7 2.9 %collective-permute-start.1 = (f32[88,128]{1,0:T(8,128)S(1)}, f32[88,128]{1,0:T(8,128)S(1)}, u32[]{:S(2)}, u32[]{:S(2)}) collective-permute-start(f32[88,128]{1,0:T(8,128)S(1)} %slice_add_fusion), channel_id=1, source_target_pairs={{0,2},{1,3},{2,0},{3,1},{4,6},{5,7},{6,4},{7,5},{8,10},{9,11},{10,... | collective-permute-start | bytes 135176 | tf_op jit(solution)/shard_map/ppermute | solution.py:411
  6.7 2.0 %collective-permute-done.1 = f32[88,128]{1,0:T(8,128)S(1)} collective-permute-done((f32[88,128]{1,0:T(8,128)S(1)}, f32[88,128]{1,0:T(8,128)S(1)}, u32[]{:S(2)}, u32[]{:S(2)}) %collective-permute-start.1) | collective-permute-done | bytes 45088 | tf_op jit(solution)/shard_map/ppermute | solution.py:411
  8.7 0.0 copy-start.1
  8.7 2.1 %collective-permute-start.2 = (f32[256,128]{1,0:T(8,128)S(1)}, f32[256,128]{1,0:T(8,128)S(1)}, u32[]{:S(2)}, u32[]{:S(2)}) collective-permute-start(f32[256,128]{1,0:T(8,128)S(1)} %pad_maximum_fusion), channel_id=1, source_target_pairs={{0,4},{4,0},{8,12},{12,8},{16,20},{20,16},{24,28},{28,24},{1,5},{5... | collective-permute-start | bytes 393224 | tf_op jit(solution)/shard_map/ppermute | solution.py:411
  10.8 0.7 %collective-permute-start.10 = (f32[640,128]{1,0:T(8,128)S(1)}, f32[640,128]{1,0:T(8,128)S(1)}, u32[]{:S(2)}, u32[]{:S(2)}) collective-permute-start(f32[640,128]{1,0:T(8,128)S(1)} %get-tuple-element.21), channel_id=1, source_target_pairs={{1,2},{2,1},{0,0},{3,3},{5,6},{6,5},{4,4},{7,7},{9,10},{10,9},{8,8... | collective-permute-start | bytes 983048 | tf_op jit(solution)/shard_map/ppermute | solution.py:466
  11.5 2.3 %collective-permute-done.2.inner = f32[256,128]{1,0:T(8,128)S(1)} collective-permute-done((f32[256,128]{1,0:T(8,128)S(1)}, f32[256,128]{1,0:T(8,128)S(1)}, u32[]{:S(2)}, u32[]{:S(2)}) %collective-permute-start.2) | collective-permute-done | bytes 131104 | tf_op jit(solution)/shard_map/ppermute | solution.py:411
  13.8 4.2 %collective-permute-start.5 = (f32[2,88,128]{2,1,0:T(8,128)S(1)}, f32[2,88,128]{2,1,0:T(8,128)S(1)}, u32[]{:S(2)}, u32[]{:S(2)}) collective-permute-start(f32[2,88,128]{2,1,0:T(8,128)S(1)} %pad_maximum_fusion.1.rest_0_), channel_id=1, source_target_pairs={{0,24},{4,28},{8,16},{12,20},{16,8},{20,12},{24,0},{28,4},{1,25},{... | collective-permute-start | bytes 270344 | tf_op jit(solution)/shard_map/ppermute | solution.py:411
  18.0 0.0 collective-permute-start.4
  18.0 0.6 %collective-permute-start.3 = (f32[2,88,128]{2,1,0:T(8,128)S(1)}, f32[2,88,128]{2,1,0:T(8,128)S(1)}, u32[]{:S(2)}, u32[]{:S(2)}) collective-permute-start(f32[2,88,128]{2,1,0:T(8,128)S(1)} %pad_maximum_fusion.1.rest_0_), channel_id=1, source_target_pairs={{0,8},{4,12},{8,0},{12,4},{16,24},{20,28},{24,16},{28,20},{1,9},{5... | collective-permute-start | bytes 270344 | tf_op jit(solution)/shard_map/ppermute | solution.py:411
  18.6 0.0 collective-permute-start.6
  18.6 2.9 %collective-permute-done.5.rest_3_ = f32[2,88,128]{2,1,0:T(8,128)S(1)} collective-permute-done((f32[2,88,128]{2,1,0:T(8,128)S(1)}, f32[2,88,128]{2,1,0:T(8,128)S(1)}, u32[]{:S(2)}, u32[]{:S(2)}) %collective-permute-start.5) | collective-permute-done | bytes 90144 | tf_op jit(solution)/shard_map/ppermute | solution.py:411
  21.5 0.0 collective-permute-start.9
  21.5 4.3 %collective-permute-done.4.rest_2_ = f32[2,88,128]{2,1,0:T(8,128)S(1)} collective-permute-done((f32[2,88,128]{2,1,0:T(8,128)S(1)}, f32[2,88,128]{2,1,0:T(8,128)S(1)}, u32[]{:S(2)}, u32[]{:S(2)}) %collective-permute-start.4) | collective-permute-done | bytes 90144 | tf_op jit(solution)/shard_map/ppermute | solution.py:411
  25.8 0.0 collective-permute-start.8
  25.8 0.0 collective-permute-done.3.rest_1_
  25.8 0.5 %collective-permute-start.7 = (f32[2,88,128]{2,1,0:T(8,128)S(1)}, f32[2,88,128]{2,1,0:T(8,128)S(1)}, u32[]{:S(2)}, u32[]{:S(2)}) collective-permute-start(f32[2,88,128]{2,1,0:T(8,128)S(1)} %collective-permute-done.3.rest_1_), channel_id=1, source_target_pairs={{0,1},{1,0},{2,3},{3,2},{4,5},{5,4},{6,7},{7,6},{8,9},{9,8},{10,11... | collective-permute-start | bytes 270344 | tf_op jit(solution)/shard_map/ppermute | solution.py:411
  26.3 0.0 collective-permute-done.6.rest_4_
  26.3 2.6 %collective-permute-start.11 = (f32[168,128]{1,0:T(8,128)S(1)}, f32[168,128]{1,0:T(8,128)S(1)}, u32[]{:S(2)}, u32[]{:S(2)}) collective-permute-start(f32[168,128]{1,0:T(8,128)S(1)} %get-tuple-element.22), channel_id=1, source_target_pairs={{4,8},{12,16},{20,24},{28,0},{8,4},{16,12},{24,20},{0,28},{5,9},{1... | collective-permute-start | bytes 258056 | tf_op jit(solution)/shard_map/ppermute | solution.py:468
  28.9 0.0 collective-permute-done.9.rest_7_
  28.9 0.0 collective-permute-done.8.rest_6_
  28.9 0.0 collective-permute-done.7.rest_5_
  28.9 0.0 copy-done
  28.9 4.8 %analyse_near.1 = (f32[28,80,128]{2,1,0:T(8,128)S(1)}, bf16[2,256,256]{2,1,0:T(8,128)(2,1)S(1)}, bf16[2,160,256]{2,1,0:T(8,128)(2,1)S(1)}, f32[2,256,128]{2,1,0:T(8,128)S(1)}, f32[2,256,128]{2,1,0:T(8,128)S(1)}) custom-call(s32[8,128]{1,0:T(8,128)S(1)} %copy-done, f32[16,80,128]{2,1,0:T(8,128)S(1)} %get-tuple-element.16.own, ...), custom_call_target="tpu_custom_call" | custom-call | tf_op jit(solution)/shard_map/analyse_near/pallas_call | solution.py:479
  33.7 0.0 collective-permute-done.11.outer
  33.7 0.0 collective-permute-done.10.y_edge
  33.7 0.0 copy-done.1
  33.7 2.8 %analyse_far_and_step.1 = f32[1280,128]{1,0:T(8,128)} custom-call(s32[8,128]{1,0:T(8,128)S(1)} %copy-done, f32[16,128]{1,0:T(8,128)S(1)} %bitcast.10, f32[28,80,128]{2,1,0:T(8,128)S(1)} %get-tuple-element.20.near, f32[640,128]{1,0:T(8,128)S(1)} %collective-permute-done.10.y_edge, f32[168,128]{1,0:T(8,128)S(1)} %collective-permute-done.11.outer, ...), custom_call_target="tpu_custom_call" | custom-call | tf_op jit(solution)/shard_map/analyse_far_and_step/pallas_call | solution.py:498
  (5 shorter events, 0.0 us)
Async XLA Ops:
  0.0 28.9 %copy-start = (s32[8,128]{1,0:T(8,128)S(1)}, s32[8,128]{1,0:T(8,128)}, u32[]{:S(2)}) copy-start(s32[8,128]{1,0:T(8,128)} %mask.5) | copy-start | bytes 12292
  1.9 1.8 %collective-permute-start = (f32[728,128]{1,0:T(8,128)S(1)}, f32[728,128]{1,0:T(8,128)S(1)}, u32[]{:S(2)}, u32[]{:S(2)}) collective-permute-start(f32[728,128]{1,0:T(8,128)S(1)} %get-tuple-element.17), channel_id=1, source_target_pairs={{0,1},{1,0},{2,3},{3,2},{4,5},{5,4},{6,7},{7,6},{8,9},{9,8},{10,11... | collective-permute-start | bytes 1118216 | tf_op jit(solution)/shard_map/ppermute | solution.py:411
  3.7 5.0 %collective-permute-start.1 = (f32[88,128]{1,0:T(8,128)S(1)}, f32[88,128]{1,0:T(8,128)S(1)}, u32[]{:S(2)}, u32[]{:S(2)}) collective-permute-start(f32[88,128]{1,0:T(8,128)S(1)} %slice_add_fusion), channel_id=1, source_target_pairs={{0,2},{1,3},{2,0},{3,1},{4,6},{5,7},{6,4},{7,5},{8,10},{9,11},{10,... | collective-permute-start | bytes 135176 | tf_op jit(solution)/shard_map/ppermute | solution.py:411
  8.7 25.0 %copy-start.1 = (f32[2,8,128]{2,1,0:T(8,128)S(1)}, f32[2,8,128]{2,1,0:T(8,128)}, u32[]{:S(2)}) copy-start(f32[2,8,128]{2,1,0:T(8,128)} %param.15) | copy-start | bytes 24580
  8.7 5.0 %collective-permute-start.2 = (f32[256,128]{1,0:T(8,128)S(1)}, f32[256,128]{1,0:T(8,128)S(1)}, u32[]{:S(2)}, u32[]{:S(2)}) collective-permute-start(f32[256,128]{1,0:T(8,128)S(1)} %pad_maximum_fusion), channel_id=1, source_target_pairs={{0,4},{4,0},{8,12},{12,8},{16,20},{20,16},{24,28},{28,24},{1,5},{5... | collective-permute-start | bytes 393224 | tf_op jit(solution)/shard_map/ppermute | solution.py:411
  10.8 22.9 %collective-permute-start.10 = (f32[640,128]{1,0:T(8,128)S(1)}, f32[640,128]{1,0:T(8,128)S(1)}, u32[]{:S(2)}, u32[]{:S(2)}) collective-permute-start(f32[640,128]{1,0:T(8,128)S(1)} %get-tuple-element.21), channel_id=1, source_target_pairs={{1,2},{2,1},{0,0},{3,3},{5,6},{6,5},{4,4},{7,7},{9,10},{10,9},{8,8... | collective-permute-start | bytes 983048 | tf_op jit(solution)/shard_map/ppermute | solution.py:466
  13.8 7.7 %collective-permute-start.5 = (f32[2,88,128]{2,1,0:T(8,128)S(1)}, f32[2,88,128]{2,1,0:T(8,128)S(1)}, u32[]{:S(2)}, u32[]{:S(2)}) collective-permute-start(f32[2,88,128]{2,1,0:T(8,128)S(1)} %pad_maximum_fusion.1.rest_0_), channel_id=1, source_target_pairs={{0,24},{4,28},{8,16},{12,20},{16,8},{20,12},{24,0},{28,4},{1,25},{... | collective-permute-start | bytes 270344 | tf_op jit(solution)/shard_map/ppermute | solution.py:411
  18.0 7.8 %collective-permute-start.4 = (f32[2,88,128]{2,1,0:T(8,128)S(1)}, f32[2,88,128]{2,1,0:T(8,128)S(1)}, u32[]{:S(2)}, u32[]{:S(2)}) collective-permute-start(f32[2,88,128]{2,1,0:T(8,128)S(1)} %pad_maximum_fusion.1.rest_0_), channel_id=1, source_target_pairs={{0,16},{4,20},{8,24},{12,28},{16,0},{20,4},{24,8},{28,12},{1,17},{... | collective-permute-start | bytes 270344 | tf_op jit(solution)/shard_map/ppermute | solution.py:411
  18.0 7.8 %collective-permute-start.3 = (f32[2,88,128]{2,1,0:T(8,128)S(1)}, f32[2,88,128]{2,1,0:T(8,128)S(1)}, u32[]{:S(2)}, u32[]{:S(2)}) collective-permute-start(f32[2,88,128]{2,1,0:T(8,128)S(1)} %pad_maximum_fusion.1.rest_0_), channel_id=1, source_target_pairs={{0,8},{4,12},{8,0},{12,4},{16,24},{20,28},{24,16},{28,20},{1,9},{5... | collective-permute-start | bytes 270344 | tf_op jit(solution)/shard_map/ppermute | solution.py:411
  18.6 7.7 %collective-permute-start.6 = (f32[2,88,128]{2,1,0:T(8,128)S(1)}, f32[2,88,128]{2,1,0:T(8,128)S(1)}, u32[]{:S(2)}, u32[]{:S(2)}) collective-permute-start(f32[2,88,128]{2,1,0:T(8,128)S(1)} %pad_maximum_fusion.1.rest_0_), channel_id=1, source_target_pairs={{0,1},{1,0},{2,3},{3,2},{4,5},{5,4},{6,7},{7,6},{8,9},{9,8},{10,11... | collective-permute-start | bytes 270344 | tf_op jit(solution)/shard_map/ppermute | solution.py:411
  21.5 7.4 %collective-permute-start.9 = (f32[2,88,128]{2,1,0:T(8,128)S(1)}, f32[2,88,128]{2,1,0:T(8,128)S(1)}, u32[]{:S(2)}, u32[]{:S(2)}) collective-permute-start(f32[2,88,128]{2,1,0:T(8,128)S(1)} %collective-permute-done.5.rest_3_), channel_id=1, source_target_pairs={{0,1},{1,0},{2,3},{3,2},{4,5},{5,4},{6,7},{7,6},{8,9},{9,8},{10,11... | collective-permute-start | bytes 270344 | tf_op jit(solution)/shard_map/ppermute | solution.py:411
  25.8 3.1 %collective-permute-start.8 = (f32[2,88,128]{2,1,0:T(8,128)S(1)}, f32[2,88,128]{2,1,0:T(8,128)S(1)}, u32[]{:S(2)}, u32[]{:S(2)}) collective-permute-start(f32[2,88,128]{2,1,0:T(8,128)S(1)} %collective-permute-done.4.rest_2_), channel_id=1, source_target_pairs={{0,1},{1,0},{2,3},{3,2},{4,5},{5,4},{6,7},{7,6},{8,9},{9,8},{10,11... | collective-permute-start | bytes 270344 | tf_op jit(solution)/shard_map/ppermute | solution.py:411
  25.8 3.1 %collective-permute-start.7 = (f32[2,88,128]{2,1,0:T(8,128)S(1)}, f32[2,88,128]{2,1,0:T(8,128)S(1)}, u32[]{:S(2)}, u32[]{:S(2)}) collective-permute-start(f32[2,88,128]{2,1,0:T(8,128)S(1)} %collective-permute-done.3.rest_1_), channel_id=1, source_target_pairs={{0,1},{1,0},{2,3},{3,2},{4,5},{5,4},{6,7},{7,6},{8,9},{9,8},{10,11... | collective-permute-start | bytes 270344 | tf_op jit(solution)/shard_map/ppermute | solution.py:411
  26.3 7.4 %collective-permute-start.11 = (f32[168,128]{1,0:T(8,128)S(1)}, f32[168,128]{1,0:T(8,128)S(1)}, u32[]{:S(2)}, u32[]{:S(2)}) collective-permute-start(f32[168,128]{1,0:T(8,128)S(1)} %get-tuple-element.22), channel_id=1, source_target_pairs={{4,8},{12,16},{20,24},{28,0},{8,4},{16,12},{24,20},{0,28},{5,9},{1... | collective-permute-start | bytes 258056 | tf_op jit(solution)/shard_map/ppermute | solution.py:468

commit v4 on v3

--- a/solution.py
+++ b/solution.py
@@ -206,7 +206,7 @@
             fields[at] = fields[at] + gained[at]
 
 
-def near_kernel(members, parts, columns, around, chunks, mask, own, core_edge, inner, *rest):
+def near_kernel(members, parts, columns, flip, around, chunks, mask, own, core_edge, inner, *rest):
     mine_parts, other_parts = rest[: len(parts)], rest[len(parts) : 2 * len(parts)]
     fields, sides, gains, row_terms, lat_terms, packed, gained = rest[2 * len(parts) :]
     mine = [part.at[i] for part, size in zip(mine_parts, parts) for i in range(size)]
@@ -218,7 +218,7 @@
     place = rows_of(members)
     denominator = 1.0 / (members - 1)
     height = members + 8
-    owners = [col ^ j if around is None else (col + around[j] + columns) % columns for j in range(blocks)]
+    owners = [col ^ i if flip else (col + i + columns) % columns for i in around]
 
     lane = iota((1, LATS), 1)
     pad = (-blocks) % 16
@@ -450,11 +450,13 @@
     mine = kept + core_edge[:height]
     for bit in range(2, floors, 2):
         mine = mine + swapped(mine, "gz", bit)
-    if columns <= 2 * WINDOW + 1 and columns & (columns - 1) == 0:
-        around = None
+    flip = columns <= 2 * WINDOW + 1 and columns & (columns - 1) == 0
+    if flip:
         inner = swapped(jnp.concatenate([mine, inner]), "col", 1)
-        pair = jnp.stack([mine, inner[:height]])
-        gathered = [pair] + [swapped(pair, "col", bit) for bit in range(2, columns, 2)]
+        passed = [swapped(mine, "col", bit) for bit in range(2, columns, 2)]
+        near = jnp.stack([mine, inner[:height]] + passed)
+        gathered = [near, swapped(near[2:], "col", 1)]
+        around = [0, 1] + list(range(2, columns, 2)) + list(range(3, columns, 2))
     else:
         inner = swapped(inner, "col", 1)
         around = tuple(range(-WINDOW, WINDOW + 1)) if columns > 2 * WINDOW + 1 else tuple(range(columns))
@@ -477,7 +479,7 @@
     count = BATCHES * chunks
     limit = room(48 if several else 16)
     near, *terms = pl.pallas_call(
-        functools.partial(near_kernel, members, parts, columns, around, chunks),
+        functools.partial(near_kernel, members, parts, columns, flip, around, chunks),
         out_shape=[
             pltpu.VMEM((rows, members, LATS), F32),
             pltpu.VMEM((count, CHUNK, CHUNK), BF16),

time: 36.6 us -> 35 us (0.956)
  waiting for transfers between devices: 12.8 us -> 10.3 us
  starting transfers between devices: 14.1 us -> 15 us
    ppermute x10 -> x9, waiting for transfers between devices: 12.8 us -> 10.1 us  [swapped(): lax.ppermute(x, axis, [(i, i ^ bit) for i in range(lax.axis_size(axis))])]
    ppermute x10 -> x9, starting transfers between devices: 10.9 us -> 11.6 us  [swapped(): lax.ppermute(x, axis, [(i, i ^ bit) for i in range(lax.axis_size(axis))])]
  transfers between devices with their start and end apart: 12 -> 11, of which waited for: 5 -> 5; matrix products, arithmetic and copies ran while one was open for 0% -> 0% of each run, Pallas kernels for 13% -> 14%
where the time goes in v4:
time: 35 us; the launch traced here: 34.8 us
  starting transfers between devices  15 us (43%)
  waiting for transfers between devices  10.3 us (29%)
  Pallas kernels  9.39 us (27%)
    ppermute x9, starting transfers between devices, swapped(): lax.ppermute(x, axis, [(i, i ^ bit) for i in range(lax.axis_size(axis))])  11.6 us
    ppermute x9, waiting for transfers between devices, swapped(): lax.ppermute(x, axis, [(i, i ^ bit) for i in range(lax.axis_size(axis))])  10.1 us
    pallas_call x1, Pallas kernels, local(): pl.pallas_call(functools.partial(near_kernel, members, parts, columns, fl...  4.76 us
    pallas_call x1, Pallas kernels, local(): pl.pallas_call(functools.partial(far_kernel, members, columns, floors, ch...  2.76 us
    ppermute x1, starting transfers between devices, local(): outer = lax.ppermute(outer, 'col', ring + [(j, i) for i, j in ring])  2.67 us
    pallas_call x1, Pallas kernels, local(): pl.pallas_call(functools.partial(pick_kernel, members, columns), out_shap...  1.87 us
  transfers between devices with their start and end apart: 11, of which 5 were waited for; matrix products, arithmetic and copies ran while one was open for 0% of the time, Pallas kernels for 14%

profile of v4, /device:TPU:0, one launch (start us, length us, event | category | flops | bytes accessed | tf_op | source)
XLA Modules:
  0.0 34.8 jit_solution(6323085023348010130)
XLA Ops:
  0.0 0.0 copy-start
  0.0 1.9 %pick_priors.1 = (f32[88,128]{1,0:T(8,128)S(1)}, f32[728,128]{1,0:T(8,128)S(1)}, f32[640,128]{1,0:T(8,128)S(1)}, f32[168,128]{1,0:T(8,128)S(1)}, f32[168,128]{1,0:T(8,128)S(1)}, /*index=5*/f32[16,80,128]{2,1,0:T(8,128)S(1)}) custom-call(s32[1,2]{1,0:T(1,128)} %bitcast.25, s32[2,1,8]{2,1,0:T(1,128)} %bitcast.24, s32[2,1024]{1,0:T(2,128)} %site.1, ...), custom_call_target="tpu_custom_call" | custom-call | tf_op jit(solution)/shard_map/pick_priors/pallas_call | solution.py:433
  1.9 0.5 %collective-permute-start = (f32[728,128]{1,0:T(8,128)S(1)}, f32[728,128]{1,0:T(8,128)S(1)}, u32[]{:S(2)}, u32[]{:S(2)}) collective-permute-start(f32[728,128]{1,0:T(8,128)S(1)} %get-tuple-element.17), channel_id=1, source_target_pairs={{0,1},{1,0},{2,3},{3,2},{4,5},{5,4},{6,7},{7,6},{8,9},{9,8},{10,11... | collective-permute-start | bytes 1118216 | tf_op jit(solution)/shard_map/ppermute | solution.py:411
  2.4 1.3 %collective-permute-done.core_edge = f32[728,128]{1,0:T(8,128)S(1)} collective-permute-done((f32[728,128]{1,0:T(8,128)S(1)}, f32[728,128]{1,0:T(8,128)S(1)}, u32[]{:S(2)}, u32[]{:S(2)}) %collective-permute-start) | collective-permute-done | bytes 372768 | tf_op jit(solution)/shard_map/ppermute | solution.py:411
  3.7 2.9 %collective-permute-start.1 = (f32[88,128]{1,0:T(8,128)S(1)}, f32[88,128]{1,0:T(8,128)S(1)}, u32[]{:S(2)}, u32[]{:S(2)}) collective-permute-start(f32[88,128]{1,0:T(8,128)S(1)} %slice_add_fusion), channel_id=1, source_target_pairs={{0,2},{1,3},{2,0},{3,1},{4,6},{5,7},{6,4},{7,5},{8,10},{9,11},{10,... | collective-permute-start | bytes 135176 | tf_op jit(solution)/shard_map/ppermute | solution.py:411
  6.7 2.0 %collective-permute-done.1 = f32[88,128]{1,0:T(8,128)S(1)} collective-permute-done((f32[88,128]{1,0:T(8,128)S(1)}, f32[88,128]{1,0:T(8,128)S(1)}, u32[]{:S(2)}, u32[]{:S(2)}) %collective-permute-start.1) | collective-permute-done | bytes 45088 | tf_op jit(solution)/shard_map/ppermute | solution.py:411
  8.7 3.2 %collective-permute-start.4 = (f32[88,128]{1,0:T(8,128)S(1)}, f32[88,128]{1,0:T(8,128)S(1)}, u32[]{:S(2)}, u32[]{:S(2)}) collective-permute-start(f32[88,128]{1,0:T(8,128)S(1)} %get-tuple-element.28), channel_id=1, source_target_pairs={{0,16},{4,20},{8,24},{12,28},{16,0},{20,4},{24,8},{28,12},{1,17},{... | collective-permute-start | bytes 135176 | tf_op jit(solution)/shard_map/ppermute | solution.py:411
  11.9 1.6 %collective-permute-start.3 = (f32[88,128]{1,0:T(8,128)S(1)}, f32[88,128]{1,0:T(8,128)S(1)}, u32[]{:S(2)}, u32[]{:S(2)}) collective-permute-start(f32[88,128]{1,0:T(8,128)S(1)} %get-tuple-element.28), channel_id=1, source_target_pairs={{0,8},{4,12},{8,0},{12,4},{16,24},{20,28},{24,16},{28,20},{1,9},{5... | collective-permute-start | bytes 135176 | tf_op jit(solution)/shard_map/ppermute | solution.py:411
  13.4 0.0 collective-permute-start.5
  13.5 1.8 %collective-permute-start.2 = (f32[256,128]{1,0:T(8,128)S(1)}, f32[256,128]{1,0:T(8,128)S(1)}, u32[]{:S(2)}, u32[]{:S(2)}) collective-permute-start(f32[256,128]{1,0:T(8,128)S(1)} %pad_maximum_fusion.1), channel_id=1, source_target_pairs={{0,4},{4,0},{8,12},{12,8},{16,20},{20,16},{24,28},{28,24},{1,5},{5... | collective-permute-start | bytes 393224 | tf_op jit(solution)/shard_map/ppermute | solution.py:411
  15.2 0.7 %collective-permute-start.9 = (f32[640,128]{1,0:T(8,128)S(1)}, f32[640,128]{1,0:T(8,128)S(1)}, u32[]{:S(2)}, u32[]{:S(2)}) collective-permute-start(f32[640,128]{1,0:T(8,128)S(1)} %get-tuple-element.21), channel_id=1, source_target_pairs={{1,2},{2,1},{0,0},{3,3},{5,6},{6,5},{4,4},{7,7},{9,10},{10,9},{8,8... | collective-permute-start | bytes 983048 | tf_op jit(solution)/shard_map/ppermute | solution.py:468
  15.9 0.0 collective-permute-done.4
  15.9 0.0 collective-permute-done.3
  15.9 3.3 %collective-permute-done.5 = f32[88,128]{1,0:T(8,128)S(1)} collective-permute-done((f32[88,128]{1,0:T(8,128)S(1)}, f32[88,128]{1,0:T(8,128)S(1)}, u32[]{:S(2)}, u32[]{:S(2)}) %collective-permute-start.5) | collective-permute-done | bytes 45088 | tf_op jit(solution)/shard_map/ppermute | solution.py:411
  19.3 0.0 copy-start.1
  19.3 1.6 %collective-permute-start.6 = (f32[3,88,128]{2,1,0:T(8,128)S(1)}, f32[3,88,128]{2,1,0:T(8,128)S(1)}, u32[]{:S(2)}, u32[]{:S(2)}) collective-permute-start(f32[3,88,128]{2,1,0:T(8,128)S(1)} %pad_maximum_fusion), channel_id=1, source_target_pairs={{0,4},{4,0},{8,12},{12,8},{16,20},{20,16},{24,28},{28,24},{1,5},{5... | collective-permute-start | bytes 405512 | tf_op jit(solution)/shard_map/ppermute | solution.py:411
  20.9 0.0 collective-permute-done.2.inner
  20.9 0.1 collective-permute-start.7
  21.0 3.4 %collective-permute-done.6.rest_1_ = f32[3,88,128]{2,1,0:T(8,128)S(1)} collective-permute-done((f32[3,88,128]{2,1,0:T(8,128)S(1)}, f32[3,88,128]{2,1,0:T(8,128)S(1)}, u32[]{:S(2)}, u32[]{:S(2)}) %collective-permute-start.6) | collective-permute-done | bytes 135200 | tf_op jit(solution)/shard_map/ppermute | solution.py:411
  24.4 0.0 collective-permute-start.8
  24.4 2.7 %collective-permute-start.10 = (f32[168,128]{1,0:T(8,128)S(1)}, f32[168,128]{1,0:T(8,128)S(1)}, u32[]{:S(2)}, u32[]{:S(2)}) collective-permute-start(f32[168,128]{1,0:T(8,128)S(1)} %get-tuple-element.22), channel_id=1, source_target_pairs={{4,8},{12,16},{20,24},{28,0},{8,4},{16,12},{24,20},{0,28},{5,9},{1... | collective-permute-start | bytes 258056 | tf_op jit(solution)/shard_map/ppermute | solution.py:470
  27.1 0.0 collective-permute-done.8.rest_3_
  27.1 0.0 collective-permute-done.7.rest_2_
  27.1 0.0 copy-done
  27.1 4.8 %analyse_near.1 = (f32[28,80,128]{2,1,0:T(8,128)S(1)}, bf16[2,256,256]{2,1,0:T(8,128)(2,1)S(1)}, bf16[2,160,256]{2,1,0:T(8,128)(2,1)S(1)}, f32[2,256,128]{2,1,0:T(8,128)S(1)}, f32[2,256,128]{2,1,0:T(8,128)S(1)}) custom-call(s32[8,128]{1,0:T(8,128)S(1)} %copy-done, f32[16,80,128]{2,1,0:T(8,128)S(1)} %get-tuple-element.16.own, ...), custom_call_target="tpu_custom_call" | custom-call | tf_op jit(solution)/shard_map/analyse_near/pallas_call | solution.py:481
  31.9 0.2 collective-permute-done.10.outer
  32.0 0.0 collective-permute-done.9.y_edge
  32.0 0.0 copy-done.1
  32.0 2.8 %analyse_far_and_step.1 = f32[1280,128]{1,0:T(8,128)} custom-call(s32[8,128]{1,0:T(8,128)S(1)} %copy-done, f32[16,128]{1,0:T(8,128)S(1)} %bitcast.19, f32[28,80,128]{2,1,0:T(8,128)S(1)} %get-tuple-element.20.near, f32[640,128]{1,0:T(8,128)S(1)} %collective-permute-done.9.y_edge, f32[168,128]{1,0:T(8,128)S(1)} %collective-permute-done.10.outer, ...), custom_call_target="tpu_custom_call" | custom-call | tf_op jit(solution)/shard_map/analyse_far_and_step/pallas_call | solution.py:500
  (8 shorter events, 0.1 us)
Async XLA Ops:
  0.0 27.1 %copy-start = (s32[8,128]{1,0:T(8,128)S(1)}, s32[8,128]{1,0:T(8,128)}, u32[]{:S(2)}) copy-start(s32[8,128]{1,0:T(8,128)} %mask.5) | copy-start | bytes 12292
  1.9 1.8 %collective-permute-start = (f32[728,128]{1,0:T(8,128)S(1)}, f32[728,128]{1,0:T(8,128)S(1)}, u32[]{:S(2)}, u32[]{:S(2)}) collective-permute-start(f32[728,128]{1,0:T(8,128)S(1)} %get-tuple-element.17), channel_id=1, source_target_pairs={{0,1},{1,0},{2,3},{3,2},{4,5},{5,4},{6,7},{7,6},{8,9},{9,8},{10,11... | collective-permute-start | bytes 1118216 | tf_op jit(solution)/shard_map/ppermute | solution.py:411
  3.7 5.0 %collective-permute-start.1 = (f32[88,128]{1,0:T(8,128)S(1)}, f32[88,128]{1,0:T(8,128)S(1)}, u32[]{:S(2)}, u32[]{:S(2)}) collective-permute-start(f32[88,128]{1,0:T(8,128)S(1)} %slice_add_fusion), channel_id=1, source_target_pairs={{0,2},{1,3},{2,0},{3,1},{4,6},{5,7},{6,4},{7,5},{8,10},{9,11},{10,... | collective-permute-start | bytes 135176 | tf_op jit(solution)/shard_map/ppermute | solution.py:411
  8.7 7.2 %collective-permute-start.4 = (f32[88,128]{1,0:T(8,128)S(1)}, f32[88,128]{1,0:T(8,128)S(1)}, u32[]{:S(2)}, u32[]{:S(2)}) collective-permute-start(f32[88,128]{1,0:T(8,128)S(1)} %get-tuple-element.28), channel_id=1, source_target_pairs={{0,16},{4,20},{8,24},{12,28},{16,0},{20,4},{24,8},{28,12},{1,17},{... | collective-permute-start | bytes 135176 | tf_op jit(solution)/shard_map/ppermute | solution.py:411
  11.9 4.1 %collective-permute-start.3 = (f32[88,128]{1,0:T(8,128)S(1)}, f32[88,128]{1,0:T(8,128)S(1)}, u32[]{:S(2)}, u32[]{:S(2)}) collective-permute-start(f32[88,128]{1,0:T(8,128)S(1)} %get-tuple-element.28), channel_id=1, source_target_pairs={{0,8},{4,12},{8,0},{12,4},{16,24},{20,28},{24,16},{28,20},{1,9},{5... | collective-permute-start | bytes 135176 | tf_op jit(solution)/shard_map/ppermute | solution.py:411
  13.4 5.8 %collective-permute-start.5 = (f32[88,128]{1,0:T(8,128)S(1)}, f32[88,128]{1,0:T(8,128)S(1)}, u32[]{:S(2)}, u32[]{:S(2)}) collective-permute-start(f32[88,128]{1,0:T(8,128)S(1)} %get-tuple-element.28), channel_id=1, source_target_pairs={{0,24},{4,28},{8,16},{12,20},{16,8},{20,12},{24,0},{28,4},{1,25},{... | collective-permute-start | bytes 135176 | tf_op jit(solution)/shard_map/ppermute | solution.py:411
  13.5 7.4 %collective-permute-start.2 = (f32[256,128]{1,0:T(8,128)S(1)}, f32[256,128]{1,0:T(8,128)S(1)}, u32[]{:S(2)}, u32[]{:S(2)}) collective-permute-start(f32[256,128]{1,0:T(8,128)S(1)} %pad_maximum_fusion.1), channel_id=1, source_target_pairs={{0,4},{4,0},{8,12},{12,8},{16,20},{20,16},{24,28},{28,24},{1,5},{5... | collective-permute-start | bytes 393224 | tf_op jit(solution)/shard_map/ppermute | solution.py:411
  15.2 16.8 %collective-permute-start.9 = (f32[640,128]{1,0:T(8,128)S(1)}, f32[640,128]{1,0:T(8,128)S(1)}, u32[]{:S(2)}, u32[]{:S(2)}) collective-permute-start(f32[640,128]{1,0:T(8,128)S(1)} %get-tuple-element.21), channel_id=1, source_target_pairs={{1,2},{2,1},{0,0},{3,3},{5,6},{6,5},{4,4},{7,7},{9,10},{10,9},{8,8... | collective-permute-start | bytes 983048 | tf_op jit(solution)/shard_map/ppermute | solution.py:468
  19.3 12.7 %copy-start.1 = (f32[2,8,128]{2,1,0:T(8,128)S(1)}, f32[2,8,128]{2,1,0:T(8,128)}, u32[]{:S(2)}) copy-start(f32[2,8,128]{2,1,0:T(8,128)} %param.15) | copy-start | bytes 24580
  19.3 5.1 %collective-permute-start.6 = (f32[3,88,128]{2,1,0:T(8,128)S(1)}, f32[3,88,128]{2,1,0:T(8,128)S(1)}, u32[]{:S(2)}, u32[]{:S(2)}) collective-permute-start(f32[3,88,128]{2,1,0:T(8,128)S(1)} %pad_maximum_fusion), channel_id=1, source_target_pairs={{0,4},{4,0},{8,12},{12,8},{16,20},{20,16},{24,28},{28,24},{1,5},{5... | collective-permute-start | bytes 405512 | tf_op jit(solution)/shard_map/ppermute | solution.py:411
  20.9 6.2 %collective-permute-start.7 = (f32[5,88,128]{2,1,0:T(8,128)S(1)}, f32[5,88,128]{2,1,0:T(8,128)S(1)}, u32[]{:S(2)}, u32[]{:S(2)}) collective-permute-start(f32[5,88,128]{2,1,0:T(8,128)S(1)} %constant_dynamic-update-slice_fusion.rest_0_), channel_id=1, source_target_pairs={{0,1},{1,0},{2,3},{3,2},{4,5},{5,4},{6,7},{7,6},{8,9},{9,8},{10,11... | collective-permute-start | bytes 675848 | tf_op jit(solution)/shard_map/ppermute | solution.py:411
  24.4 2.7 %collective-permute-start.8 = (f32[3,88,128]{2,1,0:T(8,128)S(1)}, f32[3,88,128]{2,1,0:T(8,128)S(1)}, u32[]{:S(2)}, u32[]{:S(2)}) collective-permute-start(f32[3,88,128]{2,1,0:T(8,128)S(1)} %collective-permute-done.6.rest_1_), channel_id=1, source_target_pairs={{0,1},{1,0},{2,3},{3,2},{4,5},{5,4},{6,7},{7,6},{8,9},{9,8},{10,11... | collective-permute-start | bytes 405512 | tf_op jit(solution)/shard_map/ppermute | solution.py:411
  24.4 7.6 %collective-permute-start.10 = (f32[168,128]{1,0:T(8,128)S(1)}, f32[168,128]{1,0:T(8,128)S(1)}, u32[]{:S(2)}, u32[]{:S(2)}) collective-permute-start(f32[168,128]{1,0:T(8,128)S(1)} %get-tuple-element.22), channel_id=1, source_target_pairs={{4,8},{12,16},{20,24},{28,0},{8,4},{16,12},{24,20},{0,28},{5,9},{1... | collective-permute-start | bytes 258056 | tf_op jit(solution)/shard_map/ppermute | solution.py:470

commit v5 on v4

--- a/solution.py
+++ b/solution.py
@@ -67,7 +67,7 @@
     return lax.axis_index("col").astype(jnp.int32), lax.axis_index("gz").astype(jnp.int32)
 
 
-def pick_kernel(members, columns, count, linked, site, value, noise, mask, state, kept, core_send, y_send, inner, outer, rows):
+def pick_kernel(members, columns, count, linked, site, value, noise, mask, state, kept, given):
     col, gz = position()
     core = gz % 2
     lane = iota((1, CAP), 1)
@@ -85,7 +85,6 @@
         left = []
         for r in (2 * pair, 2 * pair + 1):
             x = state[pl.ds(r, members, stride=ROWS), :]
-            rows[r] = x
             high = x.astype(BF16)
             rest = x - high.astype(F32)
             middle = rest.astype(BF16)
@@ -96,7 +95,6 @@
         hit = jnp.where(cell + pair * 2 * LATS == wanted, 1.0, 0.0).astype(BF16)
         total = total + dot(jnp.concatenate(left, 1), hit)
     m = members
-    height = m + 8
     picked = (total[:m] + total[m + 16 : 2 * m + 16]) + total[2 * m + 16 :]
     first = jnp.where(gz == 0, 1.0, 0.0)
     for b in range(BATCHES):
@@ -121,19 +119,25 @@
 
         @pl.when(core != b)
         def _():
-            core_send[:height, :] = block
-
+            given[...] = block
+
+
+def edges_kernel(members, mask, state, core_send, y_send, inner, outer, rows):
+    col, gz = position()
+    core = gz % 2
+    ocean = mask[...].astype(F32)
+    for r in range(ROWS):
+        rows[r] = state[pl.ds(r, members, stride=ROWS), :]
     for member in range(members):
-        up = state[pl.ds(pl.multiple_of(member * ROWS + (1 - core) * LONS, LONS), LONS), :]
-        core_send[height + member * LONS : height + (member + 1) * LONS, :] = up
-        down = state[pl.ds(pl.multiple_of(member * ROWS + core * LONS, LONS), LONS), :]
-        y_send[member * LONS : (member + 1) * LONS, :] = down
+        to = slice(member * LONS, (member + 1) * LONS)
+        core_send[to, :] = state[pl.ds(pl.multiple_of(member * ROWS + (1 - core) * LONS, LONS), LONS), :]
+        y_send[to, :] = state[pl.ds(pl.multiple_of(member * ROWS + core * LONS, LONS), LONS), :]
     even = col % 2 == 0
     for lev in range(LEVS):
-        west = state[pl.ds(lev * LONS, members, stride=ROWS), :]
-        east = state[pl.ds(lev * LONS + LONS - 1, members, stride=ROWS), :]
-        inner[lev * members : (lev + 1) * members, :] = jnp.where(even, east, west)
-        outer[lev * members : (lev + 1) * members, :] = jnp.where(even, west, east)
+        west, east = rows[lev * LONS], rows[lev * LONS + LONS - 1]
+        to = slice(lev * members, (lev + 1) * members)
+        inner[to, :] = jnp.where(even, east, west)
+        outer[to, :] = jnp.where(even, west, east)
     west = jnp.broadcast_to(ocean[:1], (8, LATS))
     east = jnp.broadcast_to(ocean[LONS - 1 :], (8, LATS))
     inner[LEVS * members :, :] = jnp.where(even, east, west)
@@ -171,37 +175,57 @@
     return jnp.concatenate([high, low, high, jnp.zeros((16, x.shape[1]), BF16)], 0)
 
 
+def products(covariance, local, gains):
+    members = gains.shape[0] // 2
+    high, low = halves(covariance * local)
+    return dot(gains, high), dot(gains[:members], low)
+
+
+def added(first, second):
+    members = second.shape[0]
+    return (first[:members] + first[members:]) + second
+
+
 def increment(x, sides, gains, local):
-    members = x.shape[0]
-    weighted = dot(sides, centred_parts(x)) * local
-    high, low = halves(weighted)
-    first = dot(gains, high)
-    return (first[:members] + first[members:]) + dot(gains[:members], low)
-
-
-def move_rows(fields, gained, first, last, ocean, terms, b, chunks):
+    return added(*products(dot(sides, centred_parts(x)), local, gains))
+
+
+def move_pairs(fields, into, first, last, ocean, terms, steps, meanwhile=None):
     sides, gains, row_part, lat_part = terms
-
-    def chunk(k):
-        t = b * chunks + k
-        for r in range(first, last, 2):
-            at = r - first
-            x = jnp.concatenate([fields[at], fields[at + 1]], 1)
-            columns = [ROW_COLUMN + r + h for h in range(2)]
-            tapers = [lat_part[t] * row_part[t, :, c : c + 1] for c in columns]
-            moved = increment(x, sides[t], gains[t], jnp.concatenate(tapers, 1))
-            moved = moved * jnp.concatenate([ocean[at], ocean[at + 1]], 1)
-            for h in range(2):
-                piece = slice(h * LATS, (h + 1) * LATS)
-                if chunks == 1:
-                    fields[at + h] = x[:, piece] + moved[:, piece]
-                else:
-                    gained[at + h] = gained[at + h] + moved[:, piece]
-
-    if chunks > 1:
+    ahead = []
+
+    def finish():
+        t, at, x, covariance = ahead.pop(0)
+        columns = [ROW_COLUMN + first + at + h for h in range(2)]
+        tapers = [lat_part[t] * row_part[t, :, c : c + 1] for c in columns]
+        moved = added(*products(covariance, jnp.concatenate(tapers, 1), gains[t]))
+        moved = moved * jnp.concatenate([ocean[at], ocean[at + 1]], 1)
+        for h in range(2):
+            piece = slice(h * LATS, (h + 1) * LATS)
+            if into is fields:
+                fields[at + h] = x[:, piece] + moved[:, piece]
+            else:
+                into[at + h] = into[at + h] + moved[:, piece]
+
+    for i, (t, at) in enumerate([(t, at) for t in steps for at in range(0, last - first, 2)]):
+        if meanwhile is not None and i == meanwhile[0]:
+            meanwhile[1]()
+        x = jnp.concatenate([fields[at], fields[at + 1]], 1)
+        ahead.append((t, at, x, dot(sides[t], centred_parts(x))))
+        if len(ahead) > 1:
+            finish()
+    finish()
+
+
+def move_rows(fields, gained, first, last, ocean, terms, chunks, meanwhile=None):
+    if chunks == 1:
+        move_pairs(fields, fields, first, last, ocean, terms, range(BATCHES), meanwhile)
+        return
+    if meanwhile is not None:
+        meanwhile[1]()
+    for b in range(BATCHES):
         gained[...] = jnp.zeros_like(gained)
-    for_each(chunks, chunk)
-    if chunks > 1:
+        for_each(chunks, lambda k: move_pairs(fields, gained, first, last, ocean, terms, [b * chunks + k]))
         for at in range(last - first):
             fields[at] = fields[at] + gained[at]
 
@@ -246,7 +270,7 @@
     for r in range(ROWS):
         fields[r] = own[r]
     for lon in range(LONS):
-        fields[CORE_ROW + lon] = core_edge[pl.ds(height + lon, members, stride=LONS), :]
+        fields[CORE_ROW + lon] = core_edge[pl.ds(lon, members, stride=LONS), :]
     for lev in range(LEVS):
         at = inner_start + lev * members
         fields[INNER_ROW + lev] = inner[at : at + members, :]
@@ -359,9 +383,8 @@
 
     terms = (sides, gains, row_terms, lat_terms)
     for_each(chunks, first_terms)
-    for_each(chunks, second_terms)
-    for b in range(BATCHES):
-        move_rows(fields, gained, 0, Y_ROW, ocean, terms, b, chunks)
+    meanwhile = (6, lambda: for_each(chunks, second_terms))
+    move_rows(fields, gained, 0, Y_ROW, ocean, terms, chunks, meanwhile)
 
 
 def far_kernel(
@@ -382,8 +405,7 @@
     ocean = [wet[lon : lon + 1] for lon in range(LONS)]
     edge = members * LEVS
     terms = (sides, gains, row_terms, lat_terms)
-    for b in range(BATCHES):
-        move_rows(fields, gained, Y_ROW, EXT_ROWS, ocean + [outer[edge : edge + 1, :]] * LEVS, terms, b, chunks)
+    move_rows(fields, gained, Y_ROW, EXT_ROWS, ocean + [outer[edge : edge + 1, :]] * LEVS, terms, chunks)
 
     for r in range(ROWS):
         lev, lon = r // LONS, r % LONS
@@ -430,11 +452,11 @@
     def like(*lengths):
         return [pltpu.VMEM((length, LATS), F32) for length in lengths]
 
-    kept, core_send, y_send, inner, outer, own = pl.pallas_call(
+    kept, given = pl.pallas_call(
         functools.partial(pick_kernel, members, columns),
-        out_shape=like(height, height + level, level, edge, edge) + [pltpu.VMEM((ROWS, members, LATS), F32)],
+        out_shape=like(height, height),
         in_specs=[smem] + [vmem] * 6,
-        out_specs=[vmem] * 6,
+        out_specs=[vmem] * 2,
         name="pick_priors",
     )(
         obs_count.reshape(1, BATCHES),
@@ -446,17 +468,26 @@
         flat,
     )
 
+    mine = kept + swapped(given, "gz", 1)
+    core_send, y_send, inner, outer, own = pl.pallas_call(
+        functools.partial(edges_kernel, members),
+        out_shape=like(level, level, edge, edge) + [pltpu.VMEM((ROWS, members, LATS), F32)],
+        in_specs=[vmem] * 2,
+        out_specs=[vmem] * 5,
+        cost_estimate=pl.CostEstimate(flops=0, bytes_accessed=1 << 22, transcendentals=0),
+        name="copy_edges",
+    )(ocean_mask, flat)
     core_edge = swapped(core_send, "gz", 1)
-    mine = kept + core_edge[:height]
     for bit in range(2, floors, 2):
         mine = mine + swapped(mine, "gz", bit)
     flip = columns <= 2 * WINDOW + 1 and columns & (columns - 1) == 0
     if flip:
         inner = swapped(jnp.concatenate([mine, inner]), "col", 1)
-        passed = [swapped(mine, "col", bit) for bit in range(2, columns, 2)]
+        bits = list(range(2, columns, 2))
+        passed = [swapped(mine, "col", bit) for bit in bits]
         near = jnp.stack([mine, inner[:height]] + passed)
         gathered = [near, swapped(near[2:], "col", 1)]
-        around = [0, 1] + list(range(2, columns, 2)) + list(range(3, columns, 2))
+        around = [0, 1] + bits + [bit + 1 for bit in bits]
     else:
         inner = swapped(inner, "col", 1)
         around = tuple(range(-WINDOW, WINDOW + 1)) if columns > 2 * WINDOW + 1 else tuple(range(columns))

time: 35 us -> 34.5 us (0.986)
  waiting for transfers between devices: 10.3 us -> 8.97 us
  Pallas kernels: 9.39 us -> 10.2 us
    ppermute x9 -> x10, waiting for transfers between devices: 10.1 us -> 8.3 us  [swapped(): lax.ppermute(x, axis, [(i, i ^ bit) for i in range(lax.axis_size(axis))])]
    pallas_call x0 -> x1, Pallas kernels: none -> 1.37 us  [local(): pl.pallas_call(functools.partial(edges_kernel, members), out_shape=like(l...]
    pallas_call x1, Pallas kernels: 4.76 us -> 4.26 us  [local(): pl.pallas_call(functools.partial(near_kernel, members, parts, columns, fl...]
    ppermute x1, waiting for transfers between devices: 0.19 us -> 0.67 us  [local(): outer = lax.ppermute(outer, 'col', ring + [(j, i) for i, j in ring])]
    ppermute x9 -> x10, starting transfers between devices: 11.6 us -> 11.6 us  [swapped(): lax.ppermute(x, axis, [(i, i ^ bit) for i in range(lax.axis_size(axis))])]
  transfers between devices with their start and end apart: 11 -> 12, of which waited for: 5 -> 5; matrix products, arithmetic and copies ran while one was open for 0% -> 0% of each run, Pallas kernels for 14% -> 16%
where the time goes in v5:
time: 34.5 us; the launch traced here: 34.3 us
  starting transfers between devices  14.9 us (43%)
  Pallas kernels  10.2 us (30%)
  waiting for transfers between devices  8.97 us (26%)
    ppermute x10, starting transfers between devices, swapped(): lax.ppermute(x, axis, [(i, i ^ bit) for i in range(lax.axis_size(axis))])  11.6 us
    ppermute x10, waiting for transfers between devices, swapped(): lax.ppermute(x, axis, [(i, i ^ bit) for i in range(lax.axis_size(axis))])  8.3 us
    pallas_call x1, Pallas kernels, local(): pl.pallas_call(functools.partial(near_kernel, members, parts, columns, fl...  4.26 us
    pallas_call x1, Pallas kernels, local(): pl.pallas_call(functools.partial(far_kernel, members, columns, floors, ch...  2.85 us
    ppermute x1, starting transfers between devices, local(): outer = lax.ppermute(outer, 'col', ring + [(j, i) for i, j in ring])  2.68 us
    pallas_call x1, Pallas kernels, local(): pl.pallas_call(functools.partial(pick_kernel, members, columns), out_shap...  1.75 us
    pallas_call x1, Pallas kernels, local(): pl.pallas_call(functools.partial(edges_kernel, members), out_shape=like(l...  1.37 us
  transfers between devices with their start and end apart: 12, of which 5 were waited for; matrix products, arithmetic and copies ran while one was open for 0% of the time, Pallas kernels for 16%

profile of v5, /device:TPU:0, one launch (start us, length us, event | category | flops | bytes accessed | tf_op | source)
XLA Modules:
  0.0 34.3 jit_solution(7690147734480514425)
XLA Ops:
  0.0 0.0 copy-start
  0.0 1.8 %pick_priors.1 = (f32[88,128]{1,0:T(8,128)S(1)}, f32[88,128]{1,0:T(8,128)S(1)}) custom-call(s32[1,2]{1,0:T(1,128)} %bitcast.26, s32[2,1,8]{2,1,0:T(1,128)} %bitcast.25, s32[2,1024]{1,0:T(2,128)} %site.1, f32[2,128]{1,0:T(2,128)} %value.1, f32[2,128]{1,0:T(2,128)} %noise.1, s32[8,128]{1,0:T(8,128)} %mask.7, f32[1280,128]{1,0:T(8,128)} %bitcast.20), custom_call_target="tpu_custom_call" | custom-call | tf_op jit(solution)/shard_map/pick_priors/pallas_call | solution.py:455
  1.8 0.5 %collective-permute-start.1 = (f32[88,128]{1,0:T(8,128)S(1)}, f32[88,128]{1,0:T(8,128)S(1)}, u32[]{:S(2)}, u32[]{:S(2)}) collective-permute-start(f32[88,128]{1,0:T(8,128)S(1)} %get-tuple-element.20), channel_id=1, source_target_pairs={{0,1},{1,0},{2,3},{3,2},{4,5},{5,4},{6,7},{7,6},{8,9},{9,8},{10,11... | collective-permute-start | bytes 135176 | tf_op jit(solution)/shard_map/ppermute | solution.py:433
  2.3 0.9 %collective-permute-done.1 = f32[88,128]{1,0:T(8,128)S(1)} collective-permute-done((f32[88,128]{1,0:T(8,128)S(1)}, f32[88,128]{1,0:T(8,128)S(1)}, u32[]{:S(2)}, u32[]{:S(2)}) %collective-permute-start.1) | collective-permute-done | bytes 45088 | tf_op jit(solution)/shard_map/ppermute | solution.py:433
  3.2 2.9 %collective-permute-start.2 = (f32[88,128]{1,0:T(8,128)S(1)}, f32[88,128]{1,0:T(8,128)S(1)}, u32[]{:S(2)}, u32[]{:S(2)}) collective-permute-start(f32[88,128]{1,0:T(8,128)S(1)} %add.6), channel_id=1, source_target_pairs={{0,2},{1,3},{2,0},{3,1},{4,6},{5,7},{6,4},{7,5},{8,10},{9,11},{10,... | collective-permute-start | bytes 135176 | tf_op jit(solution)/shard_map/ppermute | solution.py:433
  6.1 1.4 %copy_edges.1 = (f32[640,128]{1,0:T(8,128)S(1)}, f32[640,128]{1,0:T(8,128)S(1)}, f32[168,128]{1,0:T(8,128)S(1)}, f32[168,128]{1,0:T(8,128)S(1)}, f32[16,80,128]{2,1,0:T(8,128)S(1)}) custom-call(s32[8,128]{1,0:T(8,128)} %mask.7, f32[1280,128]{1,0:T(8,128)} %bitcast.21), custom_call_target="tpu_custom_call" | custom-call | bytes 4194304 | tf_op jit(solution)/shard_map/copy_edges/pallas_call | solution.py:472
  7.5 0.7 %collective-permute-done.2 = f32[88,128]{1,0:T(8,128)S(1)} collective-permute-done((f32[88,128]{1,0:T(8,128)S(1)}, f32[88,128]{1,0:T(8,128)S(1)}, u32[]{:S(2)}, u32[]{:S(2)}) %collective-permute-start.2) | collective-permute-done | bytes 45088 | tf_op jit(solution)/shard_map/ppermute | solution.py:433
  8.1 3.2 %collective-permute-start.5 = (f32[88,128]{1,0:T(8,128)S(1)}, f32[88,128]{1,0:T(8,128)S(1)}, u32[]{:S(2)}, u32[]{:S(2)}) collective-permute-start(f32[88,128]{1,0:T(8,128)S(1)} %get-tuple-element.30), channel_id=1, source_target_pairs={{0,16},{4,20},{8,24},{12,28},{16,0},{20,4},{24,8},{28,12},{1,17},{... | collective-permute-start | bytes 135176 | tf_op jit(solution)/shard_map/ppermute | solution.py:433
  11.3 1.6 %collective-permute-start.4 = (f32[88,128]{1,0:T(8,128)S(1)}, f32[88,128]{1,0:T(8,128)S(1)}, u32[]{:S(2)}, u32[]{:S(2)}) collective-permute-start(f32[88,128]{1,0:T(8,128)S(1)} %get-tuple-element.30), channel_id=1, source_target_pairs={{0,8},{4,12},{8,0},{12,4},{16,24},{20,28},{24,16},{28,20},{1,9},{5... | collective-permute-start | bytes 135176 | tf_op jit(solution)/shard_map/ppermute | solution.py:433
  12.9 0.0 collective-permute-start.6
  12.9 1.8 %collective-permute-start.3 = (f32[256,128]{1,0:T(8,128)S(1)}, f32[256,128]{1,0:T(8,128)S(1)}, u32[]{:S(2)}, u32[]{:S(2)}) collective-permute-start(f32[256,128]{1,0:T(8,128)S(1)} %pad_maximum_fusion.1), channel_id=1, source_target_pairs={{0,4},{4,0},{8,12},{12,8},{16,20},{20,16},{24,28},{28,24},{1,5},{5... | collective-permute-start | bytes 393224 | tf_op jit(solution)/shard_map/ppermute | solution.py:433
  14.6 0.0 collective-permute-start
  14.7 0.0 collective-permute-done.5
  14.7 0.7 %collective-permute-start.10 = (f32[640,128]{1,0:T(8,128)S(1)}, f32[640,128]{1,0:T(8,128)S(1)}, u32[]{:S(2)}, u32[]{:S(2)}) collective-permute-start(f32[640,128]{1,0:T(8,128)S(1)} %get-tuple-element.23), channel_id=1, source_target_pairs={{1,2},{2,1},{0,0},{3,3},{5,6},{6,5},{4,4},{7,7},{9,10},{10,9},{8,8... | collective-permute-start | bytes 983048 | tf_op jit(solution)/shard_map/ppermute | solution.py:499
  15.3 0.0 collective-permute-done.4
  15.3 3.4 %collective-permute-done.6 = f32[88,128]{1,0:T(8,128)S(1)} collective-permute-done((f32[88,128]{1,0:T(8,128)S(1)}, f32[88,128]{1,0:T(8,128)S(1)}, u32[]{:S(2)}, u32[]{:S(2)}) %collective-permute-start.6) | collective-permute-done | bytes 45088 | tf_op jit(solution)/shard_map/ppermute | solution.py:433
  18.7 0.0 copy-start.1
  18.7 1.6 %collective-permute-start.7 = (f32[3,88,128]{2,1,0:T(8,128)S(1)}, f32[3,88,128]{2,1,0:T(8,128)S(1)}, u32[]{:S(2)}, u32[]{:S(2)}) collective-permute-start(f32[3,88,128]{2,1,0:T(8,128)S(1)} %pad_maximum_fusion), channel_id=1, source_target_pairs={{0,4},{4,0},{8,12},{12,8},{16,20},{20,16},{24,28},{28,24},{1,5},{5... | collective-permute-start | bytes 405512 | tf_op jit(solution)/shard_map/ppermute | solution.py:433
  20.3 0.0 collective-permute-done.3.inner
  20.3 0.1 collective-permute-start.8
  20.4 3.4 %collective-permute-done.7.rest_1_ = f32[3,88,128]{2,1,0:T(8,128)S(1)} collective-permute-done((f32[3,88,128]{2,1,0:T(8,128)S(1)}, f32[3,88,128]{2,1,0:T(8,128)S(1)}, u32[]{:S(2)}, u32[]{:S(2)}) %collective-permute-start.7) | collective-permute-done | bytes 135200 | tf_op jit(solution)/shard_map/ppermute | solution.py:433
  23.8 0.0 collective-permute-start.9
  23.8 2.7 %collective-permute-start.11 = (f32[168,128]{1,0:T(8,128)S(1)}, f32[168,128]{1,0:T(8,128)S(1)}, u32[]{:S(2)}, u32[]{:S(2)}) collective-permute-start(f32[168,128]{1,0:T(8,128)S(1)} %get-tuple-element.24), channel_id=1, source_target_pairs={{4,8},{12,16},{20,24},{28,0},{8,4},{16,12},{24,20},{0,28},{5,9},{1... | collective-permute-start | bytes 258056 | tf_op jit(solution)/shard_map/ppermute | solution.py:501
  26.5 0.0 collective-permute-done.core_edge
  26.5 0.0 collective-permute-done.9.rest_3_
  26.5 0.0 collective-permute-done.8.rest_2_
  26.5 0.0 copy-done
  26.5 4.3 %analyse_near.1 = (f32[28,80,128]{2,1,0:T(8,128)S(1)}, bf16[2,256,256]{2,1,0:T(8,128)(2,1)S(1)}, bf16[2,160,256]{2,1,0:T(8,128)(2,1)S(1)}, f32[2,256,128]{2,1,0:T(8,128)S(1)}, f32[2,256,128]{2,1,0:T(8,128)S(1)}) custom-call(s32[8,128]{1,0:T(8,128)S(1)} %copy-done, f32[16,80,128]{2,1,0:T(8,128)S(1)} %get-tuple-element.17.own, ...), custom_call_target="tpu_custom_call" | custom-call | tf_op jit(solution)/shard_map/analyse_near/pallas_call | solution.py:512
  30.8 0.7 %collective-permute-done.11.outer = f32[168,128]{1,0:T(8,128)S(1)} collective-permute-done((f32[168,128]{1,0:T(8,128)S(1)}, f32[168,128]{1,0:T(8,128)S(1)}, u32[]{:S(2)}, u32[]{:S(2)}) %collective-permute-start.11) | collective-permute-done | bytes 86048 | tf_op jit(solution)/shard_map/ppermute | solution.py:501
  31.5 0.0 collective-permute-done.10.y_edge
  31.5 0.0 copy-done.1
  31.5 2.9 %analyse_far_and_step.1 = f32[1280,128]{1,0:T(8,128)} custom-call(s32[8,128]{1,0:T(8,128)S(1)} %copy-done, f32[16,128]{1,0:T(8,128)S(1)} %bitcast.19, f32[28,80,128]{2,1,0:T(8,128)S(1)} %get-tuple-element.22.near, f32[640,128]{1,0:T(8,128)S(1)} %collective-permute-done.10.y_edge, f32[168,128]{1,0:T(8,128)S(1)} %collective-permute-done.11.outer, ...), custom_call_target="tpu_custom_call" | custom-call | tf_op jit(solution)/shard_map/analyse_far_and_step/pallas_call | solution.py:531
  (8 shorter events, 0.1 us)
Async XLA Ops:
  0.0 26.5 %copy-start = (s32[8,128]{1,0:T(8,128)S(1)}, s32[8,128]{1,0:T(8,128)}, u32[]{:S(2)}) copy-start(s32[8,128]{1,0:T(8,128)} %mask.7) | copy-start | bytes 12292
  1.8 1.4 %collective-permute-start.1 = (f32[88,128]{1,0:T(8,128)S(1)}, f32[88,128]{1,0:T(8,128)S(1)}, u32[]{:S(2)}, u32[]{:S(2)}) collective-permute-start(f32[88,128]{1,0:T(8,128)S(1)} %get-tuple-element.20), channel_id=1, source_target_pairs={{0,1},{1,0},{2,3},{3,2},{4,5},{5,4},{6,7},{7,6},{8,9},{9,8},{10,11... | collective-permute-start | bytes 135176 | tf_op jit(solution)/shard_map/ppermute | solution.py:433
  3.2 4.9 %collective-permute-start.2 = (f32[88,128]{1,0:T(8,128)S(1)}, f32[88,128]{1,0:T(8,128)S(1)}, u32[]{:S(2)}, u32[]{:S(2)}) collective-permute-start(f32[88,128]{1,0:T(8,128)S(1)} %add.6), channel_id=1, source_target_pairs={{0,2},{1,3},{2,0},{3,1},{4,6},{5,7},{6,4},{7,5},{8,10},{9,11},{10,... | collective-permute-start | bytes 135176 | tf_op jit(solution)/shard_map/ppermute | solution.py:433
  8.1 6.5 %collective-permute-start.5 = (f32[88,128]{1,0:T(8,128)S(1)}, f32[88,128]{1,0:T(8,128)S(1)}, u32[]{:S(2)}, u32[]{:S(2)}) collective-permute-start(f32[88,128]{1,0:T(8,128)S(1)} %get-tuple-element.30), channel_id=1, source_target_pairs={{0,16},{4,20},{8,24},{12,28},{16,0},{20,4},{24,8},{28,12},{1,17},{... | collective-permute-start | bytes 135176 | tf_op jit(solution)/shard_map/ppermute | solution.py:433
  11.3 4.1 %collective-permute-start.4 = (f32[88,128]{1,0:T(8,128)S(1)}, f32[88,128]{1,0:T(8,128)S(1)}, u32[]{:S(2)}, u32[]{:S(2)}) collective-permute-start(f32[88,128]{1,0:T(8,128)S(1)} %get-tuple-element.30), channel_id=1, source_target_pairs={{0,8},{4,12},{8,0},{12,4},{16,24},{20,28},{24,16},{28,20},{1,9},{5... | collective-permute-start | bytes 135176 | tf_op jit(solution)/shard_map/ppermute | solution.py:433
  12.9 5.8 %collective-permute-start.6 = (f32[88,128]{1,0:T(8,128)S(1)}, f32[88,128]{1,0:T(8,128)S(1)}, u32[]{:S(2)}, u32[]{:S(2)}) collective-permute-start(f32[88,128]{1,0:T(8,128)S(1)} %get-tuple-element.30), channel_id=1, source_target_pairs={{0,24},{4,28},{8,16},{12,20},{16,8},{20,12},{24,0},{28,4},{1,25},{... | collective-permute-start | bytes 135176 | tf_op jit(solution)/shard_map/ppermute | solution.py:433
  12.9 7.4 %collective-permute-start.3 = (f32[256,128]{1,0:T(8,128)S(1)}, f32[256,128]{1,0:T(8,128)S(1)}, u32[]{:S(2)}, u32[]{:S(2)}) collective-permute-start(f32[256,128]{1,0:T(8,128)S(1)} %pad_maximum_fusion.1), channel_id=1, source_target_pairs={{0,4},{4,0},{8,12},{12,8},{16,20},{20,16},{24,28},{28,24},{1,5},{5... | collective-permute-start | bytes 393224 | tf_op jit(solution)/shard_map/ppermute | solution.py:433
  14.6 11.8 %collective-permute-start = (f32[640,128]{1,0:T(8,128)S(1)}, f32[640,128]{1,0:T(8,128)S(1)}, u32[]{:S(2)}, u32[]{:S(2)}) collective-permute-start(f32[640,128]{1,0:T(8,128)S(1)} %get-tuple-element.18), channel_id=1, source_target_pairs={{0,1},{1,0},{2,3},{3,2},{4,5},{5,4},{6,7},{7,6},{8,9},{9,8},{10,11... | collective-permute-start | bytes 983048 | tf_op jit(solution)/shard_map/ppermute | solution.py:433
  14.7 16.8 %collective-permute-start.10 = (f32[640,128]{1,0:T(8,128)S(1)}, f32[640,128]{1,0:T(8,128)S(1)}, u32[]{:S(2)}, u32[]{:S(2)}) collective-permute-start(f32[640,128]{1,0:T(8,128)S(1)} %get-tuple-element.23), channel_id=1, source_target_pairs={{1,2},{2,1},{0,0},{3,3},{5,6},{6,5},{4,4},{7,7},{9,10},{10,9},{8,8... | collective-permute-start | bytes 983048 | tf_op jit(solution)/shard_map/ppermute | solution.py:499
  18.7 12.7 %copy-start.1 = (f32[2,8,128]{2,1,0:T(8,128)S(1)}, f32[2,8,128]{2,1,0:T(8,128)}, u32[]{:S(2)}) copy-start(f32[2,8,128]{2,1,0:T(8,128)} %param.15) | copy-start | bytes 24580
  18.7 5.1 %collective-permute-start.7 = (f32[3,88,128]{2,1,0:T(8,128)S(1)}, f32[3,88,128]{2,1,0:T(8,128)S(1)}, u32[]{:S(2)}, u32[]{:S(2)}) collective-permute-start(f32[3,88,128]{2,1,0:T(8,128)S(1)} %pad_maximum_fusion), channel_id=1, source_target_pairs={{0,4},{4,0},{8,12},{12,8},{16,20},{20,16},{24,28},{28,24},{1,5},{5... | collective-permute-start | bytes 405512 | tf_op jit(solution)/shard_map/ppermute | solution.py:433
  20.3 6.2 %collective-permute-start.8 = (f32[5,88,128]{2,1,0:T(8,128)S(1)}, f32[5,88,128]{2,1,0:T(8,128)S(1)}, u32[]{:S(2)}, u32[]{:S(2)}) collective-permute-start(f32[5,88,128]{2,1,0:T(8,128)S(1)} %constant_dynamic-update-slice_fusion.rest_0_), channel_id=1, source_target_pairs={{0,1},{1,0},{2,3},{3,2},{4,5},{5,4},{6,7},{7,6},{8,9},{9,8},{10,11... | collective-permute-start | bytes 675848 | tf_op jit(solution)/shard_map/ppermute | solution.py:433
  23.8 2.7 %collective-permute-start.9 = (f32[3,88,128]{2,1,0:T(8,128)S(1)}, f32[3,88,128]{2,1,0:T(8,128)S(1)}, u32[]{:S(2)}, u32[]{:S(2)}) collective-permute-start(f32[3,88,128]{2,1,0:T(8,128)S(1)} %collective-permute-done.7.rest_1_), channel_id=1, source_target_pairs={{0,1},{1,0},{2,3},{3,2},{4,5},{5,4},{6,7},{7,6},{8,9},{9,8},{10,11... | collective-permute-start | bytes 405512 | tf_op jit(solution)/shard_map/ppermute | solution.py:433
  23.8 7.6 %collective-permute-start.11 = (f32[168,128]{1,0:T(8,128)S(1)}, f32[168,128]{1,0:T(8,128)S(1)}, u32[]{:S(2)}, u32[]{:S(2)}) collective-permute-start(f32[168,128]{1,0:T(8,128)S(1)} %get-tuple-element.24), channel_id=1, source_target_pairs={{4,8},{12,16},{20,24},{28,0},{8,4},{16,12},{24,20},{0,28},{5,9},{1... | collective-permute-start | bytes 258056 | tf_op jit(solution)/shard_map/ppermute | solution.py:501

commit v6 on v5

--- a/solution.py
+++ b/solution.py
@@ -210,11 +210,14 @@
     for i, (t, at) in enumerate([(t, at) for t in steps for at in range(0, last - first, 2)]):
         if meanwhile is not None and i == meanwhile[0]:
             meanwhile[1]()
+        if ahead and ahead[0][1] == at:
+            finish()
         x = jnp.concatenate([fields[at], fields[at + 1]], 1)
         ahead.append((t, at, x, dot(sides[t], centred_parts(x))))
         if len(ahead) > 1:
             finish()
-    finish()
+    while ahead:
+        finish()
 
 
 def move_rows(fields, gained, first, last, ocean, terms, chunks, meanwhile=None):
@@ -230,7 +233,7 @@
             fields[at] = fields[at] + gained[at]
 
 
-def near_kernel(members, parts, columns, flip, around, chunks, mask, own, core_edge, inner, *rest):
+def near_kernel(members, parts, columns, floors, flip, around, chunks, mask, own, core_edge, y_edge, inner, *rest):
     mine_parts, other_parts = rest[: len(parts)], rest[len(parts) : 2 * len(parts)]
     fields, sides, gains, row_terms, lat_terms, packed, gained = rest[2 * len(parts) :]
     mine = [part.at[i] for part, size in zip(mine_parts, parts) for i in range(size)]
@@ -269,15 +272,18 @@
     inner_start = inner.shape[0] - (members * LEVS + 8)
     for r in range(ROWS):
         fields[r] = own[r]
+    level = gz + 2 * core - 1
+    beyond = jnp.where((level >= 0) & (level < floors), 1.0, 0.0)
     for lon in range(LONS):
         fields[CORE_ROW + lon] = core_edge[pl.ds(lon, members, stride=LONS), :]
+        fields[Y_ROW + lon] = y_edge[pl.ds(lon, members, stride=LONS), :] * beyond
     for lev in range(LEVS):
         at = inner_start + lev * members
         fields[INNER_ROW + lev] = inner[at : at + members, :]
     wet = mask[...].astype(F32)
     ocean = [wet[lon : lon + 1] for lon in range(LONS)] * 3
     at = inner_start + members * LEVS
-    ocean += [inner[at : at + 1, :]] * LEVS
+    ocean += [inner[at : at + 1, :]] * LEVS + ocean[:LONS]
 
     row_lev, row_lon, inside, outside, inner_col, outer_col = place_terms(col, gz, columns)
 
@@ -314,7 +320,7 @@
         if b == 0:
             prior = wide[:members]
         else:
-            prior = jnp.concatenate([fields[Y_ROW + 2 * k], fields[Y_ROW + 2 * k + 1]], 1) * occupied
+            prior = jnp.concatenate([fields[OUTER_ROW + 2 * k], fields[OUTER_ROW + 2 * k + 1]], 1) * occupied
         noise = jnp.where(occupied > 0, row("noise"), 1.0)
         mean = jnp.sum(prior, 0, keepdims=True) / members
         anomaly = prior - mean
@@ -370,7 +376,7 @@
             x = wide[:members]
             moved = increment(x, sides[k], gains[k], taper) * wide[members : members + 1]
             for h in range(2):
-                at = Y_ROW + 2 * k1 + h
+                at = OUTER_ROW + 2 * k1 + h
                 piece = slice(h * LATS, (h + 1) * LATS)
                 before = x[:, piece] if chunks == 1 else jnp.where(k == 0, x[:, piece], fields[at])
                 fields[at] = before + moved[:, piece]
@@ -384,28 +390,24 @@
     terms = (sides, gains, row_terms, lat_terms)
     for_each(chunks, first_terms)
     meanwhile = (6, lambda: for_each(chunks, second_terms))
-    move_rows(fields, gained, 0, Y_ROW, ocean, terms, chunks, meanwhile)
+    move_rows(fields, gained, 0, OUTER_ROW, ocean, terms, chunks, meanwhile)
 
 
 def far_kernel(
-    members, columns, floors, chunks, mask, zonal, near, y_edge, outer, sides, gains, row_terms, lat_terms, out, fields, gained
+    members, columns, chunks, mask, zonal, near, outer, sides, gains, row_terms, lat_terms, out, fields, gained
 ):
     col, gz = position()
     core = gz % 2
     even_col = col % 2 == 0
     lane = iota((1, LATS), 1)
-    outer_at = OUTER_ROW - Y_ROW
-    beyond = gz + 2 * core - 1
-    inside = jnp.where((beyond >= 0) & (beyond < floors), 1.0, 0.0)
-    for lon in range(LONS):
-        fields[lon] = y_edge[pl.ds(lon, members, stride=LONS), :] * inside
+    outer_at = 0
     for lev in range(LEVS):
         fields[outer_at + lev] = outer[lev * members : (lev + 1) * members, :]
     wet = mask[...].astype(F32)
     ocean = [wet[lon : lon + 1] for lon in range(LONS)]
     edge = members * LEVS
     terms = (sides, gains, row_terms, lat_terms)
-    move_rows(fields, gained, Y_ROW, EXT_ROWS, ocean + [outer[edge : edge + 1, :]] * LEVS, terms, chunks)
+    move_rows(fields, gained, OUTER_ROW, EXT_ROWS, [outer[edge : edge + 1, :]] * LEVS, terms, chunks)
 
     for r in range(ROWS):
         lev, lon = r // LONS, r % LONS
@@ -415,7 +417,7 @@
         lon_prev = near[r - 1] if lon > 0 else jnp.where(even_col, side[1], side[0])
         lat_next = jnp.where(lane < LATS - 1, pltpu.roll(x, LATS - 1, 1), 0.0)
         lat_prev = jnp.where(lane > 0, pltpu.roll(x, 1, 1), 0.0)
-        over = jnp.where(core == 1 - lev, near[CORE_ROW + lon], fields[lon])
+        over = jnp.where(core == 1 - lev, near[CORE_ROW + lon], near[Y_ROW + lon])
         vertical = near[r ^ LONS] + over
         tendency = (
             -0.5 * zonal[r : r + 1, :] * (lon_next - lon_prev)
@@ -505,12 +507,12 @@
 
     slots = min(sum(parts) * CAP, MEAN_COUNT * columns)
     chunks = -(-slots // CHUNK)
-    rows = Y_ROW + 2 * chunks
+    rows = OUTER_ROW + 2 * chunks
     several = chunks > 1
     count = BATCHES * chunks
     limit = room(48 if several else 16)
     near, *terms = pl.pallas_call(
-        functools.partial(near_kernel, members, parts, columns, flip, around, chunks),
+        functools.partial(near_kernel, members, parts, columns, floors, flip, around, chunks),
         out_shape=[
             pltpu.VMEM((rows, members, LATS), F32),
             pltpu.VMEM((count, CHUNK, CHUNK), BF16),
@@ -518,28 +520,28 @@
             pltpu.VMEM((count, CHUNK, LATS), F32),
             pltpu.VMEM((count, CHUNK, LATS), F32),
         ],
-        in_specs=[vmem] * (4 + 2 * len(parts)),
+        in_specs=[vmem] * (5 + 2 * len(parts)),
         out_specs=[vmem] * 5,
         scratch_shapes=[
             pltpu.VMEM((BATCHES, chunks * CHUNK // CAP, height, CAP), F32),
-            pltpu.VMEM((Y_ROW if several else 1, members, LATS), F32),
+            pltpu.VMEM((OUTER_ROW if several else 1, members, LATS), F32),
         ],
         compiler_params=limit,
         cost_estimate=pl.CostEstimate(flops=0, bytes_accessed=0, transcendentals=0),
         name="analyse_near",
-    )(ocean_mask, own, core_edge, inner, *gathered, *other)
+    )(ocean_mask, own, core_edge, y_edge.reshape(level, LATS), inner, *gathered, *other)
     out = pl.pallas_call(
-        functools.partial(far_kernel, members, columns, floors, chunks),
+        functools.partial(far_kernel, members, columns, chunks),
         out_shape=jax.ShapeDtypeStruct((members * ROWS, LATS), F32),
-        in_specs=[vmem] * 9,
+        in_specs=[vmem] * 8,
         out_specs=vmem,
         scratch_shapes=[
-            pltpu.VMEM((EXT_ROWS - Y_ROW, members, LATS), F32),
-            pltpu.VMEM((EXT_ROWS - Y_ROW if several else 1, members, LATS), F32),
+            pltpu.VMEM((EXT_ROWS - OUTER_ROW, members, LATS), F32),
+            pltpu.VMEM((EXT_ROWS - OUTER_ROW if several else 1, members, LATS), F32),
         ],
         compiler_params=limit,
         name="analyse_far_and_step",
-    )(ocean_mask, zonal_current.reshape(ROWS, LATS), near, y_edge, outer, *terms)
+    )(ocean_mask, zonal_current.reshape(ROWS, LATS), near, outer, *terms)
     return out.reshape(state.shape)
 
 

time: 34.5 us -> 33.8 us (0.980)
  waiting for transfers between devices: 8.97 us -> 8.31 us
    pallas_call x1, Pallas kernels: 4.26 us -> 5.13 us  [local(): pl.pallas_call(functools.partial(near_kernel, members, parts, columns, fl...]
    pallas_call x1, Pallas kernels: 2.85 us -> 1.99 us  [local(): pl.pallas_call(functools.partial(far_kernel, members, columns, chunks), o...]
    ppermute x1, waiting for transfers between devices: 0.67 us -> 0.01 us  [local(): outer = lax.ppermute(outer, 'col', ring + [(j, i) for i, j in ring])]
  transfers between devices with their start and end apart: 12 -> 12, of which waited for: 5 -> 4; matrix products, arithmetic and copies ran while one was open for 0% -> 0% of each run, Pallas kernels for 16% -> 19%
where the time goes in v6:
time: 33.8 us; the launch traced here: 33.7 us
  starting transfers between devices  14.9 us (44%)
  Pallas kernels  10.2 us (30%)
  waiting for transfers between devices  8.31 us (25%)
    ppermute x10, starting transfers between devices, swapped(): lax.ppermute(x, axis, [(i, i ^ bit) for i in range(lax.axis_size(axis))])  11.6 us
    ppermute x10, waiting for transfers between devices, swapped(): lax.ppermute(x, axis, [(i, i ^ bit) for i in range(lax.axis_size(axis))])  8.3 us
    pallas_call x1, Pallas kernels, local(): pl.pallas_call(functools.partial(near_kernel, members, parts, columns, fl...  5.13 us
    ppermute x1, starting transfers between devices, local(): outer = lax.ppermute(outer, 'col', ring + [(j, i) for i, j in ring])  2.67 us
    pallas_call x1, Pallas kernels, local(): pl.pallas_call(functools.partial(far_kernel, members, columns, chunks), o...  1.99 us
    pallas_call x1, Pallas kernels, local(): pl.pallas_call(functools.partial(pick_kernel, members, columns), out_shap...  1.75 us
    pallas_call x1, Pallas kernels, local(): pl.pallas_call(functools.partial(edges_kernel, members), out_shape=like(l...  1.37 us
  transfers between devices with their start and end apart: 12, of which 4 were waited for; matrix products, arithmetic and copies ran while one was open for 0% of the time, Pallas kernels for 19%

profile of v6, /device:TPU:0, one launch (start us, length us, event | category | flops | bytes accessed | tf_op | source)
XLA Modules:
  0.0 33.7 jit_solution(2551745702948865394)
XLA Ops:
  0.0 0.0 copy-start
  0.0 1.8 %pick_priors.1 = (f32[88,128]{1,0:T(8,128)S(1)}, f32[88,128]{1,0:T(8,128)S(1)}) custom-call(s32[1,2]{1,0:T(1,128)} %bitcast.26, s32[2,1,8]{2,1,0:T(1,128)} %bitcast.25, s32[2,1024]{1,0:T(2,128)} %site.1, f32[2,128]{1,0:T(2,128)} %value.1, f32[2,128]{1,0:T(2,128)} %noise.1, s32[8,128]{1,0:T(8,128)} %mask.7, f32[1280,128]{1,0:T(8,128)} %bitcast.20), custom_call_target="tpu_custom_call" | custom-call | tf_op jit(solution)/shard_map/pick_priors/pallas_call | solution.py:457
  1.8 0.5 %collective-permute-start.2 = (f32[88,128]{1,0:T(8,128)S(1)}, f32[88,128]{1,0:T(8,128)S(1)}, u32[]{:S(2)}, u32[]{:S(2)}) collective-permute-start(f32[88,128]{1,0:T(8,128)S(1)} %get-tuple-element.21), channel_id=1, source_target_pairs={{0,1},{1,0},{2,3},{3,2},{4,5},{5,4},{6,7},{7,6},{8,9},{9,8},{10,11... | collective-permute-start | bytes 135176 | tf_op jit(solution)/shard_map/ppermute | solution.py:435
  2.3 0.9 %collective-permute-done.2 = f32[88,128]{1,0:T(8,128)S(1)} collective-permute-done((f32[88,128]{1,0:T(8,128)S(1)}, f32[88,128]{1,0:T(8,128)S(1)}, u32[]{:S(2)}, u32[]{:S(2)}) %collective-permute-start.2) | collective-permute-done | bytes 45088 | tf_op jit(solution)/shard_map/ppermute | solution.py:435
  3.2 2.9 %collective-permute-start.3 = (f32[88,128]{1,0:T(8,128)S(1)}, f32[88,128]{1,0:T(8,128)S(1)}, u32[]{:S(2)}, u32[]{:S(2)}) collective-permute-start(f32[88,128]{1,0:T(8,128)S(1)} %add.6), channel_id=1, source_target_pairs={{0,2},{1,3},{2,0},{3,1},{4,6},{5,7},{6,4},{7,5},{8,10},{9,11},{10,... | collective-permute-start | bytes 135176 | tf_op jit(solution)/shard_map/ppermute | solution.py:435
  6.1 1.4 %copy_edges.1 = (f32[640,128]{1,0:T(8,128)S(1)}, f32[640,128]{1,0:T(8,128)S(1)}, f32[168,128]{1,0:T(8,128)S(1)}, f32[168,128]{1,0:T(8,128)S(1)}, f32[16,80,128]{2,1,0:T(8,128)S(1)}) custom-call(s32[8,128]{1,0:T(8,128)} %mask.7, f32[1280,128]{1,0:T(8,128)} %bitcast.21), custom_call_target="tpu_custom_call" | custom-call | bytes 4194304 | tf_op jit(solution)/shard_map/copy_edges/pallas_call | solution.py:474
  7.5 0.7 %collective-permute-done.3 = f32[88,128]{1,0:T(8,128)S(1)} collective-permute-done((f32[88,128]{1,0:T(8,128)S(1)}, f32[88,128]{1,0:T(8,128)S(1)}, u32[]{:S(2)}, u32[]{:S(2)}) %collective-permute-start.3) | collective-permute-done | bytes 45088 | tf_op jit(solution)/shard_map/ppermute | solution.py:435
  8.1 3.2 %collective-permute-start.6 = (f32[88,128]{1,0:T(8,128)S(1)}, f32[88,128]{1,0:T(8,128)S(1)}, u32[]{:S(2)}, u32[]{:S(2)}) collective-permute-start(f32[88,128]{1,0:T(8,128)S(1)} %get-tuple-element.30), channel_id=1, source_target_pairs={{0,16},{4,20},{8,24},{12,28},{16,0},{20,4},{24,8},{28,12},{1,17},{... | collective-permute-start | bytes 135176 | tf_op jit(solution)/shard_map/ppermute | solution.py:435
  11.3 1.6 %collective-permute-start.5 = (f32[88,128]{1,0:T(8,128)S(1)}, f32[88,128]{1,0:T(8,128)S(1)}, u32[]{:S(2)}, u32[]{:S(2)}) collective-permute-start(f32[88,128]{1,0:T(8,128)S(1)} %get-tuple-element.30), channel_id=1, source_target_pairs={{0,8},{4,12},{8,0},{12,4},{16,24},{20,28},{24,16},{28,20},{1,9},{5... | collective-permute-start | bytes 135176 | tf_op jit(solution)/shard_map/ppermute | solution.py:435
  12.9 0.0 collective-permute-start.7
  12.9 0.0 copy-start.1
  12.9 1.8 %collective-permute-start.4 = (f32[256,128]{1,0:T(8,128)S(1)}, f32[256,128]{1,0:T(8,128)S(1)}, u32[]{:S(2)}, u32[]{:S(2)}) collective-permute-start(f32[256,128]{1,0:T(8,128)S(1)} %pad_maximum_fusion.1), channel_id=1, source_target_pairs={{0,4},{4,0},{8,12},{12,8},{16,20},{20,16},{24,28},{28,24},{1,5},{5... | collective-permute-start | bytes 393224 | tf_op jit(solution)/shard_map/ppermute | solution.py:435
  14.7 0.0 collective-permute-start
  14.7 0.0 collective-permute-done.6
  14.7 0.7 %collective-permute-start.1 = (f32[640,128]{1,0:T(8,128)S(1)}, f32[640,128]{1,0:T(8,128)S(1)}, u32[]{:S(2)}, u32[]{:S(2)}) collective-permute-start(f32[640,128]{1,0:T(8,128)S(1)} %get-tuple-element.19), channel_id=1, source_target_pairs={{1,2},{2,1},{0,0},{3,3},{5,6},{6,5},{4,4},{7,7},{9,10},{10,9},{8,8... | collective-permute-start | bytes 983048 | tf_op jit(solution)/shard_map/ppermute | solution.py:501
  15.3 0.0 collective-permute-done.5
  15.4 3.3 %collective-permute-done.7 = f32[88,128]{1,0:T(8,128)S(1)} collective-permute-done((f32[88,128]{1,0:T(8,128)S(1)}, f32[88,128]{1,0:T(8,128)S(1)}, u32[]{:S(2)}, u32[]{:S(2)}) %collective-permute-start.7) | collective-permute-done | bytes 45088 | tf_op jit(solution)/shard_map/ppermute | solution.py:435
  18.7 1.6 %collective-permute-start.8 = (f32[3,88,128]{2,1,0:T(8,128)S(1)}, f32[3,88,128]{2,1,0:T(8,128)S(1)}, u32[]{:S(2)}, u32[]{:S(2)}) collective-permute-start(f32[3,88,128]{2,1,0:T(8,128)S(1)} %pad_maximum_fusion), channel_id=1, source_target_pairs={{0,4},{4,0},{8,12},{12,8},{16,20},{20,16},{24,28},{28,24},{1,5},{5... | collective-permute-start | bytes 405512 | tf_op jit(solution)/shard_map/ppermute | solution.py:435
  20.3 0.0 collective-permute-done.4.inner
  20.3 0.1 collective-permute-start.9
  20.4 3.4 %collective-permute-done.8.rest_1_ = f32[3,88,128]{2,1,0:T(8,128)S(1)} collective-permute-done((f32[3,88,128]{2,1,0:T(8,128)S(1)}, f32[3,88,128]{2,1,0:T(8,128)S(1)}, u32[]{:S(2)}, u32[]{:S(2)}) %collective-permute-start.8) | collective-permute-done | bytes 135200 | tf_op jit(solution)/shard_map/ppermute | solution.py:435
  23.8 0.0 collective-permute-start.10
  23.8 2.7 %collective-permute-start.11 = (f32[168,128]{1,0:T(8,128)S(1)}, f32[168,128]{1,0:T(8,128)S(1)}, u32[]{:S(2)}, u32[]{:S(2)}) collective-permute-start(f32[168,128]{1,0:T(8,128)S(1)} %get-tuple-element.24), channel_id=1, source_target_pairs={{4,8},{12,16},{20,24},{28,0},{8,4},{16,12},{24,20},{0,28},{5,9},{1... | collective-permute-start | bytes 258056 | tf_op jit(solution)/shard_map/ppermute | solution.py:503
  26.5 0.0 collective-permute-done.core_edge
  26.5 0.0 collective-permute-done.1.y_edge
  26.5 0.0 collective-permute-done.10.rest_3_
  26.5 0.0 collective-permute-done.9.rest_2_
  26.5 0.0 copy-done
  26.5 5.1 %analyse_near.1 = (f32[36,80,128]{2,1,0:T(8,128)S(1)}, bf16[2,256,256]{2,1,0:T(8,128)(2,1)S(1)}, bf16[2,160,256]{2,1,0:T(8,128)(2,1)S(1)}, f32[2,256,128]{2,1,0:T(8,128)S(1)}, f32[2,256,128]{2,1,0:T(8,128)S(1)}) custom-call(s32[8,128]{1,0:T(8,128)S(1)} %copy-done, f32[16,80,128]{2,1,0:T(8,128)S(1)} %get-tuple-element.17.own, ...), custom_call_target="tpu_custom_call" | custom-call | tf_op jit(solution)/shard_map/analyse_near/pallas_call | solution.py:514
  31.6 0.0 collective-permute-done.11.outer
  31.7 0.0 copy-done.1
  31.7 2.0 %analyse_far_and_step.1 = f32[1280,128]{1,0:T(8,128)} custom-call(s32[8,128]{1,0:T(8,128)S(1)} %copy-done, f32[16,128]{1,0:T(8,128)S(1)} %bitcast.19, f32[36,80,128]{2,1,0:T(8,128)S(1)} %get-tuple-element.23.near, f32[168,128]{1,0:T(8,128)S(1)} %collective-permute-done.11.outer, bf16[2,256,256]{2,1,0:T(8,128)(2,1)S(1)} %get-tuple-element.25.sides, ...), custom_call_target="tpu_custom_call" | custom-call | tf_op jit(solution)/shard_map/analyse_far_and_step/pallas_call | solution.py:533
  (8 shorter events, 0.1 us)
Async XLA Ops:
  0.0 26.5 %copy-start = (s32[8,128]{1,0:T(8,128)S(1)}, s32[8,128]{1,0:T(8,128)}, u32[]{:S(2)}) copy-start(s32[8,128]{1,0:T(8,128)} %mask.7) | copy-start | bytes 12292
  1.8 1.4 %collective-permute-start.2 = (f32[88,128]{1,0:T(8,128)S(1)}, f32[88,128]{1,0:T(8,128)S(1)}, u32[]{:S(2)}, u32[]{:S(2)}) collective-permute-start(f32[88,128]{1,0:T(8,128)S(1)} %get-tuple-element.21), channel_id=1, source_target_pairs={{0,1},{1,0},{2,3},{3,2},{4,5},{5,4},{6,7},{7,6},{8,9},{9,8},{10,11... | collective-permute-start | bytes 135176 | tf_op jit(solution)/shard_map/ppermute | solution.py:435
  3.2 4.9 %collective-permute-start.3 = (f32[88,128]{1,0:T(8,128)S(1)}, f32[88,128]{1,0:T(8,128)S(1)}, u32[]{:S(2)}, u32[]{:S(2)}) collective-permute-start(f32[88,128]{1,0:T(8,128)S(1)} %add.6), channel_id=1, source_target_pairs={{0,2},{1,3},{2,0},{3,1},{4,6},{5,7},{6,4},{7,5},{8,10},{9,11},{10,... | collective-permute-start | bytes 135176 | tf_op jit(solution)/shard_map/ppermute | solution.py:435
  8.1 6.5 %collective-permute-start.6 = (f32[88,128]{1,0:T(8,128)S(1)}, f32[88,128]{1,0:T(8,128)S(1)}, u32[]{:S(2)}, u32[]{:S(2)}) collective-permute-start(f32[88,128]{1,0:T(8,128)S(1)} %get-tuple-element.30), channel_id=1, source_target_pairs={{0,16},{4,20},{8,24},{12,28},{16,0},{20,4},{24,8},{28,12},{1,17},{... | collective-permute-start | bytes 135176 | tf_op jit(solution)/shard_map/ppermute | solution.py:435
  11.3 4.1 %collective-permute-start.5 = (f32[88,128]{1,0:T(8,128)S(1)}, f32[88,128]{1,0:T(8,128)S(1)}, u32[]{:S(2)}, u32[]{:S(2)}) collective-permute-start(f32[88,128]{1,0:T(8,128)S(1)} %get-tuple-element.30), channel_id=1, source_target_pairs={{0,8},{4,12},{8,0},{12,4},{16,24},{20,28},{24,16},{28,20},{1,9},{5... | collective-permute-start | bytes 135176 | tf_op jit(solution)/shard_map/ppermute | solution.py:435
  12.9 5.8 %collective-permute-start.7 = (f32[88,128]{1,0:T(8,128)S(1)}, f32[88,128]{1,0:T(8,128)S(1)}, u32[]{:S(2)}, u32[]{:S(2)}) collective-permute-start(f32[88,128]{1,0:T(8,128)S(1)} %get-tuple-element.30), channel_id=1, source_target_pairs={{0,24},{4,28},{8,16},{12,20},{16,8},{20,12},{24,0},{28,4},{1,25},{... | collective-permute-start | bytes 135176 | tf_op jit(solution)/shard_map/ppermute | solution.py:435
  12.9 18.8 %copy-start.1 = (f32[2,8,128]{2,1,0:T(8,128)S(1)}, f32[2,8,128]{2,1,0:T(8,128)}, u32[]{:S(2)}) copy-start(f32[2,8,128]{2,1,0:T(8,128)} %param.15) | copy-start | bytes 24580
  12.9 7.4 %collective-permute-start.4 = (f32[256,128]{1,0:T(8,128)S(1)}, f32[256,128]{1,0:T(8,128)S(1)}, u32[]{:S(2)}, u32[]{:S(2)}) collective-permute-start(f32[256,128]{1,0:T(8,128)S(1)} %pad_maximum_fusion.1), channel_id=1, source_target_pairs={{0,4},{4,0},{8,12},{12,8},{16,20},{20,16},{24,28},{28,24},{1,5},{5... | collective-permute-start | bytes 393224 | tf_op jit(solution)/shard_map/ppermute | solution.py:435
  14.7 11.8 %collective-permute-start = (f32[640,128]{1,0:T(8,128)S(1)}, f32[640,128]{1,0:T(8,128)S(1)}, u32[]{:S(2)}, u32[]{:S(2)}) collective-permute-start(f32[640,128]{1,0:T(8,128)S(1)} %get-tuple-element.18), channel_id=1, source_target_pairs={{0,1},{1,0},{2,3},{3,2},{4,5},{5,4},{6,7},{7,6},{8,9},{9,8},{10,11... | collective-permute-start | bytes 983048 | tf_op jit(solution)/shard_map/ppermute | solution.py:435
  14.7 11.8 %collective-permute-start.1 = (f32[640,128]{1,0:T(8,128)S(1)}, f32[640,128]{1,0:T(8,128)S(1)}, u32[]{:S(2)}, u32[]{:S(2)}) collective-permute-start(f32[640,128]{1,0:T(8,128)S(1)} %get-tuple-element.19), channel_id=1, source_target_pairs={{1,2},{2,1},{0,0},{3,3},{5,6},{6,5},{4,4},{7,7},{9,10},{10,9},{8,8... | collective-permute-start | bytes 983048 | tf_op jit(solution)/shard_map/ppermute | solution.py:501
  18.7 5.1 %collective-permute-start.8 = (f32[3,88,128]{2,1,0:T(8,128)S(1)}, f32[3,88,128]{2,1,0:T(8,128)S(1)}, u32[]{:S(2)}, u32[]{:S(2)}) collective-permute-start(f32[3,88,128]{2,1,0:T(8,128)S(1)} %pad_maximum_fusion), channel_id=1, source_target_pairs={{0,4},{4,0},{8,12},{12,8},{16,20},{20,16},{24,28},{28,24},{1,5},{5... | collective-permute-start | bytes 405512 | tf_op jit(solution)/shard_map/ppermute | solution.py:435
  20.3 6.2 %collective-permute-start.9 = (f32[5,88,128]{2,1,0:T(8,128)S(1)}, f32[5,88,128]{2,1,0:T(8,128)S(1)}, u32[]{:S(2)}, u32[]{:S(2)}) collective-permute-start(f32[5,88,128]{2,1,0:T(8,128)S(1)} %constant_dynamic-update-slice_fusion.rest_0_), channel_id=1, source_target_pairs={{0,1},{1,0},{2,3},{3,2},{4,5},{5,4},{6,7},{7,6},{8,9},{9,8},{10,11... | collective-permute-start | bytes 675848 | tf_op jit(solution)/shard_map/ppermute | solution.py:435
  23.8 2.7 %collective-permute-start.10 = (f32[3,88,128]{2,1,0:T(8,128)S(1)}, f32[3,88,128]{2,1,0:T(8,128)S(1)}, u32[]{:S(2)}, u32[]{:S(2)}) collective-permute-start(f32[3,88,128]{2,1,0:T(8,128)S(1)} %collective-permute-done.8.rest_1_), channel_id=1, source_target_pairs={{0,1},{1,0},{2,3},{3,2},{4,5},{5,4},{6,7},{7,6},{8,9},{9,8},{10,11... | collective-permute-start | bytes 405512 | tf_op jit(solution)/shard_map/ppermute | solution.py:435
  23.8 7.8 %collective-permute-start.11 = (f32[168,128]{1,0:T(8,128)S(1)}, f32[168,128]{1,0:T(8,128)S(1)}, u32[]{:S(2)}, u32[]{:S(2)}) collective-permute-start(f32[168,128]{1,0:T(8,128)S(1)} %get-tuple-element.24), channel_id=1, source_target_pairs={{4,8},{12,16},{20,24},{28,0},{8,4},{16,12},{24,20},{0,28},{5,9},{1... | collective-permute-start | bytes 258056 | tf_op jit(solution)/shard_map/ppermute | solution.py:503

commit v7 on v6

--- a/solution.py
+++ b/solution.py
@@ -190,7 +190,7 @@
     return added(*products(dot(sides, centred_parts(x)), local, gains))
 
 
-def move_pairs(fields, into, first, last, ocean, terms, steps, meanwhile=None):
+def move_pairs(fields, into, first, last, ocean, terms, steps, meanwhile=None, aside=None):
     sides, gains, row_part, lat_part = terms
     ahead = []
 
@@ -198,8 +198,10 @@
         t, at, x, covariance = ahead.pop(0)
         columns = [ROW_COLUMN + first + at + h for h in range(2)]
         tapers = [lat_part[t] * row_part[t, :, c : c + 1] for c in columns]
-        moved = added(*products(covariance, jnp.concatenate(tapers, 1), gains[t]))
-        moved = moved * jnp.concatenate([ocean[at], ocean[at + 1]], 1)
+        parts = products(covariance, jnp.concatenate(tapers, 1), gains[t])
+        if aside is not None:
+            aside()
+        moved = added(*parts) * jnp.concatenate([ocean[at], ocean[at + 1]], 1)
         for h in range(2):
             piece = slice(h * LATS, (h + 1) * LATS)
             if into is fields:
@@ -214,15 +216,17 @@
             finish()
         x = jnp.concatenate([fields[at], fields[at + 1]], 1)
         ahead.append((t, at, x, dot(sides[t], centred_parts(x))))
+        if aside is not None:
+            aside()
         if len(ahead) > 1:
             finish()
     while ahead:
         finish()
 
 
-def move_rows(fields, gained, first, last, ocean, terms, chunks, meanwhile=None):
+def move_rows(fields, gained, first, last, ocean, terms, chunks, meanwhile=None, aside=None):
     if chunks == 1:
-        move_pairs(fields, fields, first, last, ocean, terms, range(BATCHES), meanwhile)
+        move_pairs(fields, fields, first, last, ocean, terms, range(BATCHES), meanwhile, aside)
         return
     if meanwhile is not None:
         meanwhile[1]()
@@ -407,9 +411,7 @@
     ocean = [wet[lon : lon + 1] for lon in range(LONS)]
     edge = members * LEVS
     terms = (sides, gains, row_terms, lat_terms)
-    move_rows(fields, gained, OUTER_ROW, EXT_ROWS, [outer[edge : edge + 1, :]] * LEVS, terms, chunks)
-
-    for r in range(ROWS):
+    def step(r):
         lev, lon = r // LONS, r % LONS
         x = near[r]
         side = [near[INNER_ROW + lev], fields[outer_at + lev]]
@@ -426,6 +428,19 @@
         )
         out[pl.ds(r, members, stride=ROWS), :] = x + ocean[lon] * tendency
 
+    inside = [r for r in range(ROWS) if 0 < r % LONS < LONS - 1]
+    left = list(inside)
+
+    def some_rows():
+        for r in left[:3]:
+            step(r)
+        del left[:3]
+
+    wet_edge = [outer[edge : edge + 1, :]] * LEVS
+    move_rows(fields, gained, OUTER_ROW, EXT_ROWS, wet_edge, terms, chunks, aside=some_rows)
+    for r in left + [r for r in range(ROWS) if r not in inside]:
+        step(r)
+
 
 def room(mebibytes):
     return pltpu.CompilerParams(vmem_limit_bytes=mebibytes * 1024 * 1024)
@@ -485,7 +500,7 @@
     flip = columns <= 2 * WINDOW + 1 and columns & (columns - 1) == 0
     if flip:
         inner = swapped(jnp.concatenate([mine, inner]), "col", 1)
-        bits = list(range(2, columns, 2))
+        bits = list(range(columns - 2, 0, -2))
         passed = [swapped(mine, "col", bit) for bit in bits]
         near = jnp.stack([mine, inner[:height]] + passed)
         gathered = [near, swapped(near[2:], "col", 1)]

time: 33.8 us -> 33.8 us (level)
  no operation moved by 1% of the time
where the time goes in v7:
time: 33.8 us; the launch traced here: 33.6 us
  starting transfers between devices  14.9 us (44%)
  Pallas kernels  10.2 us (30%)
  waiting for transfers between devices  8.31 us (25%)
    ppermute x10, starting transfers between devices, swapped(): lax.ppermute(x, axis, [(i, i ^ bit) for i in range(lax.axis_size(axis))])  11.4 us
    ppermute x10, waiting for transfers between devices, swapped(): lax.ppermute(x, axis, [(i, i ^ bit) for i in range(lax.axis_size(axis))])  8.31 us
    pallas_call x1, Pallas kernels, local(): pl.pallas_call(functools.partial(near_kernel, members, parts, columns, fl...  5.14 us
    ppermute x1, starting transfers between devices, local(): outer = lax.ppermute(outer, 'col', ring + [(j, i) for i, j in ring])  2.85 us
    pallas_call x1, Pallas kernels, local(): pl.pallas_call(functools.partial(far_kernel, members, columns, chunks), o...  1.95 us
    pallas_call x1, Pallas kernels, local(): pl.pallas_call(functools.partial(pick_kernel, members, columns), out_shap...  1.75 us
    pallas_call x1, Pallas kernels, local(): pl.pallas_call(functools.partial(edges_kernel, members), out_shape=like(l...  1.37 us
  transfers between devices with their start and end apart: 12, of which 4 were waited for; matrix products, arithmetic and copies ran while one was open for 0% of the time, Pallas kernels for 19%

profile of v7, /device:TPU:0, one launch (start us, length us, event | category | flops | bytes accessed | tf_op | source)
XLA Modules:
  0.0 33.6 jit_solution(14492757545190720639)
XLA Ops:
  0.0 0.0 copy-start
  0.0 1.8 %pick_priors.1 = (f32[88,128]{1,0:T(8,128)S(1)}, f32[88,128]{1,0:T(8,128)S(1)}) custom-call(s32[1,2]{1,0:T(1,128)} %bitcast.26, s32[2,1,8]{2,1,0:T(1,128)} %bitcast.25, s32[2,1024]{1,0:T(2,128)} %site.1, f32[2,128]{1,0:T(2,128)} %value.1, f32[2,128]{1,0:T(2,128)} %noise.1, s32[8,128]{1,0:T(8,128)} %mask.7, f32[1280,128]{1,0:T(8,128)} %bitcast.20), custom_call_target="tpu_custom_call" | custom-call | tf_op jit(solution)/shard_map/pick_priors/pallas_call | solution.py:472
  1.8 0.5 %collective-permute-start.2 = (f32[88,128]{1,0:T(8,128)S(1)}, f32[88,128]{1,0:T(8,128)S(1)}, u32[]{:S(2)}, u32[]{:S(2)}) collective-permute-start(f32[88,128]{1,0:T(8,128)S(1)} %get-tuple-element.21), channel_id=1, source_target_pairs={{0,1},{1,0},{2,3},{3,2},{4,5},{5,4},{6,7},{7,6},{8,9},{9,8},{10,11... | collective-permute-start | bytes 135176 | tf_op jit(solution)/shard_map/ppermute | solution.py:450
  2.3 0.9 %collective-permute-done.2 = f32[88,128]{1,0:T(8,128)S(1)} collective-permute-done((f32[88,128]{1,0:T(8,128)S(1)}, f32[88,128]{1,0:T(8,128)S(1)}, u32[]{:S(2)}, u32[]{:S(2)}) %collective-permute-start.2) | collective-permute-done | bytes 45088 | tf_op jit(solution)/shard_map/ppermute | solution.py:450
  3.2 2.9 %collective-permute-start.3 = (f32[88,128]{1,0:T(8,128)S(1)}, f32[88,128]{1,0:T(8,128)S(1)}, u32[]{:S(2)}, u32[]{:S(2)}) collective-permute-start(f32[88,128]{1,0:T(8,128)S(1)} %add.6), channel_id=1, source_target_pairs={{0,2},{1,3},{2,0},{3,1},{4,6},{5,7},{6,4},{7,5},{8,10},{9,11},{10,... | collective-permute-start | bytes 135176 | tf_op jit(solution)/shard_map/ppermute | solution.py:450
  6.1 1.4 %copy_edges.1 = (f32[640,128]{1,0:T(8,128)S(1)}, f32[640,128]{1,0:T(8,128)S(1)}, f32[168,128]{1,0:T(8,128)S(1)}, f32[168,128]{1,0:T(8,128)S(1)}, f32[16,80,128]{2,1,0:T(8,128)S(1)}) custom-call(s32[8,128]{1,0:T(8,128)} %mask.7, f32[1280,128]{1,0:T(8,128)} %bitcast.21), custom_call_target="tpu_custom_call" | custom-call | bytes 4194304 | tf_op jit(solution)/shard_map/copy_edges/pallas_call | solution.py:489
  7.5 0.7 %collective-permute-done.3 = f32[88,128]{1,0:T(8,128)S(1)} collective-permute-done((f32[88,128]{1,0:T(8,128)S(1)}, f32[88,128]{1,0:T(8,128)S(1)}, u32[]{:S(2)}, u32[]{:S(2)}) %collective-permute-start.3) | collective-permute-done | bytes 45088 | tf_op jit(solution)/shard_map/ppermute | solution.py:450
  8.1 3.2 %collective-permute-start.6 = (f32[88,128]{1,0:T(8,128)S(1)}, f32[88,128]{1,0:T(8,128)S(1)}, u32[]{:S(2)}, u32[]{:S(2)}) collective-permute-start(f32[88,128]{1,0:T(8,128)S(1)} %get-tuple-element.30), channel_id=1, source_target_pairs={{0,16},{4,20},{8,24},{12,28},{16,0},{20,4},{24,8},{28,12},{1,17},{... | collective-permute-start | bytes 135176 | tf_op jit(solution)/shard_map/ppermute | solution.py:450
  11.3 1.3 %collective-permute-start.5 = (f32[88,128]{1,0:T(8,128)S(1)}, f32[88,128]{1,0:T(8,128)S(1)}, u32[]{:S(2)}, u32[]{:S(2)}) collective-permute-start(f32[88,128]{1,0:T(8,128)S(1)} %get-tuple-element.30), channel_id=1, source_target_pairs={{0,24},{4,28},{8,16},{12,20},{16,8},{20,12},{24,0},{28,4},{1,25},{... | collective-permute-start | bytes 135176 | tf_op jit(solution)/shard_map/ppermute | solution.py:450
  12.6 0.2 collective-permute-start.7
  12.9 0.0 copy-start.1
  12.9 1.6 %collective-permute-start.4 = (f32[256,128]{1,0:T(8,128)S(1)}, f32[256,128]{1,0:T(8,128)S(1)}, u32[]{:S(2)}, u32[]{:S(2)}) collective-permute-start(f32[256,128]{1,0:T(8,128)S(1)} %pad_maximum_fusion.1), channel_id=1, source_target_pairs={{0,4},{4,0},{8,12},{12,8},{16,20},{20,16},{24,28},{28,24},{1,5},{5... | collective-permute-start | bytes 393224 | tf_op jit(solution)/shard_map/ppermute | solution.py:450
  14.4 0.0 collective-permute-start
  14.4 0.0 collective-permute-done.6
  14.5 0.7 %collective-permute-start.1 = (f32[640,128]{1,0:T(8,128)S(1)}, f32[640,128]{1,0:T(8,128)S(1)}, u32[]{:S(2)}, u32[]{:S(2)}) collective-permute-start(f32[640,128]{1,0:T(8,128)S(1)} %get-tuple-element.19), channel_id=1, source_target_pairs={{1,2},{2,1},{0,0},{3,3},{5,6},{6,5},{4,4},{7,7},{9,10},{10,9},{8,8... | collective-permute-start | bytes 983048 | tf_op jit(solution)/shard_map/ppermute | solution.py:516
  15.1 2.0 %collective-permute-done.5 = f32[88,128]{1,0:T(8,128)S(1)} collective-permute-done((f32[88,128]{1,0:T(8,128)S(1)}, f32[88,128]{1,0:T(8,128)S(1)}, u32[]{:S(2)}, u32[]{:S(2)}) %collective-permute-start.5) | collective-permute-done | bytes 45088 | tf_op jit(solution)/shard_map/ppermute | solution.py:450
  17.2 0.0 collective-permute-done.7
  17.2 1.6 %collective-permute-start.8 = (f32[3,88,128]{2,1,0:T(8,128)S(1)}, f32[3,88,128]{2,1,0:T(8,128)S(1)}, u32[]{:S(2)}, u32[]{:S(2)}) collective-permute-start(f32[3,88,128]{2,1,0:T(8,128)S(1)} %pad_maximum_fusion), channel_id=1, source_target_pairs={{0,4},{4,0},{8,12},{12,8},{16,20},{20,16},{24,28},{28,24},{1,5},{5... | collective-permute-start | bytes 405512 | tf_op jit(solution)/shard_map/ppermute | solution.py:450
  18.7 0.0 collective-permute-done.4.inner
  18.8 0.1 collective-permute-start.9
  18.9 4.7 %collective-permute-done.8.rest_1_ = f32[3,88,128]{2,1,0:T(8,128)S(1)} collective-permute-done((f32[3,88,128]{2,1,0:T(8,128)S(1)}, f32[3,88,128]{2,1,0:T(8,128)S(1)}, u32[]{:S(2)}, u32[]{:S(2)}) %collective-permute-start.8) | collective-permute-done | bytes 135200 | tf_op jit(solution)/shard_map/ppermute | solution.py:450
  23.6 0.0 collective-permute-start.10
  23.6 2.9 %collective-permute-start.11 = (f32[168,128]{1,0:T(8,128)S(1)}, f32[168,128]{1,0:T(8,128)S(1)}, u32[]{:S(2)}, u32[]{:S(2)}) collective-permute-start(f32[168,128]{1,0:T(8,128)S(1)} %get-tuple-element.24), channel_id=1, source_target_pairs={{4,8},{12,16},{20,24},{28,0},{8,4},{16,12},{24,20},{0,28},{5,9},{1... | collective-permute-start | bytes 258056 | tf_op jit(solution)/shard_map/ppermute | solution.py:518
  26.4 0.0 collective-permute-done.core_edge
  26.4 0.0 collective-permute-done.1.y_edge
  26.4 0.0 collective-permute-done.10.rest_3_
  26.5 0.0 collective-permute-done.9.rest_2_
  26.5 0.0 copy-done
  26.5 5.1 %analyse_near.1 = (f32[36,80,128]{2,1,0:T(8,128)S(1)}, bf16[2,256,256]{2,1,0:T(8,128)(2,1)S(1)}, bf16[2,160,256]{2,1,0:T(8,128)(2,1)S(1)}, f32[2,256,128]{2,1,0:T(8,128)S(1)}, f32[2,256,128]{2,1,0:T(8,128)S(1)}) custom-call(s32[8,128]{1,0:T(8,128)S(1)} %copy-done, f32[16,80,128]{2,1,0:T(8,128)S(1)} %get-tuple-element.17.own, ...), custom_call_target="tpu_custom_call" | custom-call | tf_op jit(solution)/shard_map/analyse_near/pallas_call | solution.py:529
  31.6 0.0 collective-permute-done.11.outer
  31.6 0.0 copy-done.1
  31.6 2.0 %analyse_far_and_step.1 = f32[1280,128]{1,0:T(8,128)} custom-call(s32[8,128]{1,0:T(8,128)S(1)} %copy-done, f32[16,128]{1,0:T(8,128)S(1)} %bitcast.19, f32[36,80,128]{2,1,0:T(8,128)S(1)} %get-tuple-element.23.near, f32[168,128]{1,0:T(8,128)S(1)} %collective-permute-done.11.outer, bf16[2,256,256]{2,1,0:T(8,128)(2,1)S(1)} %get-tuple-element.25.sides, ...), custom_call_target="tpu_custom_call" | custom-call | tf_op jit(solution)/shard_map/analyse_far_and_step/pallas_call | solution.py:548
  (8 shorter events, 0.1 us)
Async XLA Ops:
  0.0 26.5 %copy-start = (s32[8,128]{1,0:T(8,128)S(1)}, s32[8,128]{1,0:T(8,128)}, u32[]{:S(2)}) copy-start(s32[8,128]{1,0:T(8,128)} %mask.7) | copy-start | bytes 12292
  1.8 1.4 %collective-permute-start.2 = (f32[88,128]{1,0:T(8,128)S(1)}, f32[88,128]{1,0:T(8,128)S(1)}, u32[]{:S(2)}, u32[]{:S(2)}) collective-permute-start(f32[88,128]{1,0:T(8,128)S(1)} %get-tuple-element.21), channel_id=1, source_target_pairs={{0,1},{1,0},{2,3},{3,2},{4,5},{5,4},{6,7},{7,6},{8,9},{9,8},{10,11... | collective-permute-start | bytes 135176 | tf_op jit(solution)/shard_map/ppermute | solution.py:450
  3.2 4.9 %collective-permute-start.3 = (f32[88,128]{1,0:T(8,128)S(1)}, f32[88,128]{1,0:T(8,128)S(1)}, u32[]{:S(2)}, u32[]{:S(2)}) collective-permute-start(f32[88,128]{1,0:T(8,128)S(1)} %add.6), channel_id=1, source_target_pairs={{0,2},{1,3},{2,0},{3,1},{4,6},{5,7},{6,4},{7,5},{8,10},{9,11},{10,... | collective-permute-start | bytes 135176 | tf_op jit(solution)/shard_map/ppermute | solution.py:450
  8.1 6.3 %collective-permute-start.6 = (f32[88,128]{1,0:T(8,128)S(1)}, f32[88,128]{1,0:T(8,128)S(1)}, u32[]{:S(2)}, u32[]{:S(2)}) collective-permute-start(f32[88,128]{1,0:T(8,128)S(1)} %get-tuple-element.30), channel_id=1, source_target_pairs={{0,16},{4,20},{8,24},{12,28},{16,0},{20,4},{24,8},{28,12},{1,17},{... | collective-permute-start | bytes 135176 | tf_op jit(solution)/shard_map/ppermute | solution.py:450
  11.3 5.9 %collective-permute-start.5 = (f32[88,128]{1,0:T(8,128)S(1)}, f32[88,128]{1,0:T(8,128)S(1)}, u32[]{:S(2)}, u32[]{:S(2)}) collective-permute-start(f32[88,128]{1,0:T(8,128)S(1)} %get-tuple-element.30), channel_id=1, source_target_pairs={{0,24},{4,28},{8,16},{12,20},{16,8},{20,12},{24,0},{28,4},{1,25},{... | collective-permute-start | bytes 135176 | tf_op jit(solution)/shard_map/ppermute | solution.py:450
  12.6 4.5 %collective-permute-start.7 = (f32[88,128]{1,0:T(8,128)S(1)}, f32[88,128]{1,0:T(8,128)S(1)}, u32[]{:S(2)}, u32[]{:S(2)}) collective-permute-start(f32[88,128]{1,0:T(8,128)S(1)} %get-tuple-element.30), channel_id=1, source_target_pairs={{0,8},{4,12},{8,0},{12,4},{16,24},{20,28},{24,16},{28,20},{1,9},{5... | collective-permute-start | bytes 135176 | tf_op jit(solution)/shard_map/ppermute | solution.py:450
  12.9 18.8 %copy-start.1 = (f32[2,8,128]{2,1,0:T(8,128)S(1)}, f32[2,8,128]{2,1,0:T(8,128)}, u32[]{:S(2)}) copy-start(f32[2,8,128]{2,1,0:T(8,128)} %param.15) | copy-start | bytes 24580
  12.9 5.9 %collective-permute-start.4 = (f32[256,128]{1,0:T(8,128)S(1)}, f32[256,128]{1,0:T(8,128)S(1)}, u32[]{:S(2)}, u32[]{:S(2)}) collective-permute-start(f32[256,128]{1,0:T(8,128)S(1)} %pad_maximum_fusion.1), channel_id=1, source_target_pairs={{0,4},{4,0},{8,12},{12,8},{16,20},{20,16},{24,28},{28,24},{1,5},{5... | collective-permute-start | bytes 393224 | tf_op jit(solution)/shard_map/ppermute | solution.py:450
  14.4 12.0 %collective-permute-start = (f32[640,128]{1,0:T(8,128)S(1)}, f32[640,128]{1,0:T(8,128)S(1)}, u32[]{:S(2)}, u32[]{:S(2)}) collective-permute-start(f32[640,128]{1,0:T(8,128)S(1)} %get-tuple-element.18), channel_id=1, source_target_pairs={{0,1},{1,0},{2,3},{3,2},{4,5},{5,4},{6,7},{7,6},{8,9},{9,8},{10,11... | collective-permute-start | bytes 983048 | tf_op jit(solution)/shard_map/ppermute | solution.py:450
  14.5 12.0 %collective-permute-start.1 = (f32[640,128]{1,0:T(8,128)S(1)}, f32[640,128]{1,0:T(8,128)S(1)}, u32[]{:S(2)}, u32[]{:S(2)}) collective-permute-start(f32[640,128]{1,0:T(8,128)S(1)} %get-tuple-element.19), channel_id=1, source_target_pairs={{1,2},{2,1},{0,0},{3,3},{5,6},{6,5},{4,4},{7,7},{9,10},{10,9},{8,8... | collective-permute-start | bytes 983048 | tf_op jit(solution)/shard_map/ppermute | solution.py:516
  17.2 6.4 %collective-permute-start.8 = (f32[3,88,128]{2,1,0:T(8,128)S(1)}, f32[3,88,128]{2,1,0:T(8,128)S(1)}, u32[]{:S(2)}, u32[]{:S(2)}) collective-permute-start(f32[3,88,128]{2,1,0:T(8,128)S(1)} %pad_maximum_fusion), channel_id=1, source_target_pairs={{0,4},{4,0},{8,12},{12,8},{16,20},{20,16},{24,28},{28,24},{1,5},{5... | collective-permute-start | bytes 405512 | tf_op jit(solution)/shard_map/ppermute | solution.py:450
  18.8 7.7 %collective-permute-start.9 = (f32[5,88,128]{2,1,0:T(8,128)S(1)}, f32[5,88,128]{2,1,0:T(8,128)S(1)}, u32[]{:S(2)}, u32[]{:S(2)}) collective-permute-start(f32[5,88,128]{2,1,0:T(8,128)S(1)} %constant_dynamic-update-slice_fusion.rest_0_), channel_id=1, source_target_pairs={{0,1},{1,0},{2,3},{3,2},{4,5},{5,4},{6,7},{7,6},{8,9},{9,8},{10,11... | collective-permute-start | bytes 675848 | tf_op jit(solution)/shard_map/ppermute | solution.py:450
  23.6 2.9 %collective-permute-start.10 = (f32[3,88,128]{2,1,0:T(8,128)S(1)}, f32[3,88,128]{2,1,0:T(8,128)S(1)}, u32[]{:S(2)}, u32[]{:S(2)}) collective-permute-start(f32[3,88,128]{2,1,0:T(8,128)S(1)} %collective-permute-done.8.rest_1_), channel_id=1, source_target_pairs={{0,1},{1,0},{2,3},{3,2},{4,5},{5,4},{6,7},{7,6},{8,9},{9,8},{10,11... | collective-permute-start | bytes 405512 | tf_op jit(solution)/shard_map/ppermute | solution.py:450
  23.6 8.0 %collective-permute-start.11 = (f32[168,128]{1,0:T(8,128)S(1)}, f32[168,128]{1,0:T(8,128)S(1)}, u32[]{:S(2)}, u32[]{:S(2)}) collective-permute-start(f32[168,128]{1,0:T(8,128)S(1)} %get-tuple-element.24), channel_id=1, source_target_pairs={{4,8},{12,16},{20,24},{28,0},{8,4},{16,12},{24,20},{0,28},{5,9},{1... | collective-permute-start | bytes 258056 | tf_op jit(solution)/shard_map/ppermute | solution.py:518
